TPU v7x, 32 devices: a whole 2x2x4 slice. The times are simulated.
32 devices in a mesh: dp: 16 (over z, y, core), tensor: 2 (over x).
Axes of the slice: x: 2, y: 2, z: 4, core: 2. Of those that a mesh axis runs over, the one named last changes fastest.
Arguments:
- tokens: bfloat16 [7680, 1536], P(('dp', 'tensor')), may hold values from -6 to 6
- teacher: bfloat16 [7680, 1536], P(('dp', 'tensor')), may hold values from -6 to 6
- valid: int32 [7680], P(('dp', 'tensor')), may hold values from 0 to 1
- mixer_gain: bfloat16 [1536], P(('dp', 'tensor')), may hold values from 0.099609375 to 1.8984375
- in_weight: bfloat16 [1536, 3, 1536], P('dp', None, 'tensor'), may hold values from -0.15625 to 0.15625
- conv_weight: bfloat16 [3, 1536], P(None, ('dp', 'tensor')), may hold values from -3.5 to 3.5
- out_weight: bfloat16 [1536, 1536], P('dp', 'tensor'), may hold values from -0.15625 to 0.15625
- ffn_gain: bfloat16 [1536], P(('dp', 'tensor')), may hold values from 0.099609375 to 1.8984375
- gate_weight: bfloat16 [1536, 6912], P('dp', 'tensor'), may hold values from -0.15625 to 0.15625
- up_weight: bfloat16 [1536, 6912], P('dp', 'tensor'), may hold values from -0.15625 to 0.15625
- down_weight: bfloat16 [1536, 6912], P('dp', 'tensor'), may hold values from -0.078125 to 0.078125
Outputs:
- loss: float32 [], replicated
- block_output: float32 [7680, 1536], P(('dp', 'tensor'))
- tokens_grad: float32 [7680, 1536], P(('dp', 'tensor'))
- mixer_gain_grad: float32 [1536], P(('dp', 'tensor'))
- in_weight_grad: float32 [1536, 3, 1536], P('dp', None, 'tensor')
- conv_weight_grad: float32 [3, 1536], P(None, ('dp', 'tensor'))
- out_weight_grad: float32 [1536, 1536], P('dp', 'tensor')
- ffn_gain_grad: float32 [1536], P(('dp', 'tensor'))
- gate_weight_grad: float32 [1536, 6912], P('dp', 'tensor')
- up_weight_grad: float32 [1536, 6912], P('dp', 'tensor')
- down_weight_grad: float32 [1536, 6912], P('dp', 'tensor')
All inputs are finite; a program needn't handle non-finite values.
Results may differ from a plain program's by a relative error of at most 0.0088.
Values may be sent and summed in bfloat16 or wider, within the bound.
A program may use at most 192 MiB of HBM per device.

v0:
```python
import jax
import jax.numpy as jnp
from jax import lax
from jax.sharding import PartitionSpec as P

KERNEL = 3


norm_eps = 1e-05


def row_scale(source):
    return lax.rsqrt(jnp.mean(source * source, axis=1, keepdims=True) + norm_eps)


def norm_back(grad_normed, source, inverse, gain_vec):
    weighted = grad_normed * gain_vec
    inner_prod = jnp.mean(weighted * source, axis=1, keepdims=True)
    grad_source = inverse * weighted - source * (inverse * inverse * inverse) * inner_prod
    grad_gain = jnp.sum(grad_normed * source * inverse, axis=0)
    return (grad_source, grad_gain)


def contract_rows(left, right):
    return lax.dot_general(
        left, right, (((0,), (0,)), ((), ())), preferred_element_type=jnp.float32
    )


def contract_cols(left, right):
    return lax.dot_general(
        left, right, (((1,), (1,)), ((), ())), preferred_element_type=jnp.float32
    )


def mixer_params(in_weight, out_weight):
    return (
        lax.all_gather(in_weight, "dp", axis=0, tiled=True),
        lax.all_gather(out_weight, "dp", axis=0, tiled=True),
    )


def ffn_params(gate_weight, up_weight, down_weight):
    return (
        lax.all_gather(gate_weight, "dp", axis=0, tiled=True),
        lax.all_gather(up_weight, "dp", axis=0, tiled=True),
        lax.all_gather(down_weight, "dp", axis=0, tiled=True),
    )


def gather_rows(local_rows):
    return lax.all_gather(local_rows, "tensor", axis=0, tiled=True)


def sum_rows(partial_rows):
    return lax.psum_scatter(partial_rows, "tensor", scatter_dimension=0, tiled=True)


def body(
    tokens,
    teacher,
    valid,
    mixer_gain,
    in_weight,
    conv_weight,
    out_weight,
    ffn_gain,
    gate_weight,
    up_weight,
    down_weight,
):
    width = tokens.shape[1]
    channels = in_weight.shape[2]
    tensor_index = lax.axis_index("tensor")
    valid_f = valid.astype(jnp.float32)
    gain_one, gain_two, conv_full = (
        lax.all_gather(mixer_gain, ("dp", "tensor"), axis=0, tiled=True),
        lax.all_gather(ffn_gain, ("dp", "tensor"), axis=0, tiled=True),
        lax.all_gather(conv_weight, ("dp", "tensor"), axis=1, tiled=True),
    )
    gain_one = gain_one.astype(jnp.float32)
    gain_two = gain_two.astype(jnp.float32)
    conv_taps = lax.dynamic_slice_in_dim(
        conv_full.astype(jnp.float32), tensor_index * channels, channels, 1
    )
    states = tokens.astype(jnp.float32)
    inverse_one = row_scale(states)
    normed = (states * inverse_one * gain_one).astype(jnp.bfloat16)
    in_full, out_full = mixer_params(in_weight, out_weight)
    row_block = gather_rows(normed)
    length = row_block.shape[0]
    projected = jnp.einsum("ti,ikc->ktc", row_block, in_full, preferred_element_type=jnp.float32)
    b_gate = projected[0]
    c_gate = projected[1]
    x_stream = projected[2]
    mixed_in = b_gate * x_stream
    edge_zeros = jnp.zeros((KERNEL - 1, channels), jnp.float32)
    padded = jnp.concatenate([edge_zeros, mixed_in], axis=0)
    convolved = conv_taps[0] * padded[0:length]
    for offset in range(1, KERNEL):
        convolved = convolved + conv_taps[offset] * padded[offset : offset + length]
    gated = (c_gate * convolved).astype(jnp.bfloat16)
    mixer_out = sum_rows(contract_cols(gated, out_full))
    first = states + mixer_out
    inverse_two = row_scale(first)
    normed_two = (first * inverse_two * gain_two).astype(jnp.bfloat16)
    gate_full, up_full, down_full = ffn_params(gate_weight, up_weight, down_weight)
    rows_two = gather_rows(normed_two)
    gate_val = jnp.dot(rows_two, gate_full, preferred_element_type=jnp.float32)
    up_val = jnp.dot(rows_two, up_full, preferred_element_type=jnp.float32)
    sigmoid_val = jax.nn.sigmoid(gate_val)
    active = gate_val * sigmoid_val
    hidden = (active * up_val).astype(jnp.bfloat16)
    ffn_out = sum_rows(contract_cols(hidden, down_full))
    block_out = first + ffn_out
    error = block_out - teacher.astype(jnp.float32)
    loss_local = jnp.sum(valid_f[:, None] * error * error)
    valid_total, loss_total = lax.psum((jnp.sum(valid_f), loss_local), ("dp", "tensor"))
    loss_scale = 1.0 / (width * valid_total)
    grad_out = 2.0 * loss_scale * valid_f[:, None] * error
    gate_full, up_full, down_full = ffn_params(gate_weight, up_weight, down_weight)
    grad_rows = gather_rows(grad_out.astype(jnp.bfloat16))
    grad_hidden = jnp.dot(grad_rows, down_full, preferred_element_type=jnp.float32)
    grad_gate_val = (
        grad_hidden * up_val * sigmoid_val * (1.0 + gate_val * (1.0 - sigmoid_val))
    ).astype(jnp.bfloat16)
    grad_up_val = (grad_hidden * active).astype(jnp.bfloat16)
    grad_down = contract_rows(grad_rows, hidden)
    grad_gate_w = contract_rows(rows_two, grad_gate_val)
    grad_up_w = contract_rows(rows_two, grad_up_val)
    ffn_grads = (
        lax.psum_scatter(grad_gate_w, "dp", scatter_dimension=0, tiled=True),
        lax.psum_scatter(grad_up_w, "dp", scatter_dimension=0, tiled=True),
        lax.psum_scatter(grad_down, "dp", scatter_dimension=0, tiled=True),
    )
    grad_normed_two = sum_rows(
        contract_cols(grad_gate_val, gate_full) + contract_cols(grad_up_val, up_full)
    )
    grad_first_norm, grad_gain_two = norm_back(grad_normed_two, first, inverse_two, gain_two)
    grad_first = grad_out + grad_first_norm
    in_full, out_full = mixer_params(in_weight, out_weight)
    grad_mix_rows = gather_rows(grad_first.astype(jnp.bfloat16))
    grad_gated = jnp.dot(grad_mix_rows, out_full, preferred_element_type=jnp.float32)
    grad_c = (grad_gated * convolved).astype(jnp.bfloat16)
    grad_conv = grad_gated * c_gate
    grad_padded = jnp.concatenate([grad_conv, edge_zeros], axis=0)
    grad_mixed = conv_taps[0] * grad_padded[KERNEL - 1 : KERNEL - 1 + length]
    for offset in range(1, KERNEL):
        grad_mixed = (
            grad_mixed
            + conv_taps[offset] * grad_padded[KERNEL - 1 - offset : KERNEL - 1 - offset + length]
        )
    grad_taps = jnp.stack(
        [jnp.sum(grad_conv * padded[offset : offset + length], axis=0) for offset in range(KERNEL)]
    )
    grad_b = (grad_mixed * x_stream).astype(jnp.bfloat16)
    grad_x = (grad_mixed * b_gate).astype(jnp.bfloat16)
    grad_proj = jnp.stack([grad_b, grad_c, grad_x])
    grad_out_w = contract_rows(grad_mix_rows, gated)
    grad_in_w = jnp.einsum("ti,ktc->ikc", row_block, grad_proj, preferred_element_type=jnp.float32)
    mixer_grads = (
        lax.psum_scatter(grad_in_w, "dp", scatter_dimension=0, tiled=True),
        lax.psum_scatter(grad_out_w, "dp", scatter_dimension=0, tiled=True),
    )
    grad_normed = sum_rows(
        jnp.einsum("ktc,ikc->ti", grad_proj, in_full, preferred_element_type=jnp.float32)
    )
    grad_states, grad_gain_one = norm_back(grad_normed, states, inverse_one, gain_one)
    grad_tokens = grad_first + grad_states
    conv_term = lax.dynamic_update_slice_in_dim(
        jnp.zeros((KERNEL, width), jnp.float32), grad_taps, tensor_index * channels, 1
    )
    small_sums = (
        lax.psum_scatter(grad_gain_one, ("dp", "tensor"), scatter_dimension=0, tiled=True),
        lax.psum_scatter(grad_gain_two, ("dp", "tensor"), scatter_dimension=0, tiled=True),
        lax.psum_scatter(conv_term, ("dp", "tensor"), scatter_dimension=1, tiled=True),
    )
    loss = loss_total * loss_scale
    return (
        loss,
        block_out,
        grad_tokens,
        small_sums[0],
        mixer_grads[0],
        small_sums[2],
        mixer_grads[1],
        small_sums[1],
        ffn_grads[0],
        ffn_grads[1],
        ffn_grads[2],
    )


def solution(mesh):
    placed = (
        P(("dp", "tensor"), None),
        P(("dp", "tensor"), None),
        P(("dp", "tensor")),
        P(("dp", "tensor")),
        P("dp", None, "tensor"),
        P(None, ("dp", "tensor")),
        P("dp", "tensor"),
        P(("dp", "tensor")),
        P("dp", "tensor"),
        P("dp", "tensor"),
        P("dp", "tensor"),
    )
    return jax.shard_map(
        body,
        mesh=mesh,
        in_specs=placed,
        out_specs=(
            P(),
            P(("dp", "tensor"), None),
            P(("dp", "tensor"), None),
            P(("dp", "tensor")),
            P("dp", None, "tensor"),
            P(None, ("dp", "tensor")),
            P("dp", "tensor"),
            P(("dp", "tensor")),
            P("dp", "tensor"),
            P("dp", "tensor"),
            P("dp", "tensor"),
        ),
        check_vma=False,
    )
```

profile of v0, /device:TPU:0, one launch (start us, length us, event | category | flops | bytes accessed | tf_op | source)
XLA Modules:
  0.0 1762.9 jit_solution(15826962201998875629)
XLA Ops:
  8.9 42.1 %all-reduce.7 = (bf16[1536]{0:T(1024)(128)(2,1)S(1)}, bf16[1536]{0:T(1024)(128)(2,1)S(1)}) all-reduce(bf16[1536]{0:T(1024)(128)(2,1)S(1)} %dynamic-update-slice, bf16[1536]{0:T(1024)(128)(2,1)S(1)} %dynamic-update-slice.1), channel_id=1, replica_groups=mesh['dp'=16,'tensor'=2] {'dp','tensor'}, use_global_device_ids=true, to_apply=%add.2 | all-reduce | flops 3072 | bytes 12288
  51.1 1.3 fusion.2
  53.6 2.2 fusion.4
  57.4 66.2 %all-gather = bf16[32,48,3]{1,2,0:T(4,128)(2,1)S(1)} all-gather(bf16[1,48,3]{1,2,0:T(4,128)(2,1)S(1)} %bitcast.77), channel_id=1, replica_groups=mesh['dp'=16,'tensor'=2] {'dp','tensor'}, dimensions={0}, use_global_device_ids=true | all-gather | bytes 9504 | tf_op jit(solution)/shard_map/all_gather | solution.py:79
  123.8 27.4 %all-gather.13.cloned.1.call-done = bf16[1536,3,768]{2,0,1:T(8,128)(2,1)} async-done(((bf16[96,3,768]{2,0,1:T(8,128)(2,1)}), bf16[1536,3,768]{2,0,1:T(8,128)(2,1)}) %all-gather.13.cloned.1.call-update) | async-done | bytes 7077904 | tf_op jit(solution)/shard_map/all_gather | solution.py:38
  151.1 6.7 convolution_bitcast_fusion.1
  158.0 1.9 copy-done.2
  160.4 1.6 multiply_convert_fusion.7
  162.1 32.1 %all-gather.15.cloned.1.call-done = bf16[1536,768]{1,0:T(8,128)(2,1)} async-done(((bf16[96,768]{1,0:T(8,128)(2,1)}), bf16[1536,768]{1,0:T(8,128)(2,1)}) %all-gather.15.cloned.1.call-update) | async-done | bytes 2359312 | tf_op jit(solution)/shard_map/all_gather | solution.py:39
  194.1 4.6 fusion.23
  199.4 39.5 %reduce-scatter.13.cloned.1.call-done = f32[240,1536]{1,0:T(8,128)} async-done(((f32[480,1536]{1,0:T(8,128)}), f32[240,1536]{1,0:T(8,128)}) %reduce-scatter.13.cloned.1.call-update) | async-done | bytes 1474576 | tf_op jit(solution)/shard_map/reduce_scatter | solution.py:56
  238.9 1.6 multiply_reduce_fusion.5
  243.7 86.3 %all-gather.19.cloned.1.call-done = bf16[1536,3456]{1,0:T(8,128)(2,1)} async-done(((bf16[96,3456]{1,0:T(8,128)(2,1)}), bf16[1536,3456]{1,0:T(8,128)(2,1)}) %all-gather.19.cloned.1.call-update) | async-done | bytes 10616848 | tf_op jit(solution)/shard_map/all_gather | solution.py:45
  330.0 26.3 %all-gather.17.cloned.1.call-done = bf16[480,1536]{1,0:T(8,128)(2,1)} async-done(((bf16[240,1536]{1,0:T(8,128)(2,1)}), bf16[480,1536]{1,0:T(8,128)(2,1)}) %all-gather.17.cloned.1.call-update) | async-done | bytes 1474576 | tf_op jit(solution)/shard_map/all_gather | solution.py:52
  356.4 11.7 fusion.24
  368.1 79.6 %all-gather.21.cloned.1.call-done = bf16[1536,3456]{1,0:T(8,128)(2,1)} async-done(((bf16[96,3456]{1,0:T(8,128)(2,1)}), bf16[1536,3456]{1,0:T(8,128)(2,1)}) %all-gather.21.cloned.1.call-update) | async-done | bytes 10616848 | tf_op jit(solution)/shard_map/all_gather | solution.py:46
  447.6 13.2 multiply_convert_fusion.2
  460.8 76.2 %all-gather.23.cloned.1.call-done = bf16[1536,3456]{1,0:T(8,128)(2,1)} async-done(((bf16[96,3456]{1,0:T(8,128)(2,1)}), bf16[1536,3456]{1,0:T(8,128)(2,1)}) %all-gather.23.cloned.1.call-update) | async-done | bytes 10616848 | tf_op jit(solution)/shard_map/all_gather | solution.py:47
  537.0 10.4 fusion.25
  548.8 39.1 %psum.15 = f32[]{:T(128)} all-reduce(f32[]{:T(128)} %convert_reduce_fusion), channel_id=1, replica_groups=mesh['dp'=16,'tensor'=2] {'dp','tensor'}, use_global_device_ids=true, to_apply=%region_7.0 | all-reduce | flops 1 | bytes 8 | tf_op jit(solution)/shard_map/psum | solution.py:118
  588.6 2.7 multiply_convert_fusion.8
  591.5 26.9 %all-gather.25.cloned.1.call-done = bf16[480,1536]{1,0:T(8,128)(2,1)} async-done(((bf16[240,1536]{1,0:T(8,128)(2,1)}), bf16[480,1536]{1,0:T(8,128)(2,1)}) %all-gather.25.cloned.1.call-update) | async-done | bytes 1474576 | tf_op jit(solution)/shard_map/all_gather | solution.py:52
  618.4 13.9 multiply_convert_fusion
  632.3 10.6 fusion.26
  643.0 9.5 convolution_add_fusion
  652.6 41.3 %reduce-scatter.17.cloned.1.call-done = f32[240,1536]{1,0:T(8,128)} async-done(((f32[480,1536]{1,0:T(8,128)}), f32[240,1536]{1,0:T(8,128)}) %reduce-scatter.17.cloned.1.call-update) | async-done | bytes 1474576 | tf_op jit(solution)/shard_map/reduce_scatter | solution.py:56
  693.9 1.9 multiply_reduce_fusion
  695.9 2.9 fusion.22
  698.8 26.2 %all-gather.27.cloned.1.call-done = bf16[480,1536]{1,0:T(8,128)(2,1)} async-done(((bf16[240,1536]{1,0:T(8,128)(2,1)}), bf16[480,1536]{1,0:T(8,128)(2,1)}) %all-gather.27.cloned.1.call-update) | async-done | bytes 1474576 | tf_op jit(solution)/shard_map/all_gather | solution.py:52
  725.1 6.9 multiply_reduce_fusion.3
  731.9 1.4 fusion.16
  735.8 8.5 convolution_bitcast_fusion
  745.9 3.7 fusion.27
  751.2 8.3 fusion.11
  760.9 12.2 fusion.28
  773.2 12.3 fusion.29
  786.8 12.1 fusion.30
  799.0 32.2 %reduce-scatter.31.cloned.1.call-done = f32[48,3]{1,0:T(8,128)} async-done(((f32[1536,3]{1,0:T(8,128)}), f32[48,3]{1,0:T(8,128)}) %reduce-scatter.31.cloned.1.call-update) | async-done | bytes 592
  831.2 1.4 copy.26
  832.6 41.1 %reduce-scatter.19.cloned.1.call-done = f32[240,1536]{1,0:T(8,128)} async-done(((f32[480,1536]{1,0:T(8,128)}), f32[240,1536]{1,0:T(8,128)}) %reduce-scatter.19.cloned.1.call-update) | async-done | bytes 1474576 | tf_op jit(solution)/shard_map/reduce_scatter | solution.py:56
  873.8 1.9 fusion.10
  875.6 39.9 %all-reduce.6 = (f32[]{:T(128)}, f32[1536]{0:T(1024)S(1)}, f32[1536]{0:T(1024)S(1)}) all-reduce(f32[]{:T(128)} %get-tuple-element.39, f32[1536]{0:T(1024)S(1)} %get-tuple-element.16, f32[1536]{0:T(1024)S(1)} %get-tuple-element.11), channel_id=1, replica_groups=mesh['dp'=16,'tensor'=2] {'dp','tensor'}, use_global_device_ids=true, to_apply=%region_5.0 | all-reduce | flops 3073 | bytes 24584 | tf_op jit(solution)/shard_map/psum | solution.py:118
  917.4 2.9 fusion.7
  920.3 34.0 %reduce-scatter.23.cloned.1.call-done = f32[96,768]{1,0:T(8,128)} async-done(((f32[1536,768]{1,0:T(8,128)}), f32[96,768]{1,0:T(8,128)}) %reduce-scatter.23.cloned.1.call-update) | async-done | bytes 294928 | tf_op jit(solution)/shard_map/reduce_scatter | solution.py:163
  954.3 149.8 %reduce-scatter.21.cloned.1.call-done = f32[96,3,768]{2,0,1:T(8,128)} async-done(((f32[1536,3,768]{2,0,1:T(8,128)}), f32[96,3,768]{2,0,1:T(8,128)}) %reduce-scatter.21.cloned.1.call-update) | async-done | bytes 884752 | tf_op jit(solution)/shard_map/reduce_scatter | solution.py:162
  1104.1 217.0 %reduce-scatter.25.cloned.1.call-done = f32[96,3456]{1,0:T(8,128)} async-done(((f32[1536,3456]{1,0:T(8,128)}), f32[96,3456]{1,0:T(8,128)}) %reduce-scatter.25.cloned.1.call-update) | async-done | bytes 1327120 | tf_op jit(solution)/shard_map/reduce_scatter | solution.py:132
  1321.2 216.5 %reduce-scatter.27.cloned.1.call-done = f32[96,3456]{1,0:T(8,128)} async-done(((f32[1536,3456]{1,0:T(8,128)}), f32[96,3456]{1,0:T(8,128)}) %reduce-scatter.27.cloned.1.call-update) | async-done | bytes 1327120 | tf_op jit(solution)/shard_map/reduce_scatter | solution.py:133
  1537.7 217.2 %reduce-scatter.29.cloned.1.call-done = f32[96,3456]{1,0:T(8,128)} async-done(((f32[1536,3456]{1,0:T(8,128)}), f32[96,3456]{1,0:T(8,128)}) %reduce-scatter.29.cloned.1.call-update) | async-done | bytes 1327120 | tf_op jit(solution)/shard_map/reduce_scatter | solution.py:134
  (126 shorter events, 20.5 us)
Async XLA Ops:
  7.2 116.6 %all-gather.11.cloned.1.call-start = ((), (), s32[]{:S(2)}) async-start(), calls=%async_computation.10 | async-start | bytes 2211840 | tf_op jit(solution)/shard_map/all_gather | solution.py:52
  51.1 2.0 copy-start.14
  52.4 5.0 copy-start.20
  53.0 0.6 copy-start.16
  55.8 95.3 %all-gather.13.cloned.1.call-start = ((), (), s32[]{:S(2)}) async-start(), calls=%async_computation.11 | async-start | bytes 7520256 | tf_op jit(solution)/shard_map/all_gather | solution.py:38
  56.6 137.5 %all-gather.15.cloned.1.call-start = ((), (), s32[]{:S(2)}) async-start(), calls=%async_computation.12 | async-start | bytes 2506752 | tf_op jit(solution)/shard_map/all_gather | solution.py:39
  57.3 181.6 %reduce-scatter.13.cloned.1.call-start = ((), (), s32[]{:S(2)}) async-start(), calls=%async_computation.13 | async-start | bytes 4423680 | tf_op jit(solution)/shard_map/reduce_scatter | solution.py:56
  157.8 2.1 copy-start.2
  158.0 2.4 copy-start.6
  162.1 36.7 %copy-start.8 = (bf16[480,768]{1,0:T(8,128)(2,1)}, bf16[480,768]{1,0:T(8,128)(2,1)S(1)}, u32[]{:S(2)}) copy-start(bf16[480,768]{1,0:T(8,128)(2,1)S(1)} %get-tuple-element.35) | copy-start | bytes 2211844
  198.7 40.1 %copy-start = (bf16[240,1536]{1,0:T(8,128)(2,1)S(1)}, bf16[240,1536]{1,0:T(8,128)(2,1)}, u32[]{:S(2)}) copy-start(bf16[240,1536]{1,0:T(8,128)(2,1)} %param.11) | copy-start | bytes 2211844
  198.8 131.2 %all-gather.19.cloned.1.call-start = ((), (), s32[]{:S(2)}) async-start(), calls=%async_computation.15 | async-start | bytes 11280384 | tf_op jit(solution)/shard_map/all_gather | solution.py:45
  199.4 157.0 %all-gather.17.cloned.1.call-start = ((), (), s32[]{:S(2)}) async-start(), calls=%async_computation.14 | async-start | bytes 2211840 | tf_op jit(solution)/shard_map/all_gather | solution.py:52
  241.6 206.0 %all-gather.21.cloned.1.call-start = ((), (), s32[]{:S(2)}) async-start(), calls=%async_computation.16 | async-start | bytes 11280384 | tf_op jit(solution)/shard_map/all_gather | solution.py:46
  242.4 294.7 %all-gather.23.cloned.1.call-start = ((), (), s32[]{:S(2)}) async-start(), calls=%async_computation.17 | async-start | bytes 11280384 | tf_op jit(solution)/shard_map/all_gather | solution.py:47
  243.1 345.4 %reduce-scatter.15.cloned.1.call-start = ((), (), s32[]{:S(2)}) async-start(), calls=%async_computation.18 | async-start | bytes 4423680 | tf_op jit(solution)/shard_map/reduce_scatter | solution.py:56
  356.4 91.3 %copy-start.22 = (bf16[480,1536]{1,0:T(8,128)(2,1)S(1)}, bf16[480,1536]{1,0:T(8,128)(2,1)}, u32[]{:S(2)}) copy-start(bf16[480,1536]{1,0:T(8,128)(2,1)} %all-gather.17.cloned.1.call-done) | copy-start | bytes 4423684
  547.5 0.7 copy-start.18
  547.5 70.9 %all-gather.25.cloned.1.call-start = ((), (), s32[]{:S(2)}) async-start(), calls=%async_computation.19 | async-start | bytes 2211840 | tf_op jit(solution)/shard_map/all_gather | solution.py:52
  591.3 104.5 %copy-start.5 = (f32[240,1536]{1,0:T(8,128)}, f32[240,1536]{1,0:T(8,128)S(1)}, u32[]{:S(2)}) copy-start(f32[240,1536]{1,0:T(8,128)S(1)} %get-tuple-element.32) | copy-start | bytes 4423684
  591.3 102.6 %reduce-scatter.17.cloned.1.call-start = ((), (), s32[]{:S(2)}) async-start(), calls=%async_computation.20 | async-start | bytes 4423680 | tf_op jit(solution)/shard_map/reduce_scatter | solution.py:56
  632.3 10.7 copy-start.26
  632.3 10.7 copy-start.25
  652.5 72.6 %all-gather.27.cloned.1.call-start = ((), (), s32[]{:S(2)}) async-start(), calls=%async_computation.21 | async-start | bytes 2211840 | tf_op jit(solution)/shard_map/all_gather | solution.py:52
  693.9 1.9 copy-start.4
  693.9 2.0 copy-start.7
  695.9 36.1 %slice-start = ((s8[4423680]{0:T(1024)(128)(4,1)}), s8[229376]{0:T(1024)(128)(4,1)S(1)}, s32[]{:S(2)}) async-start(s8[4423680]{0:T(1024)(128)(4,1)} %bitcast.73), calls=%async_computation.29 | async-start | bytes 458752
  698.8 132.5 %reduce-scatter.31.cloned.1.call-start = ((), (), s32[]{:S(2)}) async-start(), calls=%async_computation.28 | async-start | bytes 811008
  725.0 6.9 slice-start.1
  734.3 1.3 copy-start.11
  734.3 1.5 copy-start.12
  735.6 138.2 %reduce-scatter.19.cloned.1.call-start = ((), (), s32[]{:S(2)}) async-start(), calls=%async_computation.22 | async-start | bytes 4423680 | tf_op jit(solution)/shard_map/reduce_scatter | solution.py:56
  744.3 1.1 copy-start.9
  744.3 1.6 copy-start.10
  744.3 210.0 %reduce-scatter.23.cloned.1.call-start = ((), (), s32[]{:S(2)}) async-start(), calls=%async_computation.24 | async-start | bytes 5013504 | tf_op jit(solution)/shard_map/reduce_scatter | solution.py:163
  749.6 1.1 copy-start.13
  749.6 1.6 copy-start.21
  749.6 354.5 %reduce-scatter.21.cloned.1.call-start = ((), (), s32[]{:S(2)}) async-start(), calls=%async_computation.23 | async-start | bytes 15040512 | tf_op jit(solution)/shard_map/reduce_scatter | solution.py:162
  759.5 1.4 copy-start.23
  759.6 561.6 %reduce-scatter.25.cloned.1.call-start = ((), (), s32[]{:S(2)}) async-start(), calls=%async_computation.25 | async-start | bytes 22560768 | tf_op jit(solution)/shard_map/reduce_scatter | solution.py:132
  773.2 764.6 %reduce-scatter.27.cloned.1.call-start = ((), (), s32[]{:S(2)}) async-start(), calls=%async_computation.26 | async-start | bytes 22560768 | tf_op jit(solution)/shard_map/reduce_scatter | solution.py:133
  785.5 1.4 copy-start.24
  785.5 969.5 %reduce-scatter.29.cloned.1.call-start = ((), (), s32[]{:S(2)}) async-start(), calls=%async_computation.27 | async-start | bytes 22560768 | tf_op jit(solution)/shard_map/reduce_scatter | solution.py:134
  799.0 74.8 %copy-start.1 = (bf16[240,1536]{1,0:T(8,128)(2,1)S(1)}, bf16[240,1536]{1,0:T(8,128)(2,1)}, u32[]{:S(2)}) copy-start(bf16[240,1536]{1,0:T(8,128)(2,1)} %param.11) | copy-start | bytes 2211844
  799.0 74.8 %copy-start.15 = (f32[1536]{0:T(1024)S(1)}, f32[1536]{0:T(1024)}, u32[]{:S(2)}) copy-start(f32[1536]{0:T(1024)} %copy-done.14) | copy-start | bytes 18436
  799.0 74.8 %copy-start.17 = (f32[240]{0:T(256)S(1)}, f32[240]{0:T(256)}, u32[]{:S(2)}) copy-start(f32[240]{0:T(256)} %copy-done.16) | copy-start | bytes 2884
  799.0 118.4 %copy-start.19 = (f32[240]{0:T(256)S(1)}, f32[240]{0:T(256)}, u32[]{:S(2)}) copy-start(f32[240]{0:T(256)} %get-tuple-element.41) | copy-start | bytes 2884
  873.8 43.6 %copy-start.3 = (f32[240,1536]{1,0:T(8,128)S(1)}, f32[240,1536]{1,0:T(8,128)}, u32[]{:S(2)}) copy-start(f32[240,1536]{1,0:T(8,128)} %reduce-scatter.19.cloned.1.call-done) | copy-start | bytes 4423684
Sparse Core Ops, SparseCore 0:
  56.0 26.1 all-gather.10
  84.4 66.6 all-gather.12
  153.4 40.6 all-gather.14
  198.9 39.9 reduce-scatter.12
  241.3 88.6 all-gather.18
  332.0 24.2 all-gather.16
  358.9 88.6 all-gather.20
  450.2 86.8 all-gather.22
  547.6 40.5 reduce-scatter.14
  591.4 26.9 all-gather.24
  652.6 41.2 reduce-scatter.16
  698.9 26.0 all-gather.26
  735.7 95.4 reduce-scatter.30
  833.5 40.2 reduce-scatter.18
  878.0 76.2 reduce-scatter.22
  959.5 144.6 reduce-scatter.20
  1109.2 211.8 reduce-scatter.24
  1325.7 211.9 reduce-scatter.26
  1543.0 211.9 reduce-scatter.28
where the time goes:
time: 1770 us; the launch traced here: 1760 us
  waiting for transfers between devices  1370 us (77%)
  blocking collectives  187 us (11%)
  matrix products  145 us (8%)
  other arithmetic  24 us (1%)
    reduce_scatter x1, waiting for transfers between devices, body(): lax.psum_scatter(grad_down, 'dp', scatter_dimension=0, tiled=True)  217 us
    reduce_scatter x1, waiting for transfers between devices, body(): lax.psum_scatter(grad_gate_w, 'dp', scatter_dimension=0, tiled=True)  217 us
    reduce_scatter x1, waiting for transfers between devices, body(): lax.psum_scatter(grad_up_w, 'dp', scatter_dimension=0, tiled=True)  217 us
    reduce_scatter x1, waiting for transfers between devices, body(): lax.psum_scatter(grad_in_w, 'dp', scatter_dimension=0, tiled=True)  150 us
    reduce_scatter x4, waiting for transfers between devices, sum_rows(): lax.psum_scatter(partial_rows, 'tensor', scatter_dimension=0, tiled=True)  122 us
    all_gather x1, waiting for transfers between devices, ffn_params(): lax.all_gather(gate_weight, 'dp', axis=0, tiled=True)  86.3 us
    all_gather x1, waiting for transfers between devices, ffn_params(): lax.all_gather(up_weight, 'dp', axis=0, tiled=True)  79.6 us
    all_gather x4, waiting for transfers between devices, gather_rows(): return lax.all_gather(local_rows, 'tensor', axis=0, tiled=True)  79.4 us
  transfers between devices with their start and end apart: 19, of which 17 were waited for; matrix products, arithmetic and copies ran while one was open for 6% of the time, Pallas kernels for 0%

commit v1 on v0

v1 whole, which is shorter than its diff:
```python
import functools
from types import SimpleNamespace

import jax
import jax.numpy as jnp
from jax import lax
from jax.experimental import pallas as pl
from jax.experimental.pallas import tpu as pltpu
from jax.sharding import PartitionSpec as P

MESH = pl.DeviceIdType.MESH
f32 = jnp.float32
bf16 = jnp.bfloat16
norm_eps = 1e-05
LANES = 256
NSUB = 3
VMEM = pl.BlockSpec(memory_space=pltpu.VMEM)
ANY = pl.BlockSpec(memory_space=pl.ANY)


def rows_of(start, size, step=16):
    return pl.ds(pl.multiple_of(start, step), size)


def place(ndp):
    d, x = lax.axis_index("dp"), lax.axis_index("tensor")
    core, y, z = d % 2, (d // 2) % 2, d // 4
    depth = ndp // 4
    at = SimpleNamespace(d=d, x=x, core=core, y=y, z=z, depth=depth, chip=d // 2)
    at.sib = (d + 1 - 2 * core, x)
    at.across = (d, 1 - x)
    at.beside = (d + 2 - 4 * y, x)
    at.lower, at.upper = (d - 4, x), (d + 4, x)
    at.has_lower, at.has_upper = z > 0, z < depth - 1
    at.cube = [at.sib, at.across, at.beside]
    step = 1
    while step < depth:
        at.cube.append((d + 4 * step * (1 - 2 * ((z // step) % 2)), x))
        step *= 2
    at.own = 2 * core + x
    at.own_sib = 2 * (1 - core) + x
    at.own_across = 2 * core + 1 - x
    at.own_far = 2 * (1 - core) + 1 - x
    return at


def meet(at):
    bar = pltpu.get_barrier_semaphore()
    always = [at.sib, at.across, at.beside] + at.cube[4:]
    for dev in always:
        pl.semaphore_signal(bar, 1, device_id=dev, device_id_type=MESH)
    for has, dev in ((at.has_lower, at.lower), (at.has_upper, at.upper)):

        @pl.when(has)
        def _():
            pl.semaphore_signal(bar, 1, device_id=dev, device_id_type=MESH)

    ends = jnp.where(at.has_lower, 1, 0) + jnp.where(at.has_upper, 1, 0)
    pl.semaphore_wait(bar, len(always) + ends)


def remote(src, dst, send, recv, dev):
    return pltpu.make_async_remote_copy(
        src_ref=src, dst_ref=dst, send_sem=send, recv_sem=recv, device_id=dev, device_id_type=MESH
    )


def total_step(at, step, cur, got, send, recv):
    copy = remote(cur.at[step], got.at[step], send.at[step], recv.at[step], at.cube[step])
    copy.start()
    copy.wait()
    cur[step + 1] = cur[step] + got[step]


class Share:
    def __init__(self, at, buf, rows, sems):
        self.at, self.buf, self.rows, self.sems = at, buf, rows, sems
        self.sub = rows // NSUB

    def part(self, slot, j):
        return self.buf.at[rows_of(slot * self.rows + j * self.sub, self.sub), :]

    def copy(self, slot, j, k, dev):
        part = self.part(slot, j)
        return remote(part, part, self.sems.at[2 * k, j], self.sems.at[2 * k + 1, j], dev)

    def start(self, j):
        self.copy(self.at.own, j, 0, self.at.across).start()
        self.copy(self.at.own, j, 1, self.at.sib).start()

    def forward(self, j):
        self.copy(self.at.own_across, j, 0, self.at.across).wait_recv()
        self.copy(self.at.own_across, j, 2, self.at.sib).start()

    def finish(self):
        for j in range(NSUB):
            self.copy(self.at.own_sib, j, 1, self.at.sib).wait_recv()
            self.copy(self.at.own_far, j, 2, self.at.sib).wait_recv()
            self.copy(self.at.own, j, 0, self.at.across).wait_send()
            self.copy(self.at.own, j, 1, self.at.sib).wait_send()
            self.copy(self.at.own_across, j, 2, self.at.sib).wait_send()


class Sums:
    def __init__(self, at, acc, rows, core_out, core_in, far_out, far_in, core_sems, far_sems):
        self.at, self.acc, self.rows = at, acc, rows
        self.core_out, self.core_in, self.far_out, self.far_in = core_out, core_in, far_out, far_in
        self.core_sems, self.far_sems = core_sems, far_sems
        self.sub = rows // NSUB

    def of(self, slot, j):
        return self.acc[rows_of(slot * self.rows + j * self.sub, self.sub), :]

    def core_copy(self, k, j):
        part = rows_of(j * self.sub, self.sub)
        return remote(
            self.core_out.at[k, part, :],
            self.core_in.at[k, part, :],
            self.core_sems.at[0, k, j],
            self.core_sems.at[1, k, j],
            self.at.sib,
        )

    def far_copy(self, j):
        part = rows_of(j * self.sub, self.sub)
        return remote(
            self.far_out.at[part, :],
            self.far_in.at[part, :],
            self.far_sems.at[0, j],
            self.far_sems.at[1, j],
            self.at.across,
        )

    def to_core(self):
        for k, slot in ((0, self.at.own_far), (1, self.at.own_sib)):
            for j in range(NSUB):
                self.core_out[k, rows_of(j * self.sub, self.sub), :] = self.of(slot, j).astype(bf16)
                self.core_copy(k, j).start()

    def to_far(self):
        for j in range(NSUB):
            part = rows_of(j * self.sub, self.sub)
            self.core_copy(0, j).wait_recv()
            both = self.of(self.at.own_across, j) + self.core_in[0, part, :].astype(f32)
            self.far_out[part, :] = both.astype(bf16)
            self.far_copy(j).start()

    def take(self, j):
        part = rows_of(j * self.sub, self.sub)
        self.core_copy(1, j).wait_recv()
        self.far_copy(j).wait_recv()
        return (
            self.of(self.at.own, j)
            + self.core_in[1, part, :].astype(f32)
            + self.far_in[part, :].astype(f32)
        )

    def finish(self):
        for j in range(NSUB):
            self.core_copy(0, j).wait_send()
            self.core_copy(1, j).wait_send()
            self.far_copy(j).wait_send()


def nt(left, right):
    return lax.dot_general(left, right, (((1,), (1,)), ((), ())), preferred_element_type=f32)


def tn(left, right):
    return lax.dot_general(left, right, (((0,), (0,)), ((), ())), preferred_element_type=f32)


def nn(left, right):
    return jnp.dot(left, right, preferred_element_type=f32)


def inverse_of(source):
    return lax.rsqrt(jnp.mean(source * source, axis=1, keepdims=True) + norm_eps)


def shifted(value, by):
    if by == 0:
        return value
    size = value.shape[0]
    row = lax.broadcasted_iota(jnp.int32, value.shape, 0)
    inside = row >= by if by > 0 else row < size + by
    return jnp.where(inside, pltpu.roll(value, by % size, 0), 0.0)


def convolve(mixed, taps):
    return taps[0:1] * shifted(mixed, 2) + taps[1:2] * shifted(mixed, 1) + taps[2:3] * mixed


class Gather:
    def __init__(self, at, held, chunk, early_y, sems):
        self.at, self.held, self.chunk, self.early_y = at, held, chunk, early_y
        self.recv, self.own_send, self.send = sems

    def block(self, p, chip, count=1):
        return self.held.at[p, rows_of(chip * self.chunk, count * self.chunk), :]

    def copy(self, p, chip, count, send, dev):
        block = self.block(p, chip, count)
        return remote(block, block, send, self.recv.at[p, chip], dev)

    def arrived(self, p, chip, count=1):
        self.copy(p, chip, count, self.own_send.at[0, 0], self.at.beside).wait_recv()

    def own(self, p, act):
        at = self.at
        act(self.copy(p, at.chip, 1, self.own_send.at[0, p], at.beside))
        if p not in self.early_y:
            self.own_z(p, at.chip, 1, act)

    def own_z(self, p, chip, count, act):
        at = self.at

        @pl.when(at.has_upper)
        def _():
            act(self.copy(p, chip, count, self.own_send.at[1, p], at.upper))

        @pl.when(at.has_lower)
        def _():
            act(self.copy(p, chip, count, self.own_send.at[2, p], at.lower))

    def passing(self, p, pairs, parity, wait, act):
        at = self.at

        def step(s, carry):
            for from_z, goes_on, dev, way in (
                (at.z - 1 - s, at.has_upper, at.upper, 0),
                (at.z + 1 + s, at.has_lower, at.lower, 1),
            ):

                @pl.when(jnp.logical_and(from_z >= 0, from_z < at.depth))
                def _():
                    chip = 2 * from_z if pairs else 2 * from_z + at.y
                    count = 2 if pairs else 1
                    if wait:
                        self.arrived(p, chip, count)

                    @pl.when(goes_on)
                    def _():
                        act(self.copy(p, chip, count, self.send.at[way, parity, from_z], dev))

                    if not pairs:
                        act(self.copy(p, chip, count, self.send.at[2, parity, from_z], at.beside))

            return carry

        lax.fori_loop(0, at.depth - 1, step, 0)

    def relay(self, p, parity, drop):
        if drop is not None:
            self.passing(drop[0], drop[1], parity, False, lambda copy: copy.wait_send())
        pairs = isinstance(p, int) and p in self.early_y
        if pairs:
            self.arrived(p, 2 * self.at.z + 1 - self.at.y)
            self.own_z(p, 2 * self.at.z, 2, lambda copy: copy.start())
        self.passing(p, pairs, parity, True, lambda copy: copy.start())

    def whole(self, p):
        def step(z, carry):
            self.arrived(p, 2 * z + 1 - self.at.y)
            return carry

        lax.fori_loop(0, self.at.depth, step, 0)


def forward_kernel(
    ndp,
    early_y,
    shards,
    tokens,
    teacher,
    valid,
    small,
    held_out,
    normed_out,
    normed_two_out,
    grad_rows_out,
    streams_out,
    gates_out,
    first_out,
    block_out,
    grad_out,
    small_out,
    loss_out,
    held,
    landed,
    mine,
    rows_a,
    rows_b,
    acc,
    streams,
    gates,
    core_out,
    core_in,
    far_out,
    far_in,
    first,
    result,
    error_grad,
    cur,
    got,
    chip_sems,
    recv_sems,
    own_sems,
    send_sems,
    share_sems,
    core_sems,
    far_sems,
    cube_sems,
    out_sems,
    held_sems,
    gate_sems,
):
    at = place(ndp)
    pieces, width, piece = held.shape
    part_rows = shards.shape[2]
    chunk = 2 * part_rows
    rows = tokens.shape[0]
    sub = rows // NSUB
    channels = streams.shape[1] // 3
    aligned = part_rows % 16 == 0
    go = lambda copy: copy.start()
    gather = Gather(at, held, chunk, early_y, (recv_sems, own_sems, send_sems))
    share_a = Share(at, rows_a, rows, share_sems)
    share_b = Share(at, rows_b, rows, share_sems)
    sums = Sums(at, acc, rows, core_out, core_in, far_out, far_in, core_sems, far_sems)

    def half(p, core):
        return held.at[p, rows_of(at.chip * chunk + core * part_rows, part_rows), :]

    def to_sib(p):
        dst = half(p, at.core) if aligned else landed.at[p]
        return remote(shards.at[1 - at.core, p], dst, chip_sems.at[0, p], chip_sems.at[1, p], at.sib)

    def from_sib(p):
        dst = half(p, 1 - at.core) if aligned else landed.at[p]
        return remote(dst, dst, chip_sems.at[0, p], chip_sems.at[1, p], at.sib)

    def keep(p):
        dst = half(p, at.core) if aligned else mine.at[p]
        return pltpu.make_async_copy(shards.at[at.core, p], dst, chip_sems.at[2, p])

    def own_block(p):
        keep(p).wait()
        from_sib(p).wait_recv()
        if not aligned:
            a, b = mine[p].astype(f32), landed[p].astype(f32)
            lower = jnp.where(at.core == 0, a, b)
            upper = jnp.where(at.core == 0, b, a)
            both = jnp.concatenate([lower, upper], axis=0).astype(bf16)
            held[p, rows_of(at.chip * chunk, chunk), :] = both
        gather.own(p, go)

    meet(at)
    for j in range(NSUB):
        rows_a[rows_of(at.own * rows + j * sub, sub), :] = tokens[pl.ds(j * sub, sub), :]
        share_a.start(j)
    for p in range(pieces):
        to_sib(p).start()
        keep(p).start()
    own_block(0)
    own_block(1)
    cur[0] = small[...]
    for step in range(len(at.cube)):
        total_step(at, step, cur, got, cube_sems.at[0], cube_sems.at[1])
    last = len(at.cube)
    small_out[...] = cur[last]
    own_block(2)
    for j in range(NSUB):
        share_a.forward(j)
    gain_one, gain_two = cur[last, 0:1, :], cur[last, 1:2, :]
    share_a.finish()

    def norm_rows(i, carry):
        part = rows_of(i * sub, sub)
        source = rows_a[part, :].astype(f32)
        rows_a[part, :] = (source * inverse_of(source) * gain_one).astype(bf16)
        return carry

    lax.fori_loop(0, 4 * NSUB, norm_rows, 0)
    normed_copy = pltpu.make_async_copy(rows_a, normed_out, out_sems.at[0])
    normed_copy.start()

    def save(p):
        return pltpu.make_async_copy(held.at[p], held_out.at[p], held_sems.at[p])

    gather.relay(0, 0, None)
    own_block(3)
    gather.relay(1, 1, None)
    own_block(4)
    for p in (0, 1):
        gather.whole(p)
        save(p).start()
    lane = at.x * 2 * channels + at.core * channels
    taps = cur[last, 2:5, rows_of(lane, channels, 128)]

    def mix(r, carry):
        part = rows_of(((r + 1 - at.core) % 2) * 2 * rows, 2 * rows)
        both = nn(rows_a[part, :], held[0])
        x_stream = nn(rows_a[part, :], held[1, :, 0:channels])
        streams[part, 0 : 2 * channels] = both
        streams[part, 2 * channels :] = x_stream
        convolved = convolve(both[:, 0:channels] * x_stream, taps)
        gated = (both[:, channels:] * convolved).astype(bf16)
        acc[part, :] = nt(gated, held[1, :, channels:])
        return carry

    lax.fori_loop(0, 2, mix, 0)
    streams_copy = pltpu.make_async_copy(streams, streams_out, out_sems.at[1])
    streams_copy.start()
    sums.to_core()
    gather.relay(2, 0, (0, 0 in early_y))
    own_block(5)
    sums.to_far()
    own_block(6)
    gather.relay(3, 1, (1, 1 in early_y))
    own_block(7)
    own_block(8)
    for p in range(9, pieces):
        own_block(p)
    for j in range(NSUB):
        part = rows_of(j * sub, sub)
        value = tokens[part, :].astype(f32) + sums.take(j)
        first[part, :] = value
        normed_two = (value * inverse_of(value) * gain_two).astype(bf16)
        rows_b[rows_of(at.own * rows + j * sub, sub), :] = normed_two
        share_b.start(j)
    sums.finish()
    first_copy = pltpu.make_async_copy(first, first_out, out_sems.at[2])
    first_copy.start()
    gather.relay(4, 0, (2, 2 in early_y))
    for j in range(NSUB):
        share_b.forward(j)
    share_b.finish()
    normed_two_copy = pltpu.make_async_copy(rows_b, normed_two_out, out_sems.at[3])
    normed_two_copy.start()
    acc[...] = jnp.zeros_like(acc)

    def gates_copy(p):
        slot = p % 2
        return pltpu.make_async_copy(gates.at[slot], gates_out.at[p - 2], gate_sems.at[slot])

    def feed(p, carry):
        @pl.when(p >= 5)
        def _():
            parity = p % 2

            @pl.when(p == 5)
            def _():
                gather.relay(p, parity, (3, 3 in early_y))

            @pl.when(p > 5)
            def _():
                gather.relay(p, parity, (p - 2, False))

        for q in range(2, pieces):
            if q not in early_y:

                @pl.when(p == q)
                def _():
                    gather.whole(q)

        save(p).start()

        @pl.when(p >= 4)
        def _():
            gates_copy(p - 2).wait()

        def some(r, inner):
            part = rows_of(((r + 1 - at.core) % 2) * 2 * rows, 2 * rows)
            both = nn(rows_b[part, :], held[p, :, 0 : 2 * LANES])
            gate, up = both[:, 0:LANES], both[:, LANES:]
            gates[p % 2, part, :] = both.astype(bf16)
            hidden = (gate * jax.nn.sigmoid(gate) * up).astype(bf16)
            acc[part, :] += nt(hidden, held[p, :, 2 * LANES :])
            return inner

        lax.fori_loop(0, 2, some, 0)
        gates_copy(p).start()
        return carry

    normed_copy.wait()
    lax.fori_loop(2, pieces, feed, 0)
    sums.to_core()
    sums.to_far()
    scale = 1.0 / (width * cur[last, 5:6, 0:1])
    loss = jnp.zeros((1, width), f32)
    for j in range(NSUB):
        part = rows_of(j * sub, sub)
        value = first[part, :] + sums.take(j)
        result[part, :] = value
        error = value - teacher[part, :].astype(f32)
        weighted = valid[part, :] * error
        loss = loss + jnp.sum(weighted * error, axis=0, keepdims=True)
        grad = (2.0 * scale) * weighted
        error_grad[part, :] = grad
        rows_a[rows_of(at.own * rows + j * sub, sub), :] = grad.astype(bf16)
        share_a.start(j)
    loss_out[...] = jnp.broadcast_to(jnp.sum(loss, axis=1, keepdims=True), loss_out.shape)
    sums.finish()
    result_copy = pltpu.make_async_copy(result, block_out, out_sems.at[4])
    result_copy.start()
    grad_copy = pltpu.make_async_copy(error_grad, grad_out, out_sems.at[5])
    grad_copy.start()
    for j in range(NSUB):
        share_a.forward(j)
    share_a.finish()
    rows_copy = pltpu.make_async_copy(rows_a, grad_rows_out, out_sems.at[6])
    rows_copy.start()
    for p in range(pieces):
        save(p).wait()
        to_sib(p).wait_send()
        gather.own(p, lambda copy: copy.wait_send())
        if p in early_y:
            gather.own_z(p, 2 * at.z, 2, lambda copy: copy.wait_send())
    for p in (pieces - 2, pieces - 1):
        gather.passing(p, p in early_y, p % 2, False, lambda copy: copy.wait_send())
        gates_copy(p).wait()
    for copy in (streams_copy, first_copy, normed_two_copy, result_copy, grad_copy, rows_copy):
        copy.wait()


def forward(ndp, shards, tokens, teacher, valid, small):
    _, pieces, part_rows, piece = shards.shape
    rows, width = tokens.shape
    channels = (2 * piece - piece // 2) // 3
    cube = small_steps(ndp)
    early_y = (3,)
    dma = pltpu.SemaphoreType.DMA
    landing = (pieces, part_rows, piece) if part_rows % 16 else (1, 16, 128)
    shape = jax.ShapeDtypeStruct
    outs = (
        shape((pieces, width, piece), bf16),
        shape((4 * rows, width), bf16),
        shape((4 * rows, width), bf16),
        shape((4 * rows, width), bf16),
        shape((4 * rows, 3 * channels), f32),
        shape((pieces - 2, 4 * rows, 2 * LANES), bf16),
        shape((rows, width), f32),
        shape((rows, width), f32),
        shape((rows, width), f32),
        shape((8, width), f32),
        shape((8, 128), f32),
    )
    scratch = [
        pltpu.VMEM((pieces, width, piece), bf16),
        pltpu.VMEM(landing, bf16),
        pltpu.VMEM(landing, bf16),
        pltpu.VMEM((4 * rows, width), bf16),
        pltpu.VMEM((4 * rows, width), bf16),
        pltpu.VMEM((4 * rows, width), f32),
        pltpu.VMEM((4 * rows, 3 * channels), f32),
        pltpu.VMEM((2, 4 * rows, 2 * LANES), bf16),
        pltpu.VMEM((2, rows, width), bf16),
        pltpu.VMEM((2, rows, width), bf16),
        pltpu.VMEM((rows, width), bf16),
        pltpu.VMEM((rows, width), bf16),
        pltpu.VMEM((rows, width), f32),
        pltpu.VMEM((rows, width), f32),
        pltpu.VMEM((rows, width), f32),
        pltpu.VMEM((cube + 1, 8, width), f32),
        pltpu.VMEM((cube, 8, width), f32),
        dma((3, pieces)),
        dma((pieces, ndp // 2)),
        dma((3, pieces)),
        dma((3, 2, ndp // 4)),
        dma((6, NSUB)),
        dma((2, 2, NSUB)),
        dma((2, NSUB)),
        dma((2, cube)),
        dma((7,)),
        dma((pieces,)),
        dma((2,)),
    ]
    return pl.pallas_call(
        functools.partial(forward_kernel, ndp, early_y),
        out_shape=outs,
        in_specs=[ANY, VMEM, VMEM, VMEM, VMEM],
        out_specs=[ANY] * 9 + [VMEM] * 2,
        scratch_shapes=scratch,
        compiler_params=pltpu.CompilerParams(
            collective_id=0, has_side_effects=True, vmem_limit_bytes=63 << 20
        ),
    )(shards, tokens, teacher, valid, small)


def small_steps(ndp):
    return 3 + (ndp // 4 - 1).bit_length()


def shard_pieces(in_weight, out_weight, gate_weight, up_weight, down_weight):
    part_rows, _, channels = in_weight.shape
    channels //= 2
    taps = in_weight.reshape(part_rows, 3, 2, channels).transpose(2, 0, 1, 3)
    taps = taps.reshape(2, part_rows, 3 * channels)
    outs = out_weight.reshape(part_rows, 2, channels).transpose(1, 0, 2)
    mixer = jnp.concatenate([taps, outs], axis=2)
    mixer = mixer.reshape(2, part_rows, 2, 2 * channels).transpose(0, 2, 1, 3)
    units = gate_weight.shape[1]
    count = -(-units // (2 * LANES))

    def cut(weight):
        weight = jnp.pad(weight, ((0, 0), (0, 2 * count * LANES - units)))
        return weight.reshape(part_rows, 2, count, LANES).transpose(1, 2, 0, 3)

    ffn = jnp.concatenate([cut(gate_weight), cut(up_weight), cut(down_weight)], axis=3)
    return jnp.concatenate([mixer, ffn], axis=1)


class Scatter:
    def __init__(self, at, held, chunk, count, beside_in, line_in, pair_in, pair_beside, total, sems, credits):
        self.at, self.held, self.chunk, self.count = at, held, chunk, count
        self.beside_in, self.line_in, self.pair_in, self.pair_beside = beside_in, line_in, pair_in, pair_beside
        self.total, self.credits = total, credits
        self.beside_sems, self.line_sems, self.pair_sems, self.pair_y_sems = sems

    def block(self, p, chip, count=1):
        return self.held.at[p, rows_of(chip * self.chunk, count * self.chunk), :]

    def beside_copy(self, p, m, z):
        slot = m % 2
        return remote(
            self.block(p, 2 * z + 1 - self.at.y),
            self.beside_in.at[slot, z],
            self.beside_sems.at[0, slot, z],
            self.beside_sems.at[1, slot, z],
            self.at.beside,
        )

    def line_copy(self, p, m, z, up):
        slot, way = m % 2, 0 if up else 1
        into = z + 1 if up else z
        return remote(
            self.block(p, 2 * z + self.at.y),
            self.line_in.at[slot, into],
            self.line_sems.at[way, slot, z],
            self.line_sems.at[2, slot, into],
            self.at.upper if up else self.at.lower,
        )

    def pair_copy(self, p, z, up):
        into = z + 1 if up else z
        return remote(
            self.block(p, 2 * z, 2),
            self.pair_in.at[into],
            self.pair_sems.at[0 if up else 1, z],
            self.pair_sems.at[2, into],
            self.at.upper if up else self.at.lower,
        )

    def send_beside(self, p, m, dropped):
        if m >= 2:
            pl.semaphore_wait(self.credits.at[0], 1)

        def step(s, carry):
            z = (s % 2) * (s // 2) + (1 - s % 2) * (self.at.depth - 1 - s // 2)
            if dropped is not None:
                self.beside_copy(dropped, m, z).wait_send()
            self.beside_copy(p, m, z).start()
            return carry

        lax.fori_loop(0, self.at.depth, step, 0)

    def line(self, p, m, dropped):
        at, chunk = self.at, self.chunk
        total = self.total.at[pl.ds(0, chunk), :]
        if m >= 2:
            for has, credit in ((at.has_upper, 1), (at.has_lower, 2)):

                @pl.when(has)
                def _():
                    pl.semaphore_wait(self.credits.at[credit], 1)

            self.drop(dropped, m)

        def gather(z, behind, up):
            own = self.block(p, 2 * z + at.y)
            self.beside_copy(p, m, z).wait_recv()
            total[...] = own[...].astype(f32) + self.beside_in[m % 2, z].astype(f32)
            for has, goes_up in behind:

                @pl.when(has)
                def _():
                    self.line_copy(p, m, z, goes_up).wait_recv()
                    total[...] += self.line_in[m % 2, z + 1 if goes_up else z].astype(f32)

            return own

        def step(s, carry):
            for z, wanted, has, up in (
                (at.depth - 1 - s, at.depth - 1 - s > at.z, at.has_lower, True),
                (s, s < at.z, at.has_upper, False),
            ):

                @pl.when(wanted)
                def _():
                    own = gather(z, ((has, up),), up)
                    own[...] = total[...].astype(bf16)
                    self.line_copy(p, m, z, up).start()

            return carry

        lax.fori_loop(0, at.depth - 1, step, 0)
        gather(at.z, ((at.has_lower, True), (at.has_upper, False)), True)
        if m + 2 < self.count:
            pl.semaphore_signal(self.credits.at[0], 1, device_id=at.beside, device_id_type=MESH)

            @pl.when(at.has_lower)
            def _():
                pl.semaphore_signal(self.credits.at[1], 1, device_id=at.lower, device_id_type=MESH)

            @pl.when(at.has_upper)
            def _():
                pl.semaphore_signal(self.credits.at[2], 1, device_id=at.upper, device_id_type=MESH)

    def drop(self, p, m):
        at = self.at

        def step(s, carry):
            for z, wanted, up in (
                (at.depth - 1 - s, at.depth - 1 - s > at.z, True),
                (s, s < at.z, False),
            ):

                @pl.when(wanted)
                def _():
                    self.line_copy(p, m, z, up).wait_send()

            return carry

        lax.fori_loop(0, at.depth - 1, step, 0)

    def drop_beside(self, p, m):
        def step(z, carry):
            self.beside_copy(p, m, z).wait_send()
            return carry

        lax.fori_loop(0, self.at.depth, step, 0)

    def pair_steps(self, p, at_ends, act):
        at = self.at

        def step(s, carry):
            for z, wanted, behind, up in (
                (at.depth - 1 - s, at.depth - 1 - s > at.z, at.has_lower, True),
                (s, s < at.z, at.has_upper, False),
            ):
                ok = wanted
                if at_ends is True:
                    ok = jnp.logical_and(wanted, jnp.logical_not(behind))
                elif at_ends is False:
                    ok = jnp.logical_and(wanted, behind)

                @pl.when(ok)
                def _():
                    act(z, up)

            return carry

        lax.fori_loop(0, at.depth - 1, step, 0)

    def pairs_open(self, p):
        self.pair_steps(p, True, lambda z, up: self.pair_copy(p, z, up).start())

    def pair_y_copy(self, p):
        at = self.at
        return remote(
            self.block(p, 2 * at.z + 1 - at.y),
            self.pair_beside,
            self.pair_y_sems.at[0],
            self.pair_y_sems.at[1],
            at.beside,
        )

    def pairs(self, p):
        at, total, chunk = self.at, self.total, self.chunk

        def add(z, up):
            self.pair_copy(p, z, up).wait_recv()
            total[...] += self.pair_in[z + 1 if up else z].astype(f32)

        def on(z, up):
            own = self.block(p, 2 * z, 2)
            total[...] = own[...].astype(f32)
            add(z, up)
            own[...] = total[...].astype(bf16)
            self.pair_copy(p, z, up).start()

        self.pair_steps(p, False, on)
        total[...] = self.block(p, 2 * at.z, 2)[...].astype(f32)
        for has, up in ((at.has_lower, True), (at.has_upper, False)):

            @pl.when(has)
            def _():
                add(at.z, up)

        other = self.block(p, 2 * at.z + 1 - at.y)
        other[...] = total[rows_of((1 - at.y) * chunk, chunk), :].astype(bf16)
        self.pair_y_copy(p).start()

    def pairs_close(self, p):
        at, total, chunk = self.at, self.total, self.chunk
        self.pair_y_copy(p).wait()
        mine = total[rows_of(at.y * chunk, chunk), :] + self.pair_beside[...].astype(f32)
        total[pl.ds(0, chunk), :] = mine
        self.pair_steps(p, None, lambda z, up: self.pair_copy(p, z, up).wait_send())


def backward_kernel(
    ndp,
    held_in,
    normed_in,
    normed_two_in,
    grad_rows_in,
    streams_in,
    gates_in,
    first_in,
    grad_in,
    small,
    loss,
    tokens,
    grads_out,
    tokens_grad,
    small_out,
    held,
    rows_a,
    rows_b,
    acc,
    gates,
    streams,
    core_out,
    core_in,
    far_out,
    far_in,
    first,
    grad,
    back,
    gated,
    beside_in,
    line_in,
    pair_in,
    pair_beside,
    total,
    done,
    cur,
    got,
    share_sems,
    core_sems,
    far_sems,
    cube_sems,
    load_sems,
    held_sems,
    gate_sems,
    beside_sems,
    line_sems,
    pair_sems,
    pair_y_sems,
    done_sems,
    credits,
):
    at = place(ndp)
    pieces, width, piece = held.shape
    rows = tokens.shape[0]
    sub = rows // NSUB
    chunk = 2 * width // ndp
    half = chunk // 2
    channels = piece // 2
    order = list(range(2, pieces)) + [0, 1]
    share = Share(at, rows_a, rows, share_sems)
    sums = Sums(at, acc, rows, core_out, core_in, far_out, far_in, core_sems, far_sems)
    scatter = Scatter(
        at,
        held,
        chunk,
        pieces - 1,
        beside_in,
        line_in,
        pair_in,
        pair_beside,
        total,
        (beside_sems, line_sems, pair_sems, pair_y_sems),
        credits,
    )

    def load(src, dst, k):
        return pltpu.make_async_copy(src, dst, load_sems.at[k])

    def load_held(p):
        return pltpu.make_async_copy(held_in.at[p], held.at[p], held_sems.at[p])

    def load_gates(p):
        return pltpu.make_async_copy(gates_in.at[p - 2], gates.at[p % 2], gate_sems.at[p % 2])

    def load_streams(r):
        return load(streams_in.at[pl.ds(r * 2 * rows, 2 * rows), :], streams, 5)

    opening = (
        load(grad_rows_in, rows_a, 0),
        load_gates(2),
        load_held(2),
        load(normed_two_in, rows_b, 1),
    )
    for copy in opening:
        copy.start()
    load_gates(3).start()
    for p in order[1:]:
        load_held(p).start()
    load_first, load_grad = load(first_in, first, 2), load(grad_in, grad, 3)
    load_first.start()
    load_grad.start()
    load_streams(0).start()
    meet(at)
    acc[...] = jnp.zeros_like(acc)
    opening[0].wait()
    opening[3].wait()

    def ffn(p):
        load_gates(p).wait()
        load_held(p).wait()

        def some(r, carry):
            part = rows_of(((r + 1 - at.core) % 2) * 2 * rows, 2 * rows)
            grad_hidden = nn(rows_a[part, :], held[p, :, 2 * LANES :])
            gate = gates[p % 2, part, 0:LANES].astype(f32)
            up = gates[p % 2, part, LANES:].astype(f32)
            sig = jax.nn.sigmoid(gate)
            active = gate * sig
            back[part, 2 * LANES : 3 * LANES] = (active * up).astype(bf16)
            grad_gate = grad_hidden * up * sig * (1.0 + gate * (1.0 - sig))
            back[part, 0:LANES] = grad_gate.astype(bf16)
            back[part, LANES : 2 * LANES] = (grad_hidden * active).astype(bf16)
            acc[part, :] += nt(back[part, 0 : 2 * LANES], held[p, :, 0 : 2 * LANES])
            return carry

        lax.fori_loop(0, 2, some, 0)

        def weights(i, carry):
            part = rows_of(i * piece // 2, piece // 2, 128)
            held[p, part, 0 : 2 * LANES] = tn(rows_b[:, part], back[:, 0 : 2 * LANES]).astype(bf16)
            held[p, part, 2 * LANES :] = tn(rows_a[:, part], back[:, 2 * LANES : 3 * LANES]).astype(bf16)
            return carry

        lax.fori_loop(0, 2 * width // piece, weights, 0)

    def ffn_at(k):
        p = order[k]
        ffn(p)
        if p + 2 < pieces:
            load_gates(p + 2).start()

    def out_local(k):
        src = done.at[k % 2, rows_of(at.core * half, half, 8), :]
        return pltpu.make_async_copy(src, grads_out.at[at.core, order[k]], done_sems.at[0, order[k]])

    def out_sib(k):
        src = done.at[k % 2, rows_of((1 - at.core) * half, half, 8), :]
        dst = grads_out.at[at.core, order[k]]
        return remote(src, dst, done_sems.at[1, order[k]], done_sems.at[2, order[k]], at.sib)

    def from_sib(k):
        src = done.at[k % 2, rows_of((1 - at.core) * half, half, 8), :]
        dst = grads_out.at[1 - at.core, order[k]]
        return remote(src, dst, done_sems.at[1, order[k]], done_sems.at[2, order[k]], at.sib)

    def give(k):
        if k >= 2:
            out_local(k - 2).wait()
            out_sib(k - 2).wait_send()
        done[k % 2] = total[pl.ds(0, chunk), :]
        out_local(k).start()
        out_sib(k).start()

    def beside(k):
        scatter.send_beside(order[k], k - 1, order[k - 2] if k >= 3 else None)

    def line(k):
        scatter.line(order[k], k - 1, order[k - 2] if k >= 3 else None)
        give(k)

    gain_one, gain_two = small[0:1, :], small[1:2, :]
    ffn_at(0)
    scatter.pairs_open(order[0])
    ffn_at(1)
    beside(1)
    scatter.pairs(order[0])
    ffn_at(2)
    beside(2)
    scatter.pairs_close(order[0])
    give(0)
    ffn_pieces = pieces - 2
    for k in range(3, ffn_pieces):
        ffn_at(k)
        if k == ffn_pieces - 1:
            sums.to_core()
            load_normed = load(normed_in, rows_b, 4)
            load_normed.start()
        line(k - 2)
        beside(k)
    sums.to_far()
    line(ffn_pieces - 2)
    load_first.wait()
    load_grad.wait()
    gain_two_grad = jnp.zeros((1, width), f32)
    for j in range(NSUB):
        part = rows_of(j * sub, sub)
        coming = sums.take(j)
        source = first[part, :]
        inverse = inverse_of(source)
        weighted = coming * gain_two
        inner = jnp.mean(weighted * source, axis=1, keepdims=True)
        value = grad[part, :] + inverse * weighted - source * (inverse * inverse * inverse * inner)
        grad[part, :] = value
        gain_two_grad += jnp.sum(coming * source * inverse, axis=0, keepdims=True)
        rows_a[rows_of(at.own * rows + j * sub, sub), :] = value.astype(bf16)
        share.start(j)
    sums.finish()
    for j in range(NSUB):
        share.forward(j)
    share.finish()
    lane = at.x * 2 * channels + at.core * channels
    cur[0] = jnp.zeros(cur.shape[1:], f32)
    cur[0, 1:2, :] = gain_two_grad
    cur[0, 5:6, :] = jnp.broadcast_to(loss[0:1, 0:1], (1, width))
    taps = small[2:5, rows_of(lane, channels, 128)]
    load_held(0).wait()
    load_held(1).wait()
    for r in range(2):
        load_streams(r).wait()
        part = pl.ds(r * 2 * rows, 2 * rows)
        b_gate, c_gate = streams[:, 0:channels], streams[:, channels : 2 * channels]
        x_stream = streams[:, 2 * channels :]
        mixed = b_gate * x_stream
        convolved = convolve(mixed, taps)
        grad_gated = nn(rows_a[part, :], held[1, :, channels:])
        gated[part, :] = (c_gate * convolved).astype(bf16)
        back[part, channels : 2 * channels] = (grad_gated * convolved).astype(bf16)
        grad_conv = grad_gated * c_gate
        grad_mixed = taps[2:3] * grad_conv
        grad_mixed += taps[1:2] * shifted(grad_conv, -1) + taps[0:1] * shifted(grad_conv, -2)
        for k in range(3):
            tap = jnp.sum(grad_conv * shifted(mixed, 2 - k), axis=0, keepdims=True)
            cur[0, 2 + k : 3 + k, rows_of(lane, channels, 128)] += tap
        back[part, 0:channels] = (grad_mixed * x_stream).astype(bf16)
        back[part, 2 * channels :] = (grad_mixed * b_gate).astype(bf16)
        if r == 0:
            load_streams(1).start()
        value = nt(back[part, 0 : 2 * channels], held[0])
        acc[part, :] = value + nt(back[part, 2 * channels :], held[1, :, 0:channels])
    sums.to_core()
    load_normed.wait()

    def mixer_weights(i, carry):
        part = rows_of(i * channels, channels, 128)
        left = rows_b[:, part]
        held[0, part, :] = tn(left, back[:, 0 : 2 * channels]).astype(bf16)
        held[1, part, 0:channels] = tn(left, back[:, 2 * channels :]).astype(bf16)
        held[1, part, channels:] = tn(rows_a[:, part], gated[...]).astype(bf16)
        return carry

    lax.fori_loop(0, width // channels, mixer_weights, 0)
    beside(pieces - 2)
    sums.to_far()
    line(pieces - 3)
    beside(pieces - 1)
    gain_one_grad = jnp.zeros((1, width), f32)
    for j in range(NSUB):
        part = rows_of(j * sub, sub)
        coming = sums.take(j)
        source = tokens[part, :].astype(f32)
        inverse = inverse_of(source)
        weighted = coming * gain_one
        inner = jnp.mean(weighted * source, axis=1, keepdims=True)
        grad[part, :] += inverse * weighted - source * (inverse * inverse * inverse * inner)
        gain_one_grad += jnp.sum(coming * source * inverse, axis=0, keepdims=True)
    sums.finish()
    tokens_copy = load(grad, tokens_grad, 6)
    tokens_copy.start()
    cur[0, 0:1, :] = gain_one_grad
    line(pieces - 2)
    for step in range(len(at.cube)):
        total_step(at, step, cur, got, cube_sems.at[0], cube_sems.at[1])
    small_out[...] = cur[len(at.cube)]
    line(pieces - 1)
    for k in (pieces - 2, pieces - 1):
        scatter.drop_beside(order[k], k - 1)
        scatter.drop(order[k], k - 1)
        out_local(k).wait()
        out_sib(k).wait_send()
    for k in range(pieces):
        from_sib(k).wait_recv()
    tokens_copy.wait()


def backward(ndp, held, normed, normed_two, grad_rows, streams, gates, first, grad, small, loss, tokens):
    pieces, width, piece = held.shape
    rows = tokens.shape[0]
    chunk = 2 * width // ndp
    depth = ndp // 4
    channels = piece // 2
    cube = small_steps(ndp)
    dma = pltpu.SemaphoreType.DMA
    shape = jax.ShapeDtypeStruct
    outs = (
        shape((2, pieces, chunk // 2, piece), f32),
        shape((rows, width), f32),
        shape((8, width), f32),
    )
    scratch = [
        pltpu.VMEM((pieces, width, piece), bf16),
        pltpu.VMEM((4 * rows, width), bf16),
        pltpu.VMEM((4 * rows, width), bf16),
        pltpu.VMEM((4 * rows, width), f32),
        pltpu.VMEM((2, 4 * rows, 2 * LANES), bf16),
        pltpu.VMEM((2 * rows, 3 * channels), f32),
        pltpu.VMEM((2, rows, width), bf16),
        pltpu.VMEM((2, rows, width), bf16),
        pltpu.VMEM((rows, width), bf16),
        pltpu.VMEM((rows, width), bf16),
        pltpu.VMEM((rows, width), f32),
        pltpu.VMEM((rows, width), f32),
        pltpu.VMEM((4 * rows, 3 * channels), bf16),
        pltpu.VMEM((4 * rows, channels), bf16),
        pltpu.VMEM((2, depth, chunk, piece), bf16),
        pltpu.VMEM((2, depth + 1, chunk, piece), bf16),
        pltpu.VMEM((depth + 1, 2 * chunk, piece), bf16),
        pltpu.VMEM((chunk, piece), bf16),
        pltpu.VMEM((2 * chunk, piece), f32),
        pltpu.VMEM((2, chunk, piece), f32),
        pltpu.VMEM((cube + 1, 8, width), f32),
        pltpu.VMEM((cube, 8, width), f32),
        dma((6, NSUB)),
        dma((2, 2, NSUB)),
        dma((2, NSUB)),
        dma((2, cube)),
        dma((7,)),
        dma((pieces,)),
        dma((2,)),
        dma((2, 2, depth)),
        dma((3, 2, depth + 1)),
        dma((3, depth + 1)),
        dma((2,)),
        dma((3, pieces)),
        pltpu.SemaphoreType.REGULAR((3,)),
    ]
    return pl.pallas_call(
        functools.partial(backward_kernel, ndp),
        out_shape=outs,
        in_specs=[ANY] * 8 + [VMEM] * 3,
        out_specs=[ANY, ANY, VMEM],
        scratch_shapes=scratch,
        compiler_params=pltpu.CompilerParams(
            collective_id=1, has_side_effects=True, vmem_limit_bytes=63 << 20
        ),
    )(held, normed, normed_two, grad_rows, streams, gates, first, grad, small, loss, tokens)


def body(
    tokens,
    teacher,
    valid,
    mixer_gain,
    in_weight,
    conv_weight,
    out_weight,
    ffn_gain,
    gate_weight,
    up_weight,
    down_weight,
):
    ndp = lax.axis_size("dp")
    place_of = lax.axis_index("dp") * 2 + lax.axis_index("tensor")
    width = tokens.shape[1]
    valid_f = valid.astype(f32)
    vectors = jnp.concatenate([mixer_gain[None], ffn_gain[None], conv_weight], axis=0).astype(f32)
    share = vectors.shape[1]
    small = jnp.zeros((5, width), f32)
    small = lax.dynamic_update_slice(small, vectors, (0, place_of * share))
    small = jnp.concatenate([small, jnp.full((3, width), jnp.sum(valid_f), f32)], axis=0)
    shards = shard_pieces(in_weight, out_weight, gate_weight, up_weight, down_weight)
    held, normed, normed_two, grad_rows, streams, gates, first, block_out, grad, small, loss = forward(
        ndp, shards, tokens, teacher, valid_f[:, None], small
    )
    grads, tokens_grad, small_grads = backward(
        ndp, held, normed, normed_two, grad_rows, streams, gates, first, grad, small, loss, tokens
    )
    part_rows, _, channels = in_weight.shape
    channels //= 2
    units = gate_weight.shape[1]
    mixer = grads[:, 0:2].transpose(0, 2, 1, 3).reshape(2, part_rows, 4 * channels)
    in_grad = mixer[:, :, 0 : 3 * channels].reshape(2, part_rows, 3, channels)
    in_grad = in_grad.transpose(1, 2, 0, 3).reshape(part_rows, 3, 2 * channels)
    out_grad = mixer[:, :, 3 * channels :].transpose(1, 0, 2).reshape(part_rows, 2 * channels)

    def joined(k):
        cut = grads[:, 2:, :, k * LANES : (k + 1) * LANES]
        return cut.transpose(2, 0, 1, 3).reshape(part_rows, -1)[:, 0:units]

    own = lax.dynamic_slice(small_grads, (0, place_of * share), (5, share))
    return (
        small_grads[5, 0] / (width * small[5, 0]),
        block_out,
        tokens_grad,
        own[0],
        in_grad,
        own[2:5],
        out_grad,
        own[1],
        joined(0),
        joined(1),
        joined(2),
    )


def solution(mesh):
    rows = P(("dp", "tensor"), None)
    vector = P(("dp", "tensor"))
    weight = P("dp", "tensor")
    streams = P("dp", None, "tensor")
    taps = P(None, ("dp", "tensor"))
    return jax.shard_map(
        body,
        mesh=mesh,
        in_specs=(rows, rows, vector, vector, streams, taps, weight, vector, weight, weight, weight),
        out_specs=(P(), rows, rows, vector, streams, taps, weight, vector, weight, weight, weight),
        check_vma=False,
    )
```

time: 1770 us -> 745 us (0.42)
  waiting for transfers between devices: 1370 us -> 0 us
  Pallas kernels: 0 us -> 695 us
  blocking collectives: 187 us -> 0 us
  matrix products: 145 us -> 0 us
  local copies, waits for them, and re-layouts: 14.7 us -> 37.9 us
  other arithmetic: 24 us -> 3.76 us
    reduce_scatter x9 -> x0, waiting for transfers between devices: 957 us -> none  [the longest x1 217 us: body(): lax.psum_scatter(grad_down, 'dp', scatter_dimension=0, tiled=True)]
    pallas_call x0 -> x2, Pallas kernels: none -> 695 us  [the longest x1 368 us: backward(): pl.pallas_call(functools.partial(backward_kernel, ndp), out_shape=outs, i...]
    all_gather x9 -> x0, waiting for transfers between devices: 381 us -> none  [the longest x1 86.3 us: ffn_params(): lax.all_gather(gate_weight, 'dp', axis=0, tiled=True)]
    dot_general x15 -> x0, matrix products: 145 us -> none  [the longest x4 40.3 us: contract_rows(): lax.dot_general(left, right, (((0,), (0,)), ((), ())), preferred_element_...]
    psum x2 -> x0, blocking collectives: 79 us -> none  [body(): lax.psum((jnp.sum(valid_f), loss_local), ('dp', 'tensor'))]
    all_gather x1 -> x0, blocking collectives: 66.2 us -> none  [body(): lax.all_gather(conv_weight, ('dp', 'tensor'), axis=1, tiled=True)]
    unnamed x1 -> x0, blocking collectives: 42.1 us -> none
    unnamed x20 -> x0, waiting for transfers between devices: 35.8 us -> none
  transfers between devices with their start and end apart: 19 -> 0, of which waited for: 17 -> 0; matrix products, arithmetic and copies ran while one was open for 6% -> 0% of each run, Pallas kernels for 0% -> 0%
where the time goes in v1:
time: 745 us; the launch traced here: 740 us
  Pallas kernels  695 us (93%)
  local copies, waits for them, and re-layouts  37.9 us (5%)
    pallas_call x1, Pallas kernels, backward(): pl.pallas_call(functools.partial(backward_kernel, ndp), out_shape=outs, i...  368 us
    pallas_call x1, Pallas kernels, forward(): pl.pallas_call(functools.partial(forward_kernel, ndp, early_y), out_shape...  327 us

profile of v1, /device:TPU:0, one launch (start us, length us, event | category | flops | bytes accessed | tf_op | source)
XLA Modules:
  0.0 740.4 jit_solution(11105929730660988714)
XLA Ops:
  0.7 0.7 maximum_convert_fusion
  1.4 0.0 copy-start.2
  1.4 0.3 dynamic_update_slice.3
  1.6 1.3 convert_reduce_fusion
  2.9 1.3 concatenate.19.small
  4.2 1.1 pad.12
  5.3 0.8 reshape.72
  6.2 0.8 reshape.73
  7.0 0.0 copy-start.4
  7.0 0.5 copy_bitcast_fusion
  7.5 0.5 copy-done.4
  8.0 0.1 reshape.67
  8.1 0.4 copy.59
  8.5 0.4 reshape.68
  8.9 0.0 copy-start.3
  8.9 0.0 copy-done.5
  9.0 0.9 copy-done.3
  10.0 0.8 reshape.71
  10.8 0.2 copy.57
  11.1 0.0 copy-start.6
  11.1 1.7 maximum_maximum_fusion.shards
  12.8 0.8 copy.40.valid
  13.6 327.5 %shard_map.194 = (bf16[9,1536,768]{2,1,0:T(8,128)(2,1)}, bf16[960,1536]{1,0:T(8,128)(2,1)}, bf16[960,1536]{1,0:T(8,128)(2,1)}, bf16[960,1536]{1,0:T(8,128)(2,1)}...) custom-call(bf16[2,9,96,768]{3,2,1,0:T(8,128)(2,1)} %maximum_maximum, ...), custom_call_target="tpu_custom_call" | custom-call | tf_op jit(solution)/shard_map/pallas_call | solution.py:579
  341.1 367.7 %shard_map.195 = (f32[2,9,96,768]{3,2,1,0:T(8,128)}, f32[240,1536]{1,0:T(8,128)}, f32[8,1536]{1,0:T(8,128)}) custom-call(bf16[9,1536,768]{2,1,0:T(8,128)(2,1)} %get-tuple-element.25.held_in, bf16[960,1536]{1,0:T(8,128)(2,1)} %get-tuple-element.26.normed_in, bf16[960,1536]{1,0:T(8,128)(2,1)} %get-tuple-element.27.normed_two_in, ...), custom_call_target="tpu_custom_call" | custom-call | tf_op jit(solution)/shard_map/pallas_call | solution.py:1149
  708.7 3.7 slice_bitcast_fusion
  712.4 0.8 copy.44
  713.2 1.6 reshape.78
  714.8 2.6 slice.58
  717.4 0.8 copy.45
  718.2 1.6 reshape.79
  719.7 2.5 slice.59
  722.2 0.8 copy.46
  723.0 0.5 reshape.80
  723.5 1.2 slice.60
  724.6 1.3 slice_bitcast_fusion.3
  726.0 0.1 copy.49
  726.1 0.1 slice.56
  726.2 0.4 reshape.75
  726.6 0.7 copy.42
  727.3 1.6 reshape.76
  728.9 0.7 copy.50
  729.6 0.8 constant_dynamic-slice_fusion
  730.4 0.6 slice.47
  731.0 0.5 slice_bitcast_fusion.5
  731.5 1.2 slice.42
  732.7 1.2 slice.43
  735.2 2.7 copy.64
  737.9 1.1 copy.65
  (15 shorter events, 0.2 us)
Async XLA Ops:
  1.4 4.8 copy-start.2
  7.0 1.0 copy-start.4
  8.0 0.9 copy-start.5
  8.9 1.1 copy-start.3
  11.1 1.7 copy-start.6
  714.8 2.6 copy-start
  735.2 2.7 copy-start.1

commit v2 on v1

--- a/solution.py
+++ b/solution.py
@@ -14,6 +14,8 @@
 norm_eps = 1e-05
 LANES = 256
 NSUB = 3
+YDEPTH, ZDEPTH = 3, 4
+AHEAD = 4
 VMEM = pl.BlockSpec(memory_space=pltpu.VMEM)
 ANY = pl.BlockSpec(memory_space=pl.ANY)
 
@@ -65,11 +67,19 @@
     )
 
 
-def total_step(at, step, cur, got, send, recv):
-    copy = remote(cur.at[step], got.at[step], send.at[step], recv.at[step], at.cube[step])
-    copy.start()
+def total_copy(at, step, cur, got, send, recv):
+    return remote(cur.at[step], got.at[step], send.at[step], recv.at[step], at.cube[step])
+
+
+def total_end(at, step, cur, got, copy):
     copy.wait()
     cur[step + 1] = cur[step] + got[step]
+
+
+def total_step(at, step, cur, got, send, recv):
+    copy = total_copy(at, step, cur, got, send, recv)
+    copy.start()
+    total_end(at, step, cur, got, copy)
 
 
 class Share:
@@ -102,9 +112,9 @@
 
 
 class Sums:
-    def __init__(self, at, acc, rows, core_out, core_in, far_out, far_in, core_sems, far_sems):
+    def __init__(self, at, acc, rows, core_out, core_in, far_in, core_sems, far_sems):
         self.at, self.acc, self.rows = at, acc, rows
-        self.core_out, self.core_in, self.far_out, self.far_in = core_out, core_in, far_out, far_in
+        self.core_out, self.core_in, self.far_in = core_out, core_in, far_in
         self.core_sems, self.far_sems = core_sems, far_sems
         self.sub = rows // NSUB
 
@@ -124,7 +134,7 @@
     def far_copy(self, j):
         part = rows_of(j * self.sub, self.sub)
         return remote(
-            self.far_out.at[part, :],
+            self.core_in.at[0, part, :],
             self.far_in.at[part, :],
             self.far_sems.at[0, j],
             self.far_sems.at[1, j],
@@ -142,7 +152,7 @@
             part = rows_of(j * self.sub, self.sub)
             self.core_copy(0, j).wait_recv()
             both = self.of(self.at.own_across, j) + self.core_in[0, part, :].astype(f32)
-            self.far_out[part, :] = both.astype(bf16)
+            self.core_in[0, part, :] = both.astype(bf16)
             self.far_copy(j).start()
 
     def take(self, j):
@@ -296,7 +306,6 @@
     gates,
     core_out,
     core_in,
-    far_out,
     far_in,
     first,
     result,
@@ -327,7 +336,7 @@
     gather = Gather(at, held, chunk, early_y, (recv_sems, own_sems, send_sems))
     share_a = Share(at, rows_a, rows, share_sems)
     share_b = Share(at, rows_b, rows, share_sems)
-    sums = Sums(at, acc, rows, core_out, core_in, far_out, far_in, core_sems, far_sems)
+    sums = Sums(at, acc, rows, core_out, core_in, far_in, core_sems, far_sems)
 
     def half(p, core):
         return held.at[p, rows_of(at.chip * chunk + core * part_rows, part_rows), :]
@@ -356,23 +365,29 @@
         gather.own(p, go)
 
     meet(at)
+    to_sib(0).start()
+    keep(0).start()
+    cur[0] = small[...]
+    total_step(at, 0, cur, got, cube_sems.at[0], cube_sems.at[1])
+    own_block(0)
+    total_step(at, 1, cur, got, cube_sems.at[0], cube_sems.at[1])
     for j in range(NSUB):
         rows_a[rows_of(at.own * rows + j * sub, sub), :] = tokens[pl.ds(j * sub, sub), :]
         share_a.start(j)
-    for p in range(pieces):
+    for p in range(1, pieces):
         to_sib(p).start()
         keep(p).start()
-    own_block(0)
-    own_block(1)
-    cur[0] = small[...]
-    for step in range(len(at.cube)):
+    for step in range(2, len(at.cube)):
         total_step(at, step, cur, got, cube_sems.at[0], cube_sems.at[1])
+        if step < 4:
+            own_block(step - 1)
     last = len(at.cube)
     small_out[...] = cur[last]
-    own_block(2)
     for j in range(NSUB):
         share_a.forward(j)
     gain_one, gain_two = cur[last, 0:1, :], cur[last, 1:2, :]
+    relay = lambda p: gather.relay(p, p % AHEAD, (p - AHEAD, p - AHEAD in early_y) if p >= AHEAD else None)
+    relay(0)
     share_a.finish()
 
     def norm_rows(i, carry):
@@ -388,10 +403,11 @@
     def save(p):
         return pltpu.make_async_copy(held.at[p], held_out.at[p], held_sems.at[p])
 
-    gather.relay(0, 0, None)
     own_block(3)
-    gather.relay(1, 1, None)
+    relay(1)
     own_block(4)
+    relay(2)
+    own_block(5)
     for p in (0, 1):
         gather.whole(p)
         save(p).start()
@@ -413,14 +429,11 @@
     streams_copy = pltpu.make_async_copy(streams, streams_out, out_sems.at[1])
     streams_copy.start()
     sums.to_core()
-    gather.relay(2, 0, (0, 0 in early_y))
-    own_block(5)
+    own_block(6)
+    own_block(7)
     sums.to_far()
-    own_block(6)
-    gather.relay(3, 1, (1, 1 in early_y))
-    own_block(7)
-    own_block(8)
-    for p in range(9, pieces):
+    relay(3)
+    for p in range(8, pieces):
         own_block(p)
     for j in range(NSUB):
         part = rows_of(j * sub, sub)
@@ -432,7 +445,7 @@
     sums.finish()
     first_copy = pltpu.make_async_copy(first, first_out, out_sems.at[2])
     first_copy.start()
-    gather.relay(4, 0, (2, 2 in early_y))
+    relay(4)
     for j in range(NSUB):
         share_b.forward(j)
     share_b.finish()
@@ -445,17 +458,11 @@
         return pltpu.make_async_copy(gates.at[slot], gates_out.at[p - 2], gate_sems.at[slot])
 
     def feed(p, carry):
-        @pl.when(p >= 5)
-        def _():
-            parity = p % 2
-
-            @pl.when(p == 5)
+        for q in range(5, pieces):
+
+            @pl.when(p == q - 3)
             def _():
-                gather.relay(p, parity, (3, 3 in early_y))
-
-            @pl.when(p > 5)
-            def _():
-                gather.relay(p, parity, (p - 2, False))
+                relay(q)
 
         for q in range(2, pieces):
             if q not in early_y:
@@ -517,8 +524,9 @@
         gather.own(p, lambda copy: copy.wait_send())
         if p in early_y:
             gather.own_z(p, 2 * at.z, 2, lambda copy: copy.wait_send())
+    for p in range(pieces - AHEAD, pieces):
+        gather.passing(p, p in early_y, p % AHEAD, False, lambda copy: copy.wait_send())
     for p in (pieces - 2, pieces - 1):
-        gather.passing(p, p in early_y, p % 2, False, lambda copy: copy.wait_send())
         gates_copy(p).wait()
     for copy in (streams_copy, first_copy, normed_two_copy, result_copy, grad_copy, rows_copy):
         copy.wait()
@@ -558,7 +566,6 @@
         pltpu.VMEM((2, rows, width), bf16),
         pltpu.VMEM((2, rows, width), bf16),
         pltpu.VMEM((rows, width), bf16),
-        pltpu.VMEM((rows, width), bf16),
         pltpu.VMEM((rows, width), f32),
         pltpu.VMEM((rows, width), f32),
         pltpu.VMEM((rows, width), f32),
@@ -567,7 +574,7 @@
         dma((3, pieces)),
         dma((pieces, ndp // 2)),
         dma((3, pieces)),
-        dma((3, 2, ndp // 4)),
+        dma((3, AHEAD, ndp // 4)),
         dma((6, NSUB)),
         dma((2, 2, NSUB)),
         dma((2, NSUB)),
@@ -617,12 +624,13 @@
         self.beside_in, self.line_in, self.pair_in, self.pair_beside = beside_in, line_in, pair_in, pair_beside
         self.total, self.credits = total, credits
         self.beside_sems, self.line_sems, self.pair_sems, self.pair_y_sems = sems
+        self.ydepth, self.zdepth = beside_in.shape[0], line_in.shape[0]
 
     def block(self, p, chip, count=1):
         return self.held.at[p, rows_of(chip * self.chunk, count * self.chunk), :]
 
     def beside_copy(self, p, m, z):
-        slot = m % 2
+        slot = m % self.ydepth
         return remote(
             self.block(p, 2 * z + 1 - self.at.y),
             self.beside_in.at[slot, z],
@@ -632,7 +640,7 @@
         )
 
     def line_copy(self, p, m, z, up):
-        slot, way = m % 2, 0 if up else 1
+        slot, way = m % self.zdepth, 0 if up else 1
         into = z + 1 if up else z
         return remote(
             self.block(p, 2 * z + self.at.y),
@@ -652,72 +660,31 @@
             self.at.upper if up else self.at.lower,
         )
 
-    def send_beside(self, p, m, dropped):
-        if m >= 2:
+    def turn(self, s):
+        return (s % 2) * (s // 2) + (1 - s % 2) * (self.at.depth - 1 - s // 2)
+
+    def free_beside(self, p, m, before):
+        if m >= self.ydepth:
             pl.semaphore_wait(self.credits.at[0], 1)
+            self.drop_beside(before, m)
+
+    def drop_beside(self, p, m):
+        def step(z, carry):
+            self.beside_copy(p, m, z).wait_send()
+            return carry
+
+        lax.fori_loop(0, self.at.depth, step, 0)
+
+    def send_beside(self, p, m, before):
+        self.free_beside(p, m, before)
 
         def step(s, carry):
-            z = (s % 2) * (s // 2) + (1 - s % 2) * (self.at.depth - 1 - s // 2)
-            if dropped is not None:
-                self.beside_copy(dropped, m, z).wait_send()
-            self.beside_copy(p, m, z).start()
+            self.beside_copy(p, m, self.turn(s)).start()
             return carry
 
         lax.fori_loop(0, self.at.depth, step, 0)
 
-    def line(self, p, m, dropped):
-        at, chunk = self.at, self.chunk
-        total = self.total.at[pl.ds(0, chunk), :]
-        if m >= 2:
-            for has, credit in ((at.has_upper, 1), (at.has_lower, 2)):
-
-                @pl.when(has)
-                def _():
-                    pl.semaphore_wait(self.credits.at[credit], 1)
-
-            self.drop(dropped, m)
-
-        def gather(z, behind, up):
-            own = self.block(p, 2 * z + at.y)
-            self.beside_copy(p, m, z).wait_recv()
-            total[...] = own[...].astype(f32) + self.beside_in[m % 2, z].astype(f32)
-            for has, goes_up in behind:
-
-                @pl.when(has)
-                def _():
-                    self.line_copy(p, m, z, goes_up).wait_recv()
-                    total[...] += self.line_in[m % 2, z + 1 if goes_up else z].astype(f32)
-
-            return own
-
-        def step(s, carry):
-            for z, wanted, has, up in (
-                (at.depth - 1 - s, at.depth - 1 - s > at.z, at.has_lower, True),
-                (s, s < at.z, at.has_upper, False),
-            ):
-
-                @pl.when(wanted)
-                def _():
-                    own = gather(z, ((has, up),), up)
-                    own[...] = total[...].astype(bf16)
-                    self.line_copy(p, m, z, up).start()
-
-            return carry
-
-        lax.fori_loop(0, at.depth - 1, step, 0)
-        gather(at.z, ((at.has_lower, True), (at.has_upper, False)), True)
-        if m + 2 < self.count:
-            pl.semaphore_signal(self.credits.at[0], 1, device_id=at.beside, device_id_type=MESH)
-
-            @pl.when(at.has_lower)
-            def _():
-                pl.semaphore_signal(self.credits.at[1], 1, device_id=at.lower, device_id_type=MESH)
-
-            @pl.when(at.has_upper)
-            def _():
-                pl.semaphore_signal(self.credits.at[2], 1, device_id=at.upper, device_id_type=MESH)
-
-    def drop(self, p, m):
+    def ways(self, has, act):
         at = self.at
 
         def step(s, carry):
@@ -726,36 +693,7 @@
                 (s, s < at.z, False),
             ):
 
-                @pl.when(wanted)
-                def _():
-                    self.line_copy(p, m, z, up).wait_send()
-
-            return carry
-
-        lax.fori_loop(0, at.depth - 1, step, 0)
-
-    def drop_beside(self, p, m):
-        def step(z, carry):
-            self.beside_copy(p, m, z).wait_send()
-            return carry
-
-        lax.fori_loop(0, self.at.depth, step, 0)
-
-    def pair_steps(self, p, at_ends, act):
-        at = self.at
-
-        def step(s, carry):
-            for z, wanted, behind, up in (
-                (at.depth - 1 - s, at.depth - 1 - s > at.z, at.has_lower, True),
-                (s, s < at.z, at.has_upper, False),
-            ):
-                ok = wanted
-                if at_ends is True:
-                    ok = jnp.logical_and(wanted, jnp.logical_not(behind))
-                elif at_ends is False:
-                    ok = jnp.logical_and(wanted, behind)
-
-                @pl.when(ok)
+                @pl.when(jnp.logical_and(wanted, has(up)))
                 def _():
                     act(z, up)
 
@@ -763,8 +701,90 @@
 
         lax.fori_loop(0, at.depth - 1, step, 0)
 
+    def behind(self, up):
+        return self.at.has_lower if up else self.at.has_upper
+
+    def opens(self, up):
+        return jnp.logical_not(self.behind(up))
+
+    def near(self, up):
+        low = self.at.z < self.at.depth // 2
+        return jnp.logical_and(self.behind(up), low if up else jnp.logical_not(low))
+
+    def far(self, up):
+        low = self.at.z < self.at.depth // 2
+        return jnp.logical_and(self.behind(up), jnp.logical_not(low) if up else low)
+
+    def add_beside(self, p, m, before):
+        at = self.at
+        if m >= self.zdepth:
+            for has, credit in ((at.has_upper, 1), (at.has_lower, 2)):
+
+                @pl.when(has)
+                def _():
+                    pl.semaphore_wait(self.credits.at[credit], 1)
+
+            self.drop(before, m)
+
+        def step(s, carry):
+            z = self.turn(s)
+            own = self.block(p, 2 * z + at.y)
+            self.beside_copy(p, m, z).wait_recv()
+            own[...] = (own[...].astype(f32) + self.beside_in[m % self.ydepth, z].astype(f32)).astype(bf16)
+            for up in (True, False):
+
+                @pl.when(jnp.logical_and(z > at.z if up else z < at.z, self.opens(up)))
+                def _():
+                    self.line_copy(p, m, z, up).start()
+
+            return carry
+
+        lax.fori_loop(0, at.depth, step, 0)
+        if m + self.ydepth < self.count:
+            pl.semaphore_signal(self.credits.at[0], 1, device_id=at.beside, device_id_type=MESH)
+
+    def hop(self, p, m, has):
+        def act(z, up):
+            self.line_copy(p, m, z, up).wait_recv()
+            own = self.block(p, 2 * z + self.at.y)
+            came = self.line_in[m % self.zdepth, z + 1 if up else z].astype(f32)
+            own[...] = (own[...].astype(f32) + came).astype(bf16)
+            self.line_copy(p, m, z, up).start()
+
+        self.ways(has, act)
+
+    def collect(self, p, m, slot):
+        at = self.at
+        total = self.total.at[slot]
+        total[...] = self.block(p, 2 * at.z + at.y)[...].astype(f32)
+        for up in (True, False):
+
+            @pl.when(self.behind(up))
+            def _():
+                self.line_copy(p, m, at.z, up).wait_recv()
+                total[...] += self.line_in[m % self.zdepth, at.z + 1 if up else at.z].astype(f32)
+                if m + self.zdepth < self.count:
+                    pl.semaphore_signal(
+                        self.credits.at[1 if up else 2],
+                        1,
+                        device_id=at.lower if up else at.upper,
+                        device_id_type=MESH,
+                    )
+
+    def drop(self, p, m):
+        self.ways(lambda up: True, lambda z, up: self.line_copy(p, m, z, up).wait_send())
+
     def pairs_open(self, p):
-        self.pair_steps(p, True, lambda z, up: self.pair_copy(p, z, up).start())
+        self.ways(self.opens, lambda z, up: self.pair_copy(p, z, up).start())
+
+    def pair_hop(self, p, has):
+        def act(z, up):
+            self.pair_copy(p, z, up).wait_recv()
+            own = self.block(p, 2 * z, 2)
+            own[...] = (own[...].astype(f32) + self.pair_in[z + 1 if up else z].astype(f32)).astype(bf16)
+            self.pair_copy(p, z, up).start()
+
+        self.ways(has, act)
 
     def pair_y_copy(self, p):
         at = self.at
@@ -776,38 +796,25 @@
             at.beside,
         )
 
-    def pairs(self, p):
-        at, total, chunk = self.at, self.total, self.chunk
-
-        def add(z, up):
-            self.pair_copy(p, z, up).wait_recv()
-            total[...] += self.pair_in[z + 1 if up else z].astype(f32)
-
-        def on(z, up):
-            own = self.block(p, 2 * z, 2)
-            total[...] = own[...].astype(f32)
-            add(z, up)
-            own[...] = total[...].astype(bf16)
-            self.pair_copy(p, z, up).start()
-
-        self.pair_steps(p, False, on)
-        total[...] = self.block(p, 2 * at.z, 2)[...].astype(f32)
-        for has, up in ((at.has_lower, True), (at.has_upper, False)):
-
-            @pl.when(has)
+    def pairs_cross(self, p):
+        at = self.at
+        own = self.block(p, 2 * at.z, 2)
+        for up in (True, False):
+
+            @pl.when(self.behind(up))
             def _():
-                add(at.z, up)
-
-        other = self.block(p, 2 * at.z + 1 - at.y)
-        other[...] = total[rows_of((1 - at.y) * chunk, chunk), :].astype(bf16)
+                self.pair_copy(p, at.z, up).wait_recv()
+                came = self.pair_in[at.z + 1 if up else at.z].astype(f32)
+                own[...] = (own[...].astype(f32) + came).astype(bf16)
+
         self.pair_y_copy(p).start()
 
-    def pairs_close(self, p):
-        at, total, chunk = self.at, self.total, self.chunk
+    def pairs_close(self, p, slot):
+        at = self.at
         self.pair_y_copy(p).wait()
-        mine = total[rows_of(at.y * chunk, chunk), :] + self.pair_beside[...].astype(f32)
-        total[pl.ds(0, chunk), :] = mine
-        self.pair_steps(p, None, lambda z, up: self.pair_copy(p, z, up).wait_send())
+        mine = self.block(p, 2 * at.z + at.y)[...].astype(f32)
+        self.total[slot] = mine + self.pair_beside[...].astype(f32)
+        self.ways(lambda up: True, lambda z, up: self.pair_copy(p, z, up).wait_send())
 
 
 def backward_kernel(
@@ -834,18 +841,15 @@
     streams,
     core_out,
     core_in,
-    far_out,
     far_in,
     first,
     grad,
     back,
-    gated,
     beside_in,
     line_in,
     pair_in,
     pair_beside,
     total,
-    done,
     cur,
     got,
     share_sems,
@@ -869,14 +873,15 @@
     chunk = 2 * width // ndp
     half = chunk // 2
     channels = piece // 2
-    order = list(range(2, pieces)) + [0, 1]
+    order = [2] + list(range(4, pieces)) + [0, 1]
+    paired = 3
     share = Share(at, rows_a, rows, share_sems)
-    sums = Sums(at, acc, rows, core_out, core_in, far_out, far_in, core_sems, far_sems)
+    sums = Sums(at, acc, rows, core_out, core_in, far_in, core_sems, far_sems)
     scatter = Scatter(
         at,
         held,
         chunk,
-        pieces - 1,
+        len(order),
         beside_in,
         line_in,
         pair_in,
@@ -907,7 +912,7 @@
     for copy in opening:
         copy.start()
     load_gates(3).start()
-    for p in order[1:]:
+    for p in list(range(3, pieces)) + [0, 1]:
         load_held(p).start()
     load_first, load_grad = load(first_in, first, 2), load(grad_in, grad, 3)
     load_first.start()
@@ -918,7 +923,7 @@
     opening[0].wait()
     opening[3].wait()
 
-    def ffn(p):
+    def ffn(p, m=None):
         load_gates(p).wait()
         load_held(p).wait()
 
@@ -938,70 +943,85 @@
 
         lax.fori_loop(0, 2, some, 0)
 
-        def weights(i, carry):
+        blocks = 2 * width // piece
+        each = at.depth // blocks
+
+        def weights(s, carry):
+            i = (s % 2) * (s // 2) + (1 - s % 2) * (blocks - 1 - s // 2)
             part = rows_of(i * piece // 2, piece // 2, 128)
             held[p, part, 0 : 2 * LANES] = tn(rows_b[:, part], back[:, 0 : 2 * LANES]).astype(bf16)
             held[p, part, 2 * LANES :] = tn(rows_a[:, part], back[:, 2 * LANES : 3 * LANES]).astype(bf16)
+            if m is not None:
+                for e in range(each):
+                    scatter.beside_copy(p, m, i * each + e).start()
             return carry
 
-        lax.fori_loop(0, 2 * width // piece, weights, 0)
-
-    def ffn_at(k):
-        p = order[k]
-        ffn(p)
+        lax.fori_loop(0, blocks, weights, 0)
         if p + 2 < pieces:
             load_gates(p + 2).start()
 
-    def out_local(k):
-        src = done.at[k % 2, rows_of(at.core * half, half, 8), :]
-        return pltpu.make_async_copy(src, grads_out.at[at.core, order[k]], done_sems.at[0, order[k]])
-
-    def out_sib(k):
-        src = done.at[k % 2, rows_of((1 - at.core) * half, half, 8), :]
-        dst = grads_out.at[at.core, order[k]]
-        return remote(src, dst, done_sems.at[1, order[k]], done_sems.at[2, order[k]], at.sib)
-
-    def from_sib(k):
-        src = done.at[k % 2, rows_of((1 - at.core) * half, half, 8), :]
-        dst = grads_out.at[1 - at.core, order[k]]
-        return remote(src, dst, done_sems.at[1, order[k]], done_sems.at[2, order[k]], at.sib)
-
-    def give(k):
-        if k >= 2:
-            out_local(k - 2).wait()
-            out_sib(k - 2).wait_send()
-        done[k % 2] = total[pl.ds(0, chunk), :]
-        out_local(k).start()
-        out_sib(k).start()
-
-    def beside(k):
-        scatter.send_beside(order[k], k - 1, order[k - 2] if k >= 3 else None)
-
-    def line(k):
-        scatter.line(order[k], k - 1, order[k - 2] if k >= 3 else None)
-        give(k)
+    given = []
+
+    def out_local(p):
+        src = total.at[given.index(p) % 2, rows_of(at.core * half, half, 8), :]
+        return pltpu.make_async_copy(src, grads_out.at[at.core, p], done_sems.at[0, p])
+
+    def out_sib(p):
+        src = total.at[given.index(p) % 2, rows_of((1 - at.core) * half, half, 8), :]
+        return remote(src, grads_out.at[at.core, p], done_sems.at[1, p], done_sems.at[2, p], at.sib)
+
+    def from_sib(p):
+        src = total.at[0, rows_of((1 - at.core) * half, half, 8), :]
+        return remote(src, grads_out.at[1 - at.core, p], done_sems.at[1, p], done_sems.at[2, p], at.sib)
+
+    def give(p, fill):
+        if len(given) > 1:
+            out_local(given[-2]).wait()
+            out_sib(given[-2]).wait_send()
+        given.append(p)
+        fill((len(given) - 1) % 2)
+        out_local(p).start()
+        out_sib(p).start()
+
+    def beside(m):
+        scatter.send_beside(order[m], m, order[m - YDEPTH] if m >= YDEPTH else None)
+
+    def finish(m):
+        give(order[m], functools.partial(scatter.collect, order[m], m))
+
+    def advance(m):
+        scatter.add_beside(order[m], m, order[m - ZDEPTH] if m >= ZDEPTH else None)
+        scatter.hop(order[m], m, scatter.near)
+        if m == 0:
+            scatter.pair_hop(paired, scatter.near)
+        if m >= 1:
+            scatter.hop(order[m - 1], m - 1, scatter.far)
+        if m == 2:
+            scatter.pair_hop(paired, scatter.far)
+        if m >= 2:
+            finish(m - 2)
+        if m == 3:
+            scatter.pairs_cross(paired)
+        if m == 4:
+            give(paired, functools.partial(scatter.pairs_close, paired))
 
     gain_one, gain_two = small[0:1, :], small[1:2, :]
-    ffn_at(0)
-    scatter.pairs_open(order[0])
-    ffn_at(1)
-    beside(1)
-    scatter.pairs(order[0])
-    ffn_at(2)
-    beside(2)
-    scatter.pairs_close(order[0])
-    give(0)
-    ffn_pieces = pieces - 2
-    for k in range(3, ffn_pieces):
-        ffn_at(k)
-        if k == ffn_pieces - 1:
-            sums.to_core()
-            load_normed = load(normed_in, rows_b, 4)
-            load_normed.start()
-        line(k - 2)
-        beside(k)
+    ffn(2, 0)
+    ffn(3)
+    scatter.pairs_open(paired)
+    ffn(4, 1)
+    ffn(5, 2)
+    advance(0)
+    ffn(6)
+    beside(3)
+    for p in range(7, pieces):
+        ffn(p)
+    sums.to_core()
+    load_normed = load(normed_in, rows_b, 4)
+    load_normed.start()
+    advance(1)
+    beside(4)
     sums.to_far()
-    line(ffn_pieces - 2)
     load_first.wait()
     load_grad.wait()
     gain_two_grad = jnp.zeros((1, width), f32)
@@ -1018,38 +1038,46 @@
         rows_a[rows_of(at.own * rows + j * sub, sub), :] = value.astype(bf16)
         share.start(j)
     sums.finish()
+    advance(2)
+    beside(5)
     for j in range(NSUB):
         share.forward(j)
     share.finish()
-    lane = at.x * 2 * channels + at.core * channels
+    shift = at.x * 2 * channels + at.core * channels
     cur[0] = jnp.zeros(cur.shape[1:], f32)
     cur[0, 1:2, :] = gain_two_grad
     cur[0, 5:6, :] = jnp.broadcast_to(loss[0:1, 0:1], (1, width))
-    taps = small[2:5, rows_of(lane, channels, 128)]
     load_held(0).wait()
     load_held(1).wait()
     for r in range(2):
         load_streams(r).wait()
         part = pl.ds(r * 2 * rows, 2 * rows)
-        b_gate, c_gate = streams[:, 0:channels], streams[:, channels : 2 * channels]
-        x_stream = streams[:, 2 * channels :]
-        mixed = b_gate * x_stream
-        convolved = convolve(mixed, taps)
-        grad_gated = nn(rows_a[part, :], held[1, :, channels:])
-        gated[part, :] = (c_gate * convolved).astype(bf16)
-        back[part, channels : 2 * channels] = (grad_gated * convolved).astype(bf16)
-        grad_conv = grad_gated * c_gate
-        grad_mixed = taps[2:3] * grad_conv
-        grad_mixed += taps[1:2] * shifted(grad_conv, -1) + taps[0:1] * shifted(grad_conv, -2)
-        for k in range(3):
-            tap = jnp.sum(grad_conv * shifted(mixed, 2 - k), axis=0, keepdims=True)
-            cur[0, 2 + k : 3 + k, rows_of(lane, channels, 128)] += tap
-        back[part, 0:channels] = (grad_mixed * x_stream).astype(bf16)
-        back[part, 2 * channels :] = (grad_mixed * b_gate).astype(bf16)
+        acc[part, 0:channels] = nn(rows_a[part, :], held[1, :, channels:])
+
+        def mix(q, carry):
+            lanes = [rows_of(k * channels + q * 128, 128, 128) for k in range(3)]
+            b_gate, c_gate, x_stream = (streams[:, lane] for lane in lanes)
+            tap = small[2:5, rows_of(shift + q * 128, 128, 128)]
+            mixed = b_gate * x_stream
+            convolved = convolve(mixed, tap)
+            grad_gated = acc[part, lanes[0]]
+            gates[0, part, lanes[0]] = (c_gate * convolved).astype(bf16)
+            back[part, lanes[1]] = (grad_gated * convolved).astype(bf16)
+            grad_conv = grad_gated * c_gate
+            grad_mixed = tap[2:3] * grad_conv
+            grad_mixed += tap[1:2] * shifted(grad_conv, -1) + tap[0:1] * shifted(grad_conv, -2)
+            for k in range(3):
+                term = jnp.sum(grad_conv * shifted(mixed, 2 - k), axis=0, keepdims=True)
+                cur[0, 2 + k : 3 + k, rows_of(shift + q * 128, 128, 128)] += term
+            back[part, lanes[0]] = (grad_mixed * x_stream).astype(bf16)
+            back[part, lanes[2]] = (grad_mixed * b_gate).astype(bf16)
+            return carry
+
+        lax.fori_loop(0, channels // 128, mix, 0)
         if r == 0:
             load_streams(1).start()
-        value = nt(back[part, 0 : 2 * channels], held[0])
-        acc[part, :] = value + nt(back[part, 2 * channels :], held[1, :, 0:channels])
+        acc[part, :] = nt(back[part, 0 : 2 * channels], held[0])
+        acc[part, :] += nt(back[part, 2 * channels :], held[1, :, 0:channels])
     sums.to_core()
     load_normed.wait()
 
@@ -1058,14 +1086,15 @@
         left = rows_b[:, part]
         held[0, part, :] = tn(left, back[:, 0 : 2 * channels]).astype(bf16)
         held[1, part, 0:channels] = tn(left, back[:, 2 * channels :]).astype(bf16)
-        held[1, part, channels:] = tn(rows_a[:, part], gated[...]).astype(bf16)
+        held[1, part, channels:] = tn(rows_a[:, part], gates[0, :, 0:channels]).astype(bf16)
         return carry
 
     lax.fori_loop(0, width // channels, mixer_weights, 0)
-    beside(pieces - 2)
+    advance(3)
+    beside(6)
     sums.to_far()
-    line(pieces - 3)
-    beside(pieces - 1)
+    advance(4)
+    beside(7)
     gain_one_grad = jnp.zeros((1, width), f32)
     for j in range(NSUB):
         part = rows_of(j * sub, sub)
@@ -1080,18 +1109,37 @@
     tokens_copy = load(grad, tokens_grad, 6)
     tokens_copy.start()
     cur[0, 0:1, :] = gain_one_grad
-    line(pieces - 2)
-    for step in range(len(at.cube)):
-        total_step(at, step, cur, got, cube_sems.at[0], cube_sems.at[1])
-    small_out[...] = cur[len(at.cube)]
-    line(pieces - 1)
-    for k in (pieces - 2, pieces - 1):
-        scatter.drop_beside(order[k], k - 1)
-        scatter.drop(order[k], k - 1)
-        out_local(k).wait()
-        out_sib(k).wait_send()
-    for k in range(pieces):
-        from_sib(k).wait_recv()
+    tally = lambda step: total_copy(at, step, cur, got, cube_sems.at[0], cube_sems.at[1])
+    for step in range(3):
+        tally(step).start()
+        if step < 2:
+            total_end(at, step, cur, got, tally(step))
+    steps = len(at.cube)
+    count = len(order)
+    for m in range(5, count):
+        advance(m)
+        step = m - 3
+        if step < steps:
+            total_end(at, step, cur, got, tally(step))
+            if step + 1 < steps:
+                tally(step + 1).start()
+    scatter.hop(order[count - 1], count - 1, scatter.far)
+    finish(count - 2)
+    finish(count - 1)
+    for step in range(count - 3, steps):
+        total_end(at, step, cur, got, tally(step))
+        if step + 1 < steps:
+            tally(step + 1).start()
+    small_out[...] = cur[steps]
+    for m in range(count - YDEPTH, count):
+        scatter.drop_beside(order[m], m)
+    for m in range(count - ZDEPTH, count):
+        scatter.drop(order[m], m)
+    for p in given[-2:]:
+        out_local(p).wait()
+        out_sib(p).wait_send()
+    for p in given:
+        from_sib(p).wait_recv()
     tokens_copy.wait()
 
 
@@ -1119,16 +1167,13 @@
         pltpu.VMEM((2, rows, width), bf16),
         pltpu.VMEM((2, rows, width), bf16),
         pltpu.VMEM((rows, width), bf16),
-        pltpu.VMEM((rows, width), bf16),
         pltpu.VMEM((rows, width), f32),
         pltpu.VMEM((rows, width), f32),
         pltpu.VMEM((4 * rows, 3 * channels), bf16),
-        pltpu.VMEM((4 * rows, channels), bf16),
-        pltpu.VMEM((2, depth, chunk, piece), bf16),
-        pltpu.VMEM((2, depth + 1, chunk, piece), bf16),
+        pltpu.VMEM((YDEPTH, depth, chunk, piece), bf16),
+        pltpu.VMEM((ZDEPTH, depth + 1, chunk, piece), bf16),
         pltpu.VMEM((depth + 1, 2 * chunk, piece), bf16),
         pltpu.VMEM((chunk, piece), bf16),
-        pltpu.VMEM((2 * chunk, piece), f32),
         pltpu.VMEM((2, chunk, piece), f32),
         pltpu.VMEM((cube + 1, 8, width), f32),
         pltpu.VMEM((cube, 8, width), f32),
@@ -1139,8 +1184,8 @@
         dma((7,)),
         dma((pieces,)),
         dma((2,)),
-        dma((2, 2, depth)),
-        dma((3, 2, depth + 1)),
+        dma((2, YDEPTH, depth)),
+        dma((3, ZDEPTH, depth + 1)),
         dma((3, depth + 1)),
         dma((2,)),
         dma((3, pieces)),
@@ -1153,7 +1198,7 @@
         out_specs=[ANY, ANY, VMEM],
         scratch_shapes=scratch,
         compiler_params=pltpu.CompilerParams(
-            collective_id=1, has_side_effects=True, vmem_limit_bytes=63 << 20
+            collective_id=1, has_side_effects=True, vmem_limit_bytes=127 << 19
         ),
     )(held, normed, normed_two, grad_rows, streams, gates, first, grad, small, loss, tokens)
 

time: 745 us -> 617 us (0.83)
  Pallas kernels: 695 us -> 566 us
    pallas_call x1, Pallas kernels: 368 us -> 279 us  [backward(): pl.pallas_call(functools.partial(backward_kernel, ndp), out_shape=outs, i...]
    pallas_call x1, Pallas kernels: 327 us -> 287 us  [forward(): pl.pallas_call(functools.partial(forward_kernel, ndp, early_y), out_shape...]
where the time goes in v2:
time: 617 us; the launch traced here: 612 us
  Pallas kernels  566 us (92%)
  local copies, waits for them, and re-layouts  37.9 us (6%)
    pallas_call x1, Pallas kernels, forward(): pl.pallas_call(functools.partial(forward_kernel, ndp, early_y), out_shape...  287 us
    pallas_call x1, Pallas kernels, backward(): pl.pallas_call(functools.partial(backward_kernel, ndp), out_shape=outs, i...  279 us

profile of v2, /device:TPU:0, one launch (start us, length us, event | category | flops | bytes accessed | tf_op | source)
XLA Modules:
  0.0 611.6 jit_solution(11318289274840698746)
XLA Ops:
  0.7 0.7 maximum_convert_fusion
  1.4 0.0 copy-start.2
  1.4 0.3 dynamic_update_slice.3
  1.6 1.3 convert_reduce_fusion
  2.9 1.3 concatenate.19.small
  4.2 1.1 pad.12
  5.3 0.8 reshape.72
  6.2 0.8 reshape.73
  7.0 0.0 copy-start.4
  7.0 0.5 copy_bitcast_fusion
  7.5 0.5 copy-done.4
  8.0 0.1 reshape.67
  8.1 0.4 copy.59
  8.5 0.4 reshape.68
  8.9 0.0 copy-start.3
  8.9 0.0 copy-done.5
  9.0 0.9 copy-done.3
  10.0 0.8 reshape.71
  10.8 0.2 copy.57
  11.1 0.0 copy-start.6
  11.1 1.7 maximum_maximum_fusion.shards
  12.8 0.8 copy.40.valid
  13.6 286.9 %shard_map.194 = (bf16[9,1536,768]{2,1,0:T(8,128)(2,1)}, bf16[960,1536]{1,0:T(8,128)(2,1)}, bf16[960,1536]{1,0:T(8,128)(2,1)}, bf16[960,1536]{1,0:T(8,128)(2,1)}...) custom-call(bf16[2,9,96,768]{3,2,1,0:T(8,128)(2,1)} %maximum_maximum, ...), custom_call_target="tpu_custom_call" | custom-call | tf_op jit(solution)/shard_map/pallas_call | solution.py:586
  300.5 279.2 %shard_map.195 = (f32[2,9,96,768]{3,2,1,0:T(8,128)}, f32[240,1536]{1,0:T(8,128)}, f32[8,1536]{1,0:T(8,128)}) custom-call(bf16[9,1536,768]{2,1,0:T(8,128)(2,1)} %get-tuple-element.25.held_in, bf16[960,1536]{1,0:T(8,128)(2,1)} %get-tuple-element.26.normed_in, bf16[960,1536]{1,0:T(8,128)(2,1)} %get-tuple-element.27.normed_two_in, ...), custom_call_target="tpu_custom_call" | custom-call | tf_op jit(solution)/shard_map/pallas_call | solution.py:1194
  579.7 3.7 slice_bitcast_fusion
  583.4 0.8 copy.44
  584.2 1.6 reshape.78
  585.8 2.6 slice.58
  588.4 0.8 copy.45
  589.2 1.6 reshape.79
  590.7 2.5 slice.59
  593.2 0.8 copy.46
  594.0 0.5 reshape.80
  594.5 1.2 slice.60
  595.6 1.3 slice_bitcast_fusion.3
  597.0 0.1 copy.49
  597.1 0.1 slice.56
  597.2 0.4 reshape.75
  597.6 0.7 copy.42
  598.3 1.6 reshape.76
  599.9 0.7 copy.50
  600.6 0.8 constant_dynamic-slice_fusion
  601.4 0.6 slice.47
  602.0 0.5 slice_bitcast_fusion.5
  602.5 1.2 slice.42
  603.7 1.2 slice.43
  606.2 2.7 copy.64
  608.9 1.1 copy.65
  (15 shorter events, 0.2 us)
Async XLA Ops:
  1.4 4.8 copy-start.2
  7.0 1.0 copy-start.4
  8.0 0.9 copy-start.5
  8.9 1.1 copy-start.3
  11.1 1.7 copy-start.6
  585.8 2.6 copy-start
  606.2 2.7 copy-start.1

commit v3 on v2

--- a/solution.py
+++ b/solution.py
@@ -206,6 +206,17 @@
         self.at, self.held, self.chunk, self.early_y = at, held, chunk, early_y
         self.recv, self.own_send, self.send = sems
 
+    def by_kind(self, p, act):
+        kind = self.early_y.get(p)
+        if kind != "half":
+            act(kind == "both")
+            return
+        for core in (0, 1):
+
+            @pl.when(self.at.core == core)
+            def _():
+                act(core == 1)
+
     def block(self, p, chip, count=1):
         return self.held.at[p, rows_of(chip * self.chunk, count * self.chunk), :]
 
@@ -219,8 +230,7 @@
     def own(self, p, act):
         at = self.at
         act(self.copy(p, at.chip, 1, self.own_send.at[0, p], at.beside))
-        if p not in self.early_y:
-            self.own_z(p, at.chip, 1, act)
+        self.by_kind(p, lambda pairs: None if pairs else self.own_z(p, at.chip, 1, act))
 
     def own_z(self, p, chip, count, act):
         at = self.at
@@ -260,21 +270,33 @@
 
         lax.fori_loop(0, at.depth - 1, step, 0)
 
-    def relay(self, p, parity, drop):
-        if drop is not None:
-            self.passing(drop[0], drop[1], parity, False, lambda copy: copy.wait_send())
-        pairs = isinstance(p, int) and p in self.early_y
-        if pairs:
-            self.arrived(p, 2 * self.at.z + 1 - self.at.y)
-            self.own_z(p, 2 * self.at.z, 2, lambda copy: copy.start())
-        self.passing(p, pairs, parity, True, lambda copy: copy.start())
+    def sent(self, p):
+        self.by_kind(p, lambda pairs: self.passing(p, pairs, p % AHEAD, False, lambda copy: copy.wait_send()))
+
+    def relay(self, p):
+        go = lambda copy: copy.start()
+        if p >= AHEAD:
+            self.sent(p - AHEAD)
+
+        def hand_on(pairs):
+            if pairs:
+                self.arrived(p, 2 * self.at.z + 1 - self.at.y)
+                self.own_z(p, 2 * self.at.z, 2, go)
+            self.passing(p, pairs, p % AHEAD, True, go)
+
+        self.by_kind(p, hand_on)
 
     def whole(self, p):
         def step(z, carry):
             self.arrived(p, 2 * z + 1 - self.at.y)
             return carry
 
-        lax.fori_loop(0, self.at.depth, step, 0)
+        self.by_kind(p, lambda pairs: None if pairs else lax.fori_loop(0, self.at.depth, step, 0))
+
+    def own_done(self, p):
+        done = lambda copy: copy.wait_send()
+        self.own(p, done)
+        self.by_kind(p, lambda pairs: self.own_z(p, 2 * self.at.z, 2, done) if pairs else None)
 
 
 def forward_kernel(
@@ -386,7 +408,7 @@
     for j in range(NSUB):
         share_a.forward(j)
     gain_one, gain_two = cur[last, 0:1, :], cur[last, 1:2, :]
-    relay = lambda p: gather.relay(p, p % AHEAD, (p - AHEAD, p - AHEAD in early_y) if p >= AHEAD else None)
+    relay = gather.relay
     relay(0)
     share_a.finish()
 
@@ -465,11 +487,10 @@
                 relay(q)
 
         for q in range(2, pieces):
-            if q not in early_y:
-
-                @pl.when(p == q)
-                def _():
-                    gather.whole(q)
+
+            @pl.when(p == q)
+            def _():
+                gather.whole(q)
 
         save(p).start()
 
@@ -521,11 +542,9 @@
     for p in range(pieces):
         save(p).wait()
         to_sib(p).wait_send()
-        gather.own(p, lambda copy: copy.wait_send())
-        if p in early_y:
-            gather.own_z(p, 2 * at.z, 2, lambda copy: copy.wait_send())
+        gather.own_done(p)
     for p in range(pieces - AHEAD, pieces):
-        gather.passing(p, p in early_y, p % AHEAD, False, lambda copy: copy.wait_send())
+        gather.sent(p)
     for p in (pieces - 2, pieces - 1):
         gates_copy(p).wait()
     for copy in (streams_copy, first_copy, normed_two_copy, result_copy, grad_copy, rows_copy):
@@ -537,7 +556,7 @@
     rows, width = tokens.shape
     channels = (2 * piece - piece // 2) // 3
     cube = small_steps(ndp)
-    early_y = (3,)
+    early_y = {3: "both", 6: "half"}
     dma = pltpu.SemaphoreType.DMA
     landing = (pieces, part_rows, piece) if part_rows % 16 else (1, 16, 128)
     shape = jax.ShapeDtypeStruct
@@ -661,7 +680,12 @@
         )
 
     def turn(self, s):
-        return (s % 2) * (s // 2) + (1 - s % 2) * (self.at.depth - 1 - s // 2)
+        z, last = self.at.z, self.at.depth - 1
+        low = jnp.where(z < self.at.depth // 2, 1, 0)
+        down, up = last - s, s
+        other = low * (down - jnp.where(down <= z, 1, 0)) + (1 - low) * (up + jnp.where(up >= z, 1, 0))
+        mine = jnp.where(s == last, 1, 0)
+        return mine * z + (1 - mine) * other
 
     def free_beside(self, p, m, before):
         if m >= self.ydepth:
@@ -715,7 +739,7 @@
         low = self.at.z < self.at.depth // 2
         return jnp.logical_and(self.behind(up), jnp.logical_not(low) if up else low)
 
-    def add_beside(self, p, m, before):
+    def add_beside(self, p, m, before, onward):
         at = self.at
         if m >= self.zdepth:
             for has, credit in ((at.has_upper, 1), (at.has_lower, 2)):
@@ -737,21 +761,27 @@
                 def _():
                     self.line_copy(p, m, z, up).start()
 
+                if onward:
+
+                    @pl.when(jnp.logical_and(z > at.z if up else z < at.z, self.behind(up)))
+                    def _():
+                        self.pass_on(p, m, z, up)
+
             return carry
 
         lax.fori_loop(0, at.depth, step, 0)
         if m + self.ydepth < self.count:
             pl.semaphore_signal(self.credits.at[0], 1, device_id=at.beside, device_id_type=MESH)
 
+    def pass_on(self, p, m, z, up):
+        self.line_copy(p, m, z, up).wait_recv()
+        own = self.block(p, 2 * z + self.at.y)
+        came = self.line_in[m % self.zdepth, z + 1 if up else z].astype(f32)
+        own[...] = (own[...].astype(f32) + came).astype(bf16)
+        self.line_copy(p, m, z, up).start()
+
     def hop(self, p, m, has):
-        def act(z, up):
-            self.line_copy(p, m, z, up).wait_recv()
-            own = self.block(p, 2 * z + self.at.y)
-            came = self.line_in[m % self.zdepth, z + 1 if up else z].astype(f32)
-            own[...] = (own[...].astype(f32) + came).astype(bf16)
-            self.line_copy(p, m, z, up).start()
-
-        self.ways(has, act)
+        self.ways(has, functools.partial(self.pass_on, p, m))
 
     def collect(self, p, m, slot):
         at = self.at
@@ -830,7 +860,11 @@
     small,
     loss,
     tokens,
-    grads_out,
+    streams_grad,
+    out_grad,
+    gate_grad,
+    up_grad,
+    down_grad,
     tokens_grad,
     small_out,
     held,
@@ -944,44 +978,88 @@
         lax.fori_loop(0, 2, some, 0)
 
         blocks = 2 * width // piece
-        each = at.depth // blocks
+        matched = blocks == at.depth
 
         def weights(s, carry):
-            i = (s % 2) * (s // 2) + (1 - s % 2) * (blocks - 1 - s // 2)
-            part = rows_of(i * piece // 2, piece // 2, 128)
+            i = scatter.turn(s) if matched else s
+            part = rows_of(i * (piece // 2), piece // 2, 128)
             held[p, part, 0 : 2 * LANES] = tn(rows_b[:, part], back[:, 0 : 2 * LANES]).astype(bf16)
             held[p, part, 2 * LANES :] = tn(rows_a[:, part], back[:, 2 * LANES : 3 * LANES]).astype(bf16)
-            if m is not None:
-                for e in range(each):
-                    scatter.beside_copy(p, m, i * each + e).start()
+            if m is not None and matched:
+                scatter.beside_copy(p, m, i).start()
             return carry
 
         lax.fori_loop(0, blocks, weights, 0)
+        if m is not None and not matched:
+            scatter.send_beside(p, m, None)
         if p + 2 < pieces:
             load_gates(p + 2).start()
 
     given = []
 
-    def out_local(p):
-        src = total.at[given.index(p) % 2, rows_of(at.core * half, half, 8), :]
-        return pltpu.make_async_copy(src, grads_out.at[at.core, p], done_sems.at[0, p])
-
-    def out_sib(p):
-        src = total.at[given.index(p) % 2, rows_of((1 - at.core) * half, half, 8), :]
-        return remote(src, grads_out.at[at.core, p], done_sems.at[1, p], done_sems.at[2, p], at.sib)
-
-    def from_sib(p):
-        src = total.at[0, rows_of((1 - at.core) * half, half, 8), :]
-        return remote(src, grads_out.at[1 - at.core, p], done_sems.at[1, p], done_sems.at[2, p], at.sib)
+    span = (pieces - 2) * LANES
+    short = gate_grad.shape[1] - 2 * span + LANES
+
+    def parts(p, core):
+        if p == 0:
+            at_columns = rows_of(core * channels, channels, 128)
+            return [(k * channels, channels, streams_grad.at[k, :, at_columns]) for k in range(2)]
+        if p == 1:
+            at_columns = rows_of(core * channels, channels, 128)
+            return [
+                (0, channels, streams_grad.at[2, :, at_columns]),
+                (channels, channels, out_grad.at[:, at_columns]),
+            ]
+        found = []
+        for k, out in enumerate((gate_grad, up_grad, down_grad)):
+            found.append((k * LANES, LANES, out.at[:, rows_of(core * span + (p - 2) * LANES, LANES, 128)]))
+        return found
+
+    def narrow(p, core):
+        found = []
+        for k, out in enumerate((gate_grad, up_grad, down_grad)):
+            found.append((k * LANES, short, out.at[:, rows_of(core * span + (p - 2) * LANES, short, 128)]))
+        return found
+
+    def each_part(p, core, act):
+        if p < pieces - 1 or short == LANES:
+            for k, (first_column, count, dst) in enumerate(parts(p, core)):
+                act(k, first_column, count, dst)
+            return
+
+        for is_short, found in ((False, parts), (True, narrow)):
+
+            @pl.when((core == 1) if is_short else (core == 0))
+            def _():
+                for k, (first_column, count, dst) in enumerate(found(p, 0 if not is_short else 1)):
+                    act(k, first_column, count, dst)
+
+    def piece_rows(p, core, first_column, count):
+        slot = given.index(p) % 2 if p in given else 0
+        return total.at[slot, rows_of(core * half, half, 8), pl.ds(first_column, count)]
+
+    def out_local(p, act):
+        def copy(k, first_column, count, dst):
+            src = piece_rows(p, at.core, first_column, count)
+            act(pltpu.make_async_copy(src, dst, done_sems.at[0, p, k]))
+
+        each_part(p, at.core, copy)
+
+    def out_sib(p, core, act):
+        def copy(k, first_column, count, dst):
+            src = piece_rows(p, 1 - at.core, first_column, count)
+            act(remote(src, dst, done_sems.at[1, p, k], done_sems.at[2, p, k], at.sib))
+
+        each_part(p, core, copy)
 
     def give(p, fill):
         if len(given) > 1:
-            out_local(given[-2]).wait()
-            out_sib(given[-2]).wait_send()
+            out_local(given[-2], lambda copy: copy.wait())
+            out_sib(given[-2], at.core, lambda copy: copy.wait_send())
         given.append(p)
         fill((len(given) - 1) % 2)
-        out_local(p).start()
-        out_sib(p).start()
+        out_local(p, lambda copy: copy.start())
+        out_sib(p, at.core, lambda copy: copy.start())
 
     def beside(m):
         scatter.send_beside(order[m], m, order[m - YDEPTH] if m >= YDEPTH else None)
@@ -990,7 +1068,13 @@
         give(order[m], functools.partial(scatter.collect, order[m], m))
 
     def advance(m):
-        scatter.add_beside(order[m], m, order[m - ZDEPTH] if m >= ZDEPTH else None)
+        onward = m == len(order) - 1
+        if onward:
+            scatter.hop(order[m - 1], m - 1, scatter.far)
+            finish(m - 2)
+        scatter.add_beside(order[m], m, order[m - ZDEPTH] if m >= ZDEPTH else None, onward)
+        if onward:
+            return
         scatter.hop(order[m], m, scatter.near)
         if m == 0:
             scatter.pair_hop(paired, scatter.near)
@@ -1123,7 +1207,6 @@
             total_end(at, step, cur, got, tally(step))
             if step + 1 < steps:
                 tally(step + 1).start()
-    scatter.hop(order[count - 1], count - 1, scatter.far)
     finish(count - 2)
     finish(count - 1)
     for step in range(count - 3, steps):
@@ -1136,14 +1219,14 @@
     for m in range(count - ZDEPTH, count):
         scatter.drop(order[m], m)
     for p in given[-2:]:
-        out_local(p).wait()
-        out_sib(p).wait_send()
+        out_local(p, lambda copy: copy.wait())
+        out_sib(p, at.core, lambda copy: copy.wait_send())
     for p in given:
-        from_sib(p).wait_recv()
+        out_sib(p, 1 - at.core, lambda copy: copy.wait_recv())
     tokens_copy.wait()
 
 
-def backward(ndp, held, normed, normed_two, grad_rows, streams, gates, first, grad, small, loss, tokens):
+def backward(ndp, units, held, normed, normed_two, grad_rows, streams, gates, first, grad, small, loss, tokens):
     pieces, width, piece = held.shape
     rows = tokens.shape[0]
     chunk = 2 * width // ndp
@@ -1153,7 +1236,11 @@
     dma = pltpu.SemaphoreType.DMA
     shape = jax.ShapeDtypeStruct
     outs = (
-        shape((2, pieces, chunk // 2, piece), f32),
+        shape((3, chunk // 2, 2 * channels), f32),
+        shape((chunk // 2, 2 * channels), f32),
+        shape((chunk // 2, units), f32),
+        shape((chunk // 2, units), f32),
+        shape((chunk // 2, units), f32),
         shape((rows, width), f32),
         shape((8, width), f32),
     )
@@ -1188,14 +1275,14 @@
         dma((3, ZDEPTH, depth + 1)),
         dma((3, depth + 1)),
         dma((2,)),
-        dma((3, pieces)),
+        dma((3, pieces, 3)),
         pltpu.SemaphoreType.REGULAR((3,)),
     ]
     return pl.pallas_call(
         functools.partial(backward_kernel, ndp),
         out_shape=outs,
         in_specs=[ANY] * 8 + [VMEM] * 3,
-        out_specs=[ANY, ANY, VMEM],
+        out_specs=[ANY] * 6 + [VMEM],
         scratch_shapes=scratch,
         compiler_params=pltpu.CompilerParams(
             collective_id=1, has_side_effects=True, vmem_limit_bytes=127 << 19
@@ -1229,34 +1316,34 @@
     held, normed, normed_two, grad_rows, streams, gates, first, block_out, grad, small, loss = forward(
         ndp, shards, tokens, teacher, valid_f[:, None], small
     )
-    grads, tokens_grad, small_grads = backward(
-        ndp, held, normed, normed_two, grad_rows, streams, gates, first, grad, small, loss, tokens
+    streams_grad, out_grad, gate_grad, up_grad, down_grad, tokens_grad, small_grads = backward(
+        ndp,
+        gate_weight.shape[1],
+        held,
+        normed,
+        normed_two,
+        grad_rows,
+        streams,
+        gates,
+        first,
+        grad,
+        small,
+        loss,
+        tokens,
     )
-    part_rows, _, channels = in_weight.shape
-    channels //= 2
-    units = gate_weight.shape[1]
-    mixer = grads[:, 0:2].transpose(0, 2, 1, 3).reshape(2, part_rows, 4 * channels)
-    in_grad = mixer[:, :, 0 : 3 * channels].reshape(2, part_rows, 3, channels)
-    in_grad = in_grad.transpose(1, 2, 0, 3).reshape(part_rows, 3, 2 * channels)
-    out_grad = mixer[:, :, 3 * channels :].transpose(1, 0, 2).reshape(part_rows, 2 * channels)
-
-    def joined(k):
-        cut = grads[:, 2:, :, k * LANES : (k + 1) * LANES]
-        return cut.transpose(2, 0, 1, 3).reshape(part_rows, -1)[:, 0:units]
-
     own = lax.dynamic_slice(small_grads, (0, place_of * share), (5, share))
     return (
         small_grads[5, 0] / (width * small[5, 0]),
         block_out,
         tokens_grad,
         own[0],
-        in_grad,
+        streams_grad.transpose(1, 0, 2),
         own[2:5],
         out_grad,
         own[1],
-        joined(0),
-        joined(1),
-        joined(2),
+        gate_grad,
+        up_grad,
+        down_grad,
     )
 
 

time: 617 us -> 587 us (0.951)
  local copies, waits for them, and re-layouts: 37.9 us -> 21.7 us
  Pallas kernels: 566 us -> 554 us
    pallas_call x1, Pallas kernels: 287 us -> 275 us  [forward(): pl.pallas_call(functools.partial(forward_kernel, ndp, early_y), out_shape...]
    transpose x5 -> x0, local copies, waits for them, and re-layouts: 6.79 us -> none  [the longest x4 6.1 us: joined(): return cut.transpose(2, 0, 1, 3).reshape(part_rows, -1)[:, 0:units]]
    reshape x7 -> x0, local copies, waits for them, and re-layouts: 6.42 us -> none  [the longest x3 3.57 us: joined(): return cut.transpose(2, 0, 1, 3).reshape(part_rows, -1)[:, 0:units]]
    slice x4 -> x0, local copies, waits for them, and re-layouts: 6.26 us -> none  [the longest x3 6.19 us: joined(): return cut.transpose(2, 0, 1, 3).reshape(part_rows, -1)[:, 0:units]]
where the time goes in v3:
time: 587 us; the launch traced here: 583 us
  Pallas kernels  554 us (94%)
  local copies, waits for them, and re-layouts  21.7 us (4%)
    pallas_call x1, Pallas kernels, backward(): pl.pallas_call(functools.partial(backward_kernel, ndp), out_shape=outs, i...  278 us
    pallas_call x1, Pallas kernels, forward(): pl.pallas_call(functools.partial(forward_kernel, ndp, early_y), out_shape...  275 us

profile of v3, /device:TPU:0, one launch (start us, length us, event | category | flops | bytes accessed | tf_op | source)
XLA Modules:
  0.0 582.6 jit_solution(6999312825408546102)
XLA Ops:
  0.6 0.0 copy-start.5
  0.7 0.8 maximum_convert_fusion
  1.4 0.3 dynamic_update_slice.3
  1.7 1.3 convert_reduce_fusion
  3.0 1.3 concatenate.19.small
  4.3 1.1 pad.12
  5.4 0.8 reshape.51
  6.2 0.0 copy-done.5
  6.2 0.0 copy-start.6
  6.3 0.8 reshape.52
  7.1 0.0 copy-start.8
  7.1 0.5 copy_bitcast_fusion
  7.6 0.0 copy-done.6
  7.6 0.1 reshape.46
  7.7 0.4 copy.46
  8.1 0.4 reshape.47
  8.5 0.0 copy-done.8
  8.6 1.1 pad.11
  9.8 0.8 reshape.50
  10.6 0.2 copy.44
  10.8 0.0 copy-start.9
  10.8 1.7 maximum_maximum_fusion.shards
  12.5 0.0 copy-done.9
  12.5 0.8 copy.35.valid
  13.3 275.5 %shard_map.194 = (bf16[9,1536,768]{2,1,0:T(8,128)(2,1)}, bf16[960,1536]{1,0:T(8,128)(2,1)}, bf16[960,1536]{1,0:T(8,128)(2,1)}, bf16[960,1536]{1,0:T(8,128)(2,1)}...) custom-call(bf16[2,9,96,768]{3,2,1,0:T(8,128)(2,1)} %maximum_maximum, ...), custom_call_target="tpu_custom_call" | custom-call | tf_op jit(solution)/shard_map/pallas_call | solution.py:605
  288.8 278.2 %shard_map.195 = (f32[3,96,768]{2,1,0:T(8,128)}, f32[96,768]{1,0:T(8,128)}, f32[96,3456]{1,0:T(8,128)}, f32[96,3456]{1,0:T(8,128)}, f32[96,3456]{1,0:T(8,128)}, /*index=5*/f32[240,1536]{1,0:T(8,128)}, f32[8,1536]{1,0:T(8,128)}) custom-call(bf16[9,1536,768]{2,1,0:T(8,128)(2,1)} %get-tuple-element.29.held_in, bf16[960,1536]{1,0:T(8,128)(2,1)} %get-tuple-element.30.normed_in, ...), custom_call_target="tpu_custom_call" | custom-call | tf_op jit(solution)/shard_map/pallas_call | solution.py:1281
  567.0 0.0 copy-start
  567.0 0.9 constant_dynamic-slice_fusion
  567.9 0.6 slice.18
  568.4 0.5 slice_bitcast_fusion
  569.0 1.2 slice.15
  570.1 1.2 slice.16
  572.6 0.0 copy-start.4
  572.6 2.7 copy.56
  575.3 0.0 copy-done
  575.3 0.0 copy-start.7
  575.3 0.0 copy-start.3
  575.3 1.1 copy.57
  576.4 0.0 copy-done.4
  576.4 0.9 copy.58
  577.3 0.0 copy-done.7
  577.3 0.7 copy.59
  578.1 0.0 copy-done.3
  578.1 1.1 copy.60
  579.1 0.0 copy-done.2
  579.1 1.1 copy.61
  580.2 0.0 copy-done.1
  580.2 1.1 copy.62
  (8 shorter events, 0.2 us)
Async XLA Ops:
  0.6 5.6 copy-start.5
  6.2 1.4 copy-start.6
  7.1 1.4 copy-start.8
  10.8 1.7 copy-start.9
  567.0 8.3 %copy-start = (f32[240,1536]{1,0:T(8,128)S(1)}, f32[240,1536]{1,0:T(8,128)}, u32[]{:S(2)}) copy-start(f32[240,1536]{1,0:T(8,128)} %get-tuple-element.64) | copy-start | bytes 4423684
  572.6 3.8 copy-start.4
  575.3 2.0 copy-start.7
  575.3 2.7 copy-start.3
  576.4 2.7 copy-start.2
  578.1 2.1 copy-start.1

commit v4 on v3

--- a/solution.py
+++ b/solution.py
@@ -302,11 +302,17 @@
 def forward_kernel(
     ndp,
     early_y,
-    shards,
+    in_weight,
+    out_weight,
+    gate_weight,
+    up_weight,
+    down_weight,
     tokens,
     teacher,
     valid,
-    small,
+    mixer_gain,
+    ffn_gain,
+    conv_weight,
     held_out,
     normed_out,
     normed_two_out,
@@ -348,7 +354,7 @@
 ):
     at = place(ndp)
     pieces, width, piece = held.shape
-    part_rows = shards.shape[2]
+    part_rows = out_weight.shape[0]
     chunk = 2 * part_rows
     rows = tokens.shape[0]
     sub = rows // NSUB
@@ -360,36 +366,86 @@
     share_b = Share(at, rows_b, rows, share_sems)
     sums = Sums(at, acc, rows, core_out, core_in, far_in, core_sems, far_sems)
 
-    def half(p, core):
-        return held.at[p, rows_of(at.chip * chunk + core * part_rows, part_rows), :]
-
-    def to_sib(p):
-        dst = half(p, at.core) if aligned else landed.at[p]
-        return remote(shards.at[1 - at.core, p], dst, chip_sems.at[0, p], chip_sems.at[1, p], at.sib)
+    span = (pieces - 2) * LANES
+    short = gate_weight.shape[1] - 2 * span + LANES
+
+    def parts(p, core, count=LANES):
+        at_columns = rows_of(core * channels, channels, 128)
+        if p == 0:
+            return [(in_weight.at[k, :, at_columns], k * channels, channels) for k in range(2)]
+        if p == 1:
+            return [(in_weight.at[2, :, at_columns], 0, channels), (out_weight.at[:, at_columns], channels, channels)]
+        at_columns = rows_of(core * span + (p - 2) * LANES, count, 128)
+        return [(w.at[:, at_columns], k * LANES, count) for k, w in enumerate((gate_weight, up_weight, down_weight))]
+
+    def each_part(p, core, act):
+        if p < pieces - 1 or short == LANES:
+            for k, (src, column, count) in enumerate(parts(p, core)):
+                act(k, src, column, count)
+            return
+        for to, count in ((0, LANES), (1, short)):
+
+            @pl.when(core == to)
+            def _():
+                for k, (src, column, size) in enumerate(parts(p, to, count)):
+                    act(k, src, column, size)
+
+    def landing(p, core, column, count, buffer):
+        if not aligned:
+            return buffer.at[p, :, pl.ds(column, count)]
+        rows_there = rows_of(at.chip * chunk + core * part_rows, part_rows)
+        return held.at[p, rows_there, pl.ds(column, count)]
+
+    def to_sib(p, act):
+        def copy(k, src, column, count):
+            dst = landing(p, at.core, column, count, landed)
+            act(remote(src, dst, chip_sems.at[0, p, k], chip_sems.at[1, p, k], at.sib))
+
+        each_part(p, 1 - at.core, copy)
 
     def from_sib(p):
-        dst = half(p, 1 - at.core) if aligned else landed.at[p]
-        return remote(dst, dst, chip_sems.at[0, p], chip_sems.at[1, p], at.sib)
-
-    def keep(p):
-        dst = half(p, at.core) if aligned else mine.at[p]
-        return pltpu.make_async_copy(shards.at[at.core, p], dst, chip_sems.at[2, p])
+        def copy(k, src, column, count):
+            dst = landing(p, 1 - at.core, column, count, landed)
+            remote(src, dst, chip_sems.at[0, p, k], chip_sems.at[1, p, k], at.sib).wait_recv()
+
+        each_part(p, at.core, copy)
+
+    def keep(p, act):
+        def copy(k, src, column, count):
+            dst = landing(p, at.core, column, count, mine)
+            act(pltpu.make_async_copy(src, dst, chip_sems.at[2, p, k]))
+
+        each_part(p, at.core, copy)
 
     def own_block(p):
-        keep(p).wait()
-        from_sib(p).wait_recv()
+        keep(p, lambda copy: copy.wait())
+        from_sib(p)
+        here = rows_of(at.chip * chunk, chunk)
         if not aligned:
             a, b = mine[p].astype(f32), landed[p].astype(f32)
             lower = jnp.where(at.core == 0, a, b)
             upper = jnp.where(at.core == 0, b, a)
-            both = jnp.concatenate([lower, upper], axis=0).astype(bf16)
-            held[p, rows_of(at.chip * chunk, chunk), :] = both
+            held[p, here, :] = jnp.concatenate([lower, upper], axis=0).astype(bf16)
+        if p == pieces - 1 and short < LANES:
+
+            @pl.when(at.core == 1)
+            def _():
+                for k in range(3):
+                    held[p, here, k * LANES + short : (k + 1) * LANES] = jnp.zeros((chunk, LANES - short), bf16)
+
         gather.own(p, go)
 
     meet(at)
-    to_sib(0).start()
-    keep(0).start()
-    cur[0] = small[...]
+    to_sib(0, go)
+    keep(0, go)
+    share = mixer_gain.shape[1]
+    cur[0] = jnp.zeros(cur.shape[1:], f32)
+    cur[0, 0:1, 0:share] = mixer_gain[...].astype(f32)
+    cur[0, 1:2, 0:share] = ffn_gain[...].astype(f32)
+    cur[0, 2:5, 0:share] = conv_weight[...].astype(f32)
+    placed = pltpu.roll(cur[0], (at.d * 2 + at.x) * share, 1)
+    line = lax.broadcasted_iota(jnp.int32, placed.shape, 0)
+    cur[0] = jnp.where(line < 5, placed, jnp.sum(valid[...]))
     total_step(at, 0, cur, got, cube_sems.at[0], cube_sems.at[1])
     own_block(0)
     total_step(at, 1, cur, got, cube_sems.at[0], cube_sems.at[1])
@@ -397,8 +453,8 @@
         rows_a[rows_of(at.own * rows + j * sub, sub), :] = tokens[pl.ds(j * sub, sub), :]
         share_a.start(j)
     for p in range(1, pieces):
-        to_sib(p).start()
-        keep(p).start()
+        to_sib(p, go)
+        keep(p, go)
     for step in range(2, len(at.cube)):
         total_step(at, step, cur, got, cube_sems.at[0], cube_sems.at[1])
         if step < 4:
@@ -541,7 +597,7 @@
     rows_copy.start()
     for p in range(pieces):
         save(p).wait()
-        to_sib(p).wait_send()
+        to_sib(p, lambda copy: copy.wait_send())
         gather.own_done(p)
     for p in range(pieces - AHEAD, pieces):
         gather.sent(p)
@@ -551,10 +607,12 @@
         copy.wait()
 
 
-def forward(ndp, shards, tokens, teacher, valid, small):
-    _, pieces, part_rows, piece = shards.shape
+def forward(ndp, weights, tokens, teacher, valid, vectors):
+    part_rows, channels = weights[1].shape
+    channels //= 2
+    piece = 2 * channels
+    pieces = 2 - (-weights[2].shape[1] // (2 * LANES))
     rows, width = tokens.shape
-    channels = (2 * piece - piece // 2) // 3
     cube = small_steps(ndp)
     early_y = {3: "both", 6: "half"}
     dma = pltpu.SemaphoreType.DMA
@@ -590,7 +648,7 @@
         pltpu.VMEM((rows, width), f32),
         pltpu.VMEM((cube + 1, 8, width), f32),
         pltpu.VMEM((cube, 8, width), f32),
-        dma((3, pieces)),
+        dma((3, pieces, 3)),
         dma((pieces, ndp // 2)),
         dma((3, pieces)),
         dma((3, AHEAD, ndp // 4)),
@@ -605,36 +663,17 @@
     return pl.pallas_call(
         functools.partial(forward_kernel, ndp, early_y),
         out_shape=outs,
-        in_specs=[ANY, VMEM, VMEM, VMEM, VMEM],
+        in_specs=[ANY] * 5 + [VMEM] * 6,
         out_specs=[ANY] * 9 + [VMEM] * 2,
         scratch_shapes=scratch,
         compiler_params=pltpu.CompilerParams(
             collective_id=0, has_side_effects=True, vmem_limit_bytes=63 << 20
         ),
-    )(shards, tokens, teacher, valid, small)
+    )(*weights, tokens, teacher, valid, *vectors)
 
 
 def small_steps(ndp):
     return 3 + (ndp // 4 - 1).bit_length()
-
-
-def shard_pieces(in_weight, out_weight, gate_weight, up_weight, down_weight):
-    part_rows, _, channels = in_weight.shape
-    channels //= 2
-    taps = in_weight.reshape(part_rows, 3, 2, channels).transpose(2, 0, 1, 3)
-    taps = taps.reshape(2, part_rows, 3 * channels)
-    outs = out_weight.reshape(part_rows, 2, channels).transpose(1, 0, 2)
-    mixer = jnp.concatenate([taps, outs], axis=2)
-    mixer = mixer.reshape(2, part_rows, 2, 2 * channels).transpose(0, 2, 1, 3)
-    units = gate_weight.shape[1]
-    count = -(-units // (2 * LANES))
-
-    def cut(weight):
-        weight = jnp.pad(weight, ((0, 0), (0, 2 * count * LANES - units)))
-        return weight.reshape(part_rows, 2, count, LANES).transpose(1, 2, 0, 3)
-
-    ffn = jnp.concatenate([cut(gate_weight), cut(up_weight), cut(down_weight)], axis=3)
-    return jnp.concatenate([mixer, ffn], axis=1)
 
 
 class Scatter:
@@ -866,7 +905,10 @@
     up_grad,
     down_grad,
     tokens_grad,
-    small_out,
+    mixer_gain_grad,
+    ffn_gain_grad,
+    conv_grad,
+    loss_out,
     held,
     rows_a,
     rows_b,
@@ -1178,7 +1220,6 @@
     beside(6)
     sums.to_far()
     advance(4)
-    beside(7)
     gain_one_grad = jnp.zeros((1, width), f32)
     for j in range(NSUB):
         part = rows_of(j * sub, sub)
@@ -1194,26 +1235,31 @@
     tokens_copy.start()
     cur[0, 0:1, :] = gain_one_grad
     tally = lambda step: total_copy(at, step, cur, got, cube_sems.at[0], cube_sems.at[1])
-    for step in range(3):
+    for step in range(2):
         tally(step).start()
-        if step < 2:
-            total_end(at, step, cur, got, tally(step))
+        total_end(at, step, cur, got, tally(step))
+    tally(2).start()
+    beside(7)
     steps = len(at.cube)
     count = len(order)
-    for m in range(5, count):
-        advance(m)
-        step = m - 3
-        if step < steps:
-            total_end(at, step, cur, got, tally(step))
-            if step + 1 < steps:
-                tally(step + 1).start()
-    finish(count - 2)
-    finish(count - 1)
-    for step in range(count - 3, steps):
+    advance(5)
+    advance(6)
+    total_end(at, 2, cur, got, tally(2))
+    tally(3).start()
+    advance(7)
+    for step in range(3, steps):
         total_end(at, step, cur, got, tally(step))
         if step + 1 < steps:
             tally(step + 1).start()
-    small_out[...] = cur[steps]
+        if step == 3:
+            finish(count - 2)
+    finish(count - 1)
+    share_lanes = mixer_gain_grad.shape[1]
+    own = pltpu.roll(cur[steps], (width - (at.d * 2 + at.x) * share_lanes) % width, 1)
+    mixer_gain_grad[...] = own[0:1, 0:share_lanes]
+    ffn_gain_grad[...] = own[1:2, 0:share_lanes]
+    conv_grad[...] = own[2:5, 0:share_lanes]
+    loss_out[...] = cur[steps, 5:6, 0:1] / (width * small[5:6, 0:1])
     for m in range(count - YDEPTH, count):
         scatter.drop_beside(order[m], m)
     for m in range(count - ZDEPTH, count):
@@ -1242,7 +1288,10 @@
         shape((chunk // 2, units), f32),
         shape((chunk // 2, units), f32),
         shape((rows, width), f32),
-        shape((8, width), f32),
+        shape((1, width // (2 * ndp)), f32),
+        shape((1, width // (2 * ndp)), f32),
+        shape((3, width // (2 * ndp)), f32),
+        shape((1, 1), f32),
     )
     scratch = [
         pltpu.VMEM((pieces, width, piece), bf16),
@@ -1282,7 +1331,7 @@
         functools.partial(backward_kernel, ndp),
         out_shape=outs,
         in_specs=[ANY] * 8 + [VMEM] * 3,
-        out_specs=[ANY] * 6 + [VMEM],
+        out_specs=[ANY] * 6 + [VMEM] * 4,
         scratch_shapes=scratch,
         compiler_params=pltpu.CompilerParams(
             collective_id=1, has_side_effects=True, vmem_limit_bytes=127 << 19
@@ -1304,19 +1353,15 @@
     down_weight,
 ):
     ndp = lax.axis_size("dp")
-    place_of = lax.axis_index("dp") * 2 + lax.axis_index("tensor")
-    width = tokens.shape[1]
-    valid_f = valid.astype(f32)
-    vectors = jnp.concatenate([mixer_gain[None], ffn_gain[None], conv_weight], axis=0).astype(f32)
-    share = vectors.shape[1]
-    small = jnp.zeros((5, width), f32)
-    small = lax.dynamic_update_slice(small, vectors, (0, place_of * share))
-    small = jnp.concatenate([small, jnp.full((3, width), jnp.sum(valid_f), f32)], axis=0)
-    shards = shard_pieces(in_weight, out_weight, gate_weight, up_weight, down_weight)
     held, normed, normed_two, grad_rows, streams, gates, first, block_out, grad, small, loss = forward(
-        ndp, shards, tokens, teacher, valid_f[:, None], small
+        ndp,
+        (in_weight.transpose(1, 0, 2), out_weight, gate_weight, up_weight, down_weight),
+        tokens,
+        teacher,
+        valid.astype(f32)[:, None],
+        (mixer_gain[None], ffn_gain[None], conv_weight),
     )
-    streams_grad, out_grad, gate_grad, up_grad, down_grad, tokens_grad, small_grads = backward(
+    streams_grad, out_grad, gate_grad, up_grad, down_grad, tokens_grad, *small_grads = backward(
         ndp,
         gate_weight.shape[1],
         held,
@@ -1331,16 +1376,16 @@
         loss,
         tokens,
     )
-    own = lax.dynamic_slice(small_grads, (0, place_of * share), (5, share))
+    mixer_gain_grad, ffn_gain_grad, conv_grad, loss = small_grads
     return (
-        small_grads[5, 0] / (width * small[5, 0]),
+        loss[0, 0],
         block_out,
         tokens_grad,
-        own[0],
+        mixer_gain_grad[0],
         streams_grad.transpose(1, 0, 2),
-        own[2:5],
+        conv_grad,
         out_grad,
-        own[1],
+        ffn_gain_grad[0],
         gate_grad,
         up_grad,
         down_grad,

time: 587 us -> 547 us (0.932)
  Pallas kernels: 554 us -> 524 us
  local copies, waits for them, and re-layouts: 21.7 us -> 11.8 us
    pallas_call x1, Pallas kernels: 278 us -> 249 us  [backward(): pl.pallas_call(functools.partial(backward_kernel, ndp), out_shape=outs, i...]
where the time goes in v4:
time: 547 us; the launch traced here: 540 us
  Pallas kernels  524 us (96%)
  local copies, waits for them, and re-layouts  11.8 us (2%)
    pallas_call x1, Pallas kernels, forward(): pl.pallas_call(functools.partial(forward_kernel, ndp, early_y), out_shape...  276 us
    pallas_call x1, Pallas kernels, backward(): pl.pallas_call(functools.partial(backward_kernel, ndp), out_shape=outs, i...  249 us
    unnamed x28, local copies, waits for them, and re-layouts  11 us

profile of v4, /device:TPU:0, one launch (start us, length us, event | category | flops | bytes accessed | tf_op | source)
XLA Modules:
  0.0 539.7 jit_solution(12966475961564337241)
XLA Ops:
  0.6 0.7 convert_element_type.3
  1.3 0.8 copy.22.valid
  2.1 275.7 %shard_map.194 = (bf16[9,1536,768]{2,1,0:T(8,128)(2,1)}, bf16[960,1536]{1,0:T(8,128)(2,1)}, bf16[960,1536]{1,0:T(8,128)(2,1)}, bf16[960,1536]{1,0:T(8,128)(2,1)}...) custom-call(bf16[3,96,768]{2,1,0:T(8,128)(2,1)} %bitcast.9, ...), custom_call_target="tpu_custom_call" | custom-call | tf_op jit(solution)/shard_map/pallas_call | solution.py:663
  277.9 248.6 %shard_map.195 = (f32[3,96,768]{2,1,0:T(8,128)}, f32[96,768]{1,0:T(8,128)}, f32[96,3456]{1,0:T(8,128)}, f32[96,3456]{1,0:T(8,128)}, f32[96,3456]{1,0:T(8,128)}, ...) custom-call(bf16[9,1536,768]{2,1,0:T(8,128)(2,1)} %get-tuple-element.32.held_i, ...), custom_call_target="tpu_custom_call" | custom-call | tf_op jit(solution)/shard_map/pallas_call | solution.py:1330
  527.1 0.0 copy-start
  527.1 2.7 copy.35
  529.8 0.0 copy-done
  529.8 0.0 copy-start.8
  529.8 0.0 copy-start.4
  529.8 1.1 copy.36
  530.9 0.0 copy-done.8
  530.9 0.0 copy-start.6
  530.9 0.0 copy-start.5
  530.9 0.0 copy-start.7
  530.9 0.0 copy-start.3
  531.0 0.5 copy.37
  531.5 0.1 copy-done.4
  531.5 0.9 copy.38
  532.4 0.0 copy-done.6
  532.4 0.6 copy.39
  533.0 0.0 copy-done.5
  533.0 0.7 copy.40
  533.7 0.0 copy-done.7
  533.7 0.0 copy-start.2
  533.7 0.5 copy.41
  534.2 0.0 copy-done.3
  534.2 1.1 copy.42
  535.3 0.0 copy-done.2
  535.3 0.0 copy-start.1
  535.3 1.1 copy.43
  536.4 0.7 copy-done.1
  537.1 1.1 copy.44
Async XLA Ops:
  527.1 2.7 copy-start
  529.8 1.1 copy-start.8
  529.8 1.7 copy-start.4
  530.9 1.5 copy-start.6
  530.9 2.1 copy-start.5
  530.9 2.8 copy-start.7
  530.9 3.3 copy-start.3
  533.7 1.6 copy-start.2
  535.3 1.8 copy-start.1

commit v5 on v4

--- a/solution.py
+++ b/solution.py
@@ -76,10 +76,31 @@
     cur[step + 1] = cur[step] + got[step]
 
 
-def total_step(at, step, cur, got, send, recv):
-    copy = total_copy(at, step, cur, got, send, recv)
+def start(copy):
     copy.start()
-    total_end(at, step, cur, got, copy)
+
+
+def wait(copy):
+    copy.wait()
+
+
+def wait_send(copy):
+    copy.wait_send()
+
+
+def wait_recv(copy):
+    copy.wait_recv()
+
+
+def by_core(at, p, short, width, act):
+    if p != short:
+        act(width)
+        return
+    for core, count in ((0, width), (1, width // 2)):
+
+        @pl.when(at.core == core)
+        def _():
+            act(count)
 
 
 class Share:
@@ -201,10 +222,23 @@
     return taps[0:1] * shifted(mixed, 2) + taps[1:2] * shifted(mixed, 1) + taps[2:3] * mixed
 
 
+def ffn_columns(p, pieces, core):
+    if p < pieces - 1:
+        return [(k * LANES, LANES, 0, k) for k in range(3)]
+    half = LANES // 2
+    return [((3 * h + k) * half, half, h * half, k) for h in range(2 - core) for k in range(3)]
+
+
+def ffn_blocks(p, pieces):
+    last = isinstance(p, int) and p == pieces - 1
+    return [(0, LANES // 2), (3 * LANES // 2, LANES // 2)] if last else [(0, LANES)]
+
+
 class Gather:
     def __init__(self, at, held, chunk, early_y, sems):
         self.at, self.held, self.chunk, self.early_y = at, held, chunk, early_y
         self.recv, self.own_send, self.send = sems
+        self.short = held.shape[0] - 1
 
     def by_kind(self, p, act):
         kind = self.early_y.get(p)
@@ -217,19 +251,19 @@
             def _():
                 act(core == 1)
 
-    def block(self, p, chip, count=1):
-        return self.held.at[p, rows_of(chip * self.chunk, count * self.chunk), :]
-
-    def copy(self, p, chip, count, send, dev):
-        block = self.block(p, chip, count)
-        return remote(block, block, send, self.recv.at[p, chip], dev)
+    def run(self, act, p, chip, count, send, dev):
+        def of(width):
+            block = self.held.at[p, rows_of(chip * self.chunk, count * self.chunk), pl.ds(0, width)]
+            act(remote(block, block, send, self.recv.at[p, chip], dev))
+
+        by_core(self.at, p, self.short, self.held.shape[2], of)
 
     def arrived(self, p, chip, count=1):
-        self.copy(p, chip, count, self.own_send.at[0, 0], self.at.beside).wait_recv()
+        self.run(wait_recv, p, chip, count, self.own_send.at[0, 0], self.at.beside)
 
     def own(self, p, act):
         at = self.at
-        act(self.copy(p, at.chip, 1, self.own_send.at[0, p], at.beside))
+        self.run(act, p, at.chip, 1, self.own_send.at[0, p], at.beside)
         self.by_kind(p, lambda pairs: None if pairs else self.own_z(p, at.chip, 1, act))
 
     def own_z(self, p, chip, count, act):
@@ -237,11 +271,11 @@
 
         @pl.when(at.has_upper)
         def _():
-            act(self.copy(p, chip, count, self.own_send.at[1, p], at.upper))
+            self.run(act, p, chip, count, self.own_send.at[1, p], at.upper)
 
         @pl.when(at.has_lower)
         def _():
-            act(self.copy(p, chip, count, self.own_send.at[2, p], at.lower))
+            self.run(act, p, chip, count, self.own_send.at[2, p], at.lower)
 
     def passing(self, p, pairs, parity, wait, act):
         at = self.at
@@ -261,28 +295,27 @@
 
                     @pl.when(goes_on)
                     def _():
-                        act(self.copy(p, chip, count, self.send.at[way, parity, from_z], dev))
+                        self.run(act, p, chip, count, self.send.at[way, parity, from_z], dev)
 
                     if not pairs:
-                        act(self.copy(p, chip, count, self.send.at[2, parity, from_z], at.beside))
+                        self.run(act, p, chip, count, self.send.at[2, parity, from_z], at.beside)
 
             return carry
 
         lax.fori_loop(0, at.depth - 1, step, 0)
 
     def sent(self, p):
-        self.by_kind(p, lambda pairs: self.passing(p, pairs, p % AHEAD, False, lambda copy: copy.wait_send()))
+        self.by_kind(p, lambda pairs: self.passing(p, pairs, p % AHEAD, False, wait_send))
 
     def relay(self, p):
-        go = lambda copy: copy.start()
         if p >= AHEAD:
             self.sent(p - AHEAD)
 
         def hand_on(pairs):
             if pairs:
                 self.arrived(p, 2 * self.at.z + 1 - self.at.y)
-                self.own_z(p, 2 * self.at.z, 2, go)
-            self.passing(p, pairs, p % AHEAD, True, go)
+                self.own_z(p, 2 * self.at.z, 2, start)
+            self.passing(p, pairs, p % AHEAD, True, start)
 
         self.by_kind(p, hand_on)
 
@@ -294,9 +327,8 @@
         self.by_kind(p, lambda pairs: None if pairs else lax.fori_loop(0, self.at.depth, step, 0))
 
     def own_done(self, p):
-        done = lambda copy: copy.wait_send()
-        self.own(p, done)
-        self.by_kind(p, lambda pairs: self.own_z(p, 2 * self.at.z, 2, done) if pairs else None)
+        self.own(p, wait_send)
+        self.by_kind(p, lambda pairs: self.own_z(p, 2 * self.at.z, 2, wait_send) if pairs else None)
 
 
 def forward_kernel(
@@ -360,35 +392,37 @@
     sub = rows // NSUB
     channels = streams.shape[1] // 3
     aligned = part_rows % 16 == 0
-    go = lambda copy: copy.start()
     gather = Gather(at, held, chunk, early_y, (recv_sems, own_sems, send_sems))
     share_a = Share(at, rows_a, rows, share_sems)
     share_b = Share(at, rows_b, rows, share_sems)
     sums = Sums(at, acc, rows, core_out, core_in, far_in, core_sems, far_sems)
 
     span = (pieces - 2) * LANES
-    short = gate_weight.shape[1] - 2 * span + LANES
-
-    def parts(p, core, count=LANES):
+    assert gate_weight.shape[1] == 2 * span - LANES // 2
+
+    def parts(p, core):
         at_columns = rows_of(core * channels, channels, 128)
         if p == 0:
             return [(in_weight.at[k, :, at_columns], k * channels, channels) for k in range(2)]
         if p == 1:
             return [(in_weight.at[2, :, at_columns], 0, channels), (out_weight.at[:, at_columns], channels, channels)]
-        at_columns = rows_of(core * span + (p - 2) * LANES, count, 128)
-        return [(w.at[:, at_columns], k * LANES, count) for k, w in enumerate((gate_weight, up_weight, down_weight))]
+        found = []
+        for column, count, unit, k in ffn_columns(p, pieces, core):
+            at_columns = rows_of(core * span + (p - 2) * LANES + unit, count, 128)
+            found.append(((gate_weight, up_weight, down_weight)[k].at[:, at_columns], column, count))
+        return found
 
     def each_part(p, core, act):
-        if p < pieces - 1 or short == LANES:
-            for k, (src, column, count) in enumerate(parts(p, core)):
-                act(k, src, column, count)
+        if p < pieces - 1:
+            for k, part in enumerate(parts(p, core)):
+                act(k, *part)
             return
-        for to, count in ((0, LANES), (1, short)):
+        for to in (0, 1):
 
             @pl.when(core == to)
             def _():
-                for k, (src, column, size) in enumerate(parts(p, to, count)):
-                    act(k, src, column, size)
+                for k, part in enumerate(parts(p, to)):
+                    act(k, *part)
 
     def landing(p, core, column, count, buffer):
         if not aligned:
@@ -418,7 +452,7 @@
         each_part(p, at.core, copy)
 
     def own_block(p):
-        keep(p, lambda copy: copy.wait())
+        keep(p, wait)
         from_sib(p)
         here = rows_of(at.chip * chunk, chunk)
         if not aligned:
@@ -426,18 +460,16 @@
             lower = jnp.where(at.core == 0, a, b)
             upper = jnp.where(at.core == 0, b, a)
             held[p, here, :] = jnp.concatenate([lower, upper], axis=0).astype(bf16)
-        if p == pieces - 1 and short < LANES:
-
-            @pl.when(at.core == 1)
-            def _():
-                for k in range(3):
-                    held[p, here, k * LANES + short : (k + 1) * LANES] = jnp.zeros((chunk, LANES - short), bf16)
-
-        gather.own(p, go)
+        gather.own(p, start)
 
     meet(at)
-    to_sib(0, go)
-    keep(0, go)
+    to_sib(0, start)
+    keep(0, start)
+
+    @pl.when(at.core == 1)
+    def _():
+        held[pieces - 1, :, piece // 2 :] = jnp.zeros((width, piece - piece // 2), bf16)
+
     share = mixer_gain.shape[1]
     cur[0] = jnp.zeros(cur.shape[1:], f32)
     cur[0, 0:1, 0:share] = mixer_gain[...].astype(f32)
@@ -446,26 +478,39 @@
     placed = pltpu.roll(cur[0], (at.d * 2 + at.x) * share, 1)
     line = lax.broadcasted_iota(jnp.int32, placed.shape, 0)
     cur[0] = jnp.where(line < 5, placed, jnp.sum(valid[...]))
-    total_step(at, 0, cur, got, cube_sems.at[0], cube_sems.at[1])
-    own_block(0)
-    total_step(at, 1, cur, got, cube_sems.at[0], cube_sems.at[1])
+    tally = lambda step: total_copy(at, step, cur, got, cube_sems.at[0], cube_sems.at[1])
+    tallied = lambda step: total_end(at, step, cur, got, tally(step))
+    last = len(at.cube)
+    tally(0).start()
     for j in range(NSUB):
         rows_a[rows_of(at.own * rows + j * sub, sub), :] = tokens[pl.ds(j * sub, sub), :]
+    own_block(0)
+    tallied(0)
+    tally(1).start()
+    for p in range(1, pieces):
+        to_sib(p, start)
+        keep(p, start)
+    tallied(1)
+    for j in range(NSUB):
         share_a.start(j)
-    for p in range(1, pieces):
-        to_sib(p, go)
-        keep(p, go)
-    for step in range(2, len(at.cube)):
-        total_step(at, step, cur, got, cube_sems.at[0], cube_sems.at[1])
-        if step < 4:
-            own_block(step - 1)
-    last = len(at.cube)
-    small_out[...] = cur[last]
+    tally(2).start()
+    own_block(1)
+    tallied(2)
+    tally(3).start()
+    own_block(2)
+    tallied(3)
+    if last > 4:
+        tally(4).start()
+    relay = gather.relay
+    relay(0)
+    for step in range(4, last):
+        tallied(step)
+        if step + 1 < last:
+            tally(step + 1).start()
     for j in range(NSUB):
         share_a.forward(j)
+    small_out[...] = cur[last]
     gain_one, gain_two = cur[last, 0:1, :], cur[last, 1:2, :]
-    relay = gather.relay
-    relay(0)
     share_a.finish()
 
     def norm_rows(i, carry):
@@ -535,6 +580,16 @@
         slot = p % 2
         return pltpu.make_async_copy(gates.at[slot], gates_out.at[p - 2], gate_sems.at[slot])
 
+    def some(p, r):
+        part = rows_of(((r + 1 - at.core) % 2) * 2 * rows, 2 * rows)
+        for column, units in ffn_blocks(p, pieces):
+            both = nn(rows_b[part, :], held[p, :, column : column + 2 * units])
+            gate, up = both[:, 0:units], both[:, units:]
+            kept = 2 * column // 3
+            gates[p % 2, part, kept : kept + 2 * units] = both.astype(bf16)
+            hidden = (gate * jax.nn.sigmoid(gate) * up).astype(bf16)
+            acc[part, :] += nt(hidden, held[p, :, column + 2 * units : column + 3 * units])
+
     def feed(p, carry):
         for q in range(5, pieces):
 
@@ -542,7 +597,7 @@
             def _():
                 relay(q)
 
-        for q in range(2, pieces):
+        for q in range(2, pieces - 1):
 
             @pl.when(p == q)
             def _():
@@ -554,23 +609,25 @@
         def _():
             gates_copy(p - 2).wait()
 
-        def some(r, inner):
-            part = rows_of(((r + 1 - at.core) % 2) * 2 * rows, 2 * rows)
-            both = nn(rows_b[part, :], held[p, :, 0 : 2 * LANES])
-            gate, up = both[:, 0:LANES], both[:, LANES:]
-            gates[p % 2, part, :] = both.astype(bf16)
-            hidden = (gate * jax.nn.sigmoid(gate) * up).astype(bf16)
-            acc[part, :] += nt(hidden, held[p, :, 2 * LANES :])
+        def rows_part(r, inner):
+            some(p, r)
             return inner
 
-        lax.fori_loop(0, 2, some, 0)
+        lax.fori_loop(0, 2, rows_part, 0)
         gates_copy(p).start()
         return carry
 
     normed_copy.wait()
-    lax.fori_loop(2, pieces, feed, 0)
+    lax.fori_loop(2, pieces - 1, feed, 0)
+    final = pieces - 1
+    gather.whole(final)
+    gates_copy(final - 2).wait()
+    some(final, 0)
     sums.to_core()
+    some(final, 1)
     sums.to_far()
+    save(final).start()
+    gates_copy(final).start()
     scale = 1.0 / (width * cur[last, 5:6, 0:1])
     loss = jnp.zeros((1, width), f32)
     for j in range(NSUB):
@@ -597,7 +654,7 @@
     rows_copy.start()
     for p in range(pieces):
         save(p).wait()
-        to_sib(p, lambda copy: copy.wait_send())
+        to_sib(p, wait_send)
         gather.own_done(p)
     for p in range(pieces - AHEAD, pieces):
         gather.sent(p)
@@ -648,7 +705,7 @@
         pltpu.VMEM((rows, width), f32),
         pltpu.VMEM((cube + 1, 8, width), f32),
         pltpu.VMEM((cube, 8, width), f32),
-        dma((3, pieces, 3)),
+        dma((3, pieces, 6)),
         dma((pieces, ndp // 2)),
         dma((3, pieces)),
         dma((3, AHEAD, ndp // 4)),
@@ -682,27 +739,32 @@
         self.beside_in, self.line_in, self.pair_in, self.pair_beside = beside_in, line_in, pair_in, pair_beside
         self.total, self.credits = total, credits
         self.beside_sems, self.line_sems, self.pair_sems, self.pair_y_sems = sems
+        self.short, self.width = held.shape[0] - 1, held.shape[2]
         self.ydepth, self.zdepth = beside_in.shape[0], line_in.shape[0]
 
-    def block(self, p, chip, count=1):
-        return self.held.at[p, rows_of(chip * self.chunk, count * self.chunk), :]
-
-    def beside_copy(self, p, m, z):
+    def block(self, p, chip, count=1, width=None):
+        here = rows_of(chip * self.chunk, count * self.chunk)
+        return self.held.at[p, here, pl.ds(0, width or self.width)]
+
+    def run(self, act, copy, p, *rest):
+        by_core(self.at, p, self.short, self.width, lambda width: act(copy(p, *rest, width)))
+
+    def beside_copy(self, p, m, z, width):
         slot = m % self.ydepth
         return remote(
-            self.block(p, 2 * z + 1 - self.at.y),
-            self.beside_in.at[slot, z],
+            self.block(p, 2 * z + 1 - self.at.y, 1, width),
+            self.beside_in.at[slot, z, :, pl.ds(0, width)],
             self.beside_sems.at[0, slot, z],
             self.beside_sems.at[1, slot, z],
             self.at.beside,
         )
 
-    def line_copy(self, p, m, z, up):
+    def line_copy(self, p, m, z, up, width):
         slot, way = m % self.zdepth, 0 if up else 1
         into = z + 1 if up else z
         return remote(
-            self.block(p, 2 * z + self.at.y),
-            self.line_in.at[slot, into],
+            self.block(p, 2 * z + self.at.y, 1, width),
+            self.line_in.at[slot, into, :, pl.ds(0, width)],
             self.line_sems.at[way, slot, z],
             self.line_sems.at[2, slot, into],
             self.at.upper if up else self.at.lower,
@@ -733,7 +795,7 @@
 
     def drop_beside(self, p, m):
         def step(z, carry):
-            self.beside_copy(p, m, z).wait_send()
+            self.run(wait_send, self.beside_copy, p, m, z)
             return carry
 
         lax.fori_loop(0, self.at.depth, step, 0)
@@ -742,7 +804,7 @@
         self.free_beside(p, m, before)
 
         def step(s, carry):
-            self.beside_copy(p, m, self.turn(s)).start()
+            self.run(start, self.beside_copy, p, m, self.turn(s))
             return carry
 
         lax.fori_loop(0, self.at.depth, step, 0)
@@ -792,13 +854,13 @@
         def step(s, carry):
             z = self.turn(s)
             own = self.block(p, 2 * z + at.y)
-            self.beside_copy(p, m, z).wait_recv()
+            self.run(wait_recv, self.beside_copy, p, m, z)
             own[...] = (own[...].astype(f32) + self.beside_in[m % self.ydepth, z].astype(f32)).astype(bf16)
             for up in (True, False):
 
                 @pl.when(jnp.logical_and(z > at.z if up else z < at.z, self.opens(up)))
                 def _():
-                    self.line_copy(p, m, z, up).start()
+                    self.run(start, self.line_copy, p, m, z, up)
 
                 if onward:
 
@@ -813,11 +875,11 @@
             pl.semaphore_signal(self.credits.at[0], 1, device_id=at.beside, device_id_type=MESH)
 
     def pass_on(self, p, m, z, up):
-        self.line_copy(p, m, z, up).wait_recv()
+        self.run(wait_recv, self.line_copy, p, m, z, up)
         own = self.block(p, 2 * z + self.at.y)
         came = self.line_in[m % self.zdepth, z + 1 if up else z].astype(f32)
         own[...] = (own[...].astype(f32) + came).astype(bf16)
-        self.line_copy(p, m, z, up).start()
+        self.run(start, self.line_copy, p, m, z, up)
 
     def hop(self, p, m, has):
         self.ways(has, functools.partial(self.pass_on, p, m))
@@ -830,7 +892,7 @@
 
             @pl.when(self.behind(up))
             def _():
-                self.line_copy(p, m, at.z, up).wait_recv()
+                self.run(wait_recv, self.line_copy, p, m, at.z, up)
                 total[...] += self.line_in[m % self.zdepth, at.z + 1 if up else at.z].astype(f32)
                 if m + self.zdepth < self.count:
                     pl.semaphore_signal(
@@ -841,7 +903,7 @@
                     )
 
     def drop(self, p, m):
-        self.ways(lambda up: True, lambda z, up: self.line_copy(p, m, z, up).wait_send())
+        self.ways(lambda up: True, lambda z, up: self.run(wait_send, self.line_copy, p, m, z, up))
 
     def pairs_open(self, p):
         self.ways(self.opens, lambda z, up: self.pair_copy(p, z, up).start())
@@ -997,7 +1059,6 @@
     meet(at)
     acc[...] = jnp.zeros_like(acc)
     opening[0].wait()
-    opening[3].wait()
 
     def ffn(p, m=None):
         load_gates(p).wait()
@@ -1005,30 +1066,37 @@
 
         def some(r, carry):
             part = rows_of(((r + 1 - at.core) % 2) * 2 * rows, 2 * rows)
-            grad_hidden = nn(rows_a[part, :], held[p, :, 2 * LANES :])
-            gate = gates[p % 2, part, 0:LANES].astype(f32)
-            up = gates[p % 2, part, LANES:].astype(f32)
-            sig = jax.nn.sigmoid(gate)
-            active = gate * sig
-            back[part, 2 * LANES : 3 * LANES] = (active * up).astype(bf16)
-            grad_gate = grad_hidden * up * sig * (1.0 + gate * (1.0 - sig))
-            back[part, 0:LANES] = grad_gate.astype(bf16)
-            back[part, LANES : 2 * LANES] = (grad_hidden * active).astype(bf16)
-            acc[part, :] += nt(back[part, 0 : 2 * LANES], held[p, :, 0 : 2 * LANES])
+            for column, units in ffn_blocks(p, pieces):
+                ends = [column + k * units for k in range(4)]
+                grad_hidden = nn(rows_a[part, :], held[p, :, ends[2] : ends[3]])
+                kept = 2 * column // 3
+                gate = gates[p % 2, part, kept : kept + units].astype(f32)
+                up = gates[p % 2, part, kept + units : kept + 2 * units].astype(f32)
+                sig = jax.nn.sigmoid(gate)
+                active = gate * sig
+                back[part, ends[2] : ends[3]] = (active * up).astype(bf16)
+                grad_gate = grad_hidden * up * sig * (1.0 + gate * (1.0 - sig))
+                back[part, ends[0] : ends[1]] = grad_gate.astype(bf16)
+                back[part, ends[1] : ends[2]] = (grad_hidden * active).astype(bf16)
+                acc[part, :] += nt(back[part, ends[0] : ends[2]], held[p, :, ends[0] : ends[2]])
             return carry
 
         lax.fori_loop(0, 2, some, 0)
 
+        if p == 2:
+            opening[3].wait()
         blocks = 2 * width // piece
         matched = blocks == at.depth
 
         def weights(s, carry):
             i = scatter.turn(s) if matched else s
             part = rows_of(i * (piece // 2), piece // 2, 128)
-            held[p, part, 0 : 2 * LANES] = tn(rows_b[:, part], back[:, 0 : 2 * LANES]).astype(bf16)
-            held[p, part, 2 * LANES :] = tn(rows_a[:, part], back[:, 2 * LANES : 3 * LANES]).astype(bf16)
+            for column, units in ffn_blocks(p, pieces):
+                ends = [column + k * units for k in range(4)]
+                held[p, part, ends[0] : ends[2]] = tn(rows_b[:, part], back[:, ends[0] : ends[2]]).astype(bf16)
+                held[p, part, ends[2] : ends[3]] = tn(rows_a[:, part], back[:, ends[2] : ends[3]]).astype(bf16)
             if m is not None and matched:
-                scatter.beside_copy(p, m, i).start()
+                scatter.run(start, scatter.beside_copy, p, m, i)
             return carry
 
         lax.fori_loop(0, blocks, weights, 0)
@@ -1040,41 +1108,33 @@
     given = []
 
     span = (pieces - 2) * LANES
-    short = gate_grad.shape[1] - 2 * span + LANES
 
     def parts(p, core):
+        at_columns = rows_of(core * channels, channels, 128)
         if p == 0:
-            at_columns = rows_of(core * channels, channels, 128)
             return [(k * channels, channels, streams_grad.at[k, :, at_columns]) for k in range(2)]
         if p == 1:
-            at_columns = rows_of(core * channels, channels, 128)
             return [
                 (0, channels, streams_grad.at[2, :, at_columns]),
                 (channels, channels, out_grad.at[:, at_columns]),
             ]
         found = []
-        for k, out in enumerate((gate_grad, up_grad, down_grad)):
-            found.append((k * LANES, LANES, out.at[:, rows_of(core * span + (p - 2) * LANES, LANES, 128)]))
+        for column, count, unit, k in ffn_columns(p, pieces, core):
+            at_columns = rows_of(core * span + (p - 2) * LANES + unit, count, 128)
+            found.append((column, count, (gate_grad, up_grad, down_grad)[k].at[:, at_columns]))
         return found
 
-    def narrow(p, core):
-        found = []
-        for k, out in enumerate((gate_grad, up_grad, down_grad)):
-            found.append((k * LANES, short, out.at[:, rows_of(core * span + (p - 2) * LANES, short, 128)]))
-        return found
-
     def each_part(p, core, act):
-        if p < pieces - 1 or short == LANES:
-            for k, (first_column, count, dst) in enumerate(parts(p, core)):
-                act(k, first_column, count, dst)
+        if p < pieces - 1:
+            for k, part in enumerate(parts(p, core)):
+                act(k, *part)
             return
-
-        for is_short, found in ((False, parts), (True, narrow)):
-
-            @pl.when((core == 1) if is_short else (core == 0))
+        for to in (0, 1):
+
+            @pl.when(core == to)
             def _():
-                for k, (first_column, count, dst) in enumerate(found(p, 0 if not is_short else 1)):
-                    act(k, first_column, count, dst)
+                for k, part in enumerate(parts(p, to)):
+                    act(k, *part)
 
     def piece_rows(p, core, first_column, count):
         slot = given.index(p) % 2 if p in given else 0
@@ -1096,12 +1156,12 @@
 
     def give(p, fill):
         if len(given) > 1:
-            out_local(given[-2], lambda copy: copy.wait())
-            out_sib(given[-2], at.core, lambda copy: copy.wait_send())
+            out_local(given[-2], wait)
+            out_sib(given[-2], at.core, wait_send)
         given.append(p)
         fill((len(given) - 1) % 2)
-        out_local(p, lambda copy: copy.start())
-        out_sib(p, at.core, lambda copy: copy.start())
+        out_local(p, start)
+        out_sib(p, at.core, start)
 
     def beside(m):
         scatter.send_beside(order[m], m, order[m - YDEPTH] if m >= YDEPTH else None)
@@ -1265,10 +1325,10 @@
     for m in range(count - ZDEPTH, count):
         scatter.drop(order[m], m)
     for p in given[-2:]:
-        out_local(p, lambda copy: copy.wait())
-        out_sib(p, at.core, lambda copy: copy.wait_send())
+        out_local(p, wait)
+        out_sib(p, at.core, wait_send)
     for p in given:
-        out_sib(p, 1 - at.core, lambda copy: copy.wait_recv())
+        out_sib(p, 1 - at.core, wait_recv)
     tokens_copy.wait()
 
 
@@ -1324,7 +1384,7 @@
         dma((3, ZDEPTH, depth + 1)),
         dma((3, depth + 1)),
         dma((2,)),
-        dma((3, pieces, 3)),
+        dma((3, pieces, 6)),
         pltpu.SemaphoreType.REGULAR((3,)),
     ]
     return pl.pallas_call(

time: 547 us -> 532 us (0.973)
  Pallas kernels: 524 us -> 513 us
    pallas_call x1, Pallas kernels: 276 us -> 267 us  [forward(): pl.pallas_call(functools.partial(forward_kernel, ndp, early_y), out_shape...]
where the time goes in v5:
time: 532 us; the launch traced here: 528 us
  Pallas kernels  513 us (96%)
  local copies, waits for them, and re-layouts  11.8 us (2%)
    pallas_call x1, Pallas kernels, forward(): pl.pallas_call(functools.partial(forward_kernel, ndp, early_y), out_shape...  267 us
    pallas_call x1, Pallas kernels, backward(): pl.pallas_call(functools.partial(backward_kernel, ndp), out_shape=outs, i...  246 us
    unnamed x28, local copies, waits for them, and re-layouts  11 us

profile of v5, /device:TPU:0, one launch (start us, length us, event | category | flops | bytes accessed | tf_op | source)
XLA Modules:
  0.0 528.4 jit_solution(2314134858562330494)
XLA Ops:
  0.6 0.7 convert_element_type.3
  1.3 0.8 copy.22.valid
  2.1 266.9 %shard_map.194 = (bf16[9,1536,768]{2,1,0:T(8,128)(2,1)}, bf16[960,1536]{1,0:T(8,128)(2,1)}, bf16[960,1536]{1,0:T(8,128)(2,1)}, bf16[960,1536]{1,0:T(8,128)(2,1)}...) custom-call(bf16[3,96,768]{2,1,0:T(8,128)(2,1)} %bitcast.9, ...), custom_call_target="tpu_custom_call" | custom-call | tf_op jit(solution)/shard_map/pallas_call | solution.py:720
  269.0 246.3 %shard_map.195 = (f32[3,96,768]{2,1,0:T(8,128)}, f32[96,768]{1,0:T(8,128)}, f32[96,3456]{1,0:T(8,128)}, f32[96,3456]{1,0:T(8,128)}, f32[96,3456]{1,0:T(8,128)}, ...) custom-call(bf16[9,1536,768]{2,1,0:T(8,128)(2,1)} %get-tuple-element.32.held_i, ...), custom_call_target="tpu_custom_call" | custom-call | tf_op jit(solution)/shard_map/pallas_call | solution.py:1390
  516.0 0.0 copy-start
  516.0 2.7 copy.35
  518.7 0.0 copy-done
  518.7 0.0 copy-start.8
  518.7 0.0 copy-start.4
  518.7 1.1 copy.36
  519.8 0.0 copy-done.8
  519.8 0.0 copy-start.6
  519.8 0.0 copy-start.5
  519.8 0.0 copy-start.7
  519.8 0.0 copy-start.3
  519.9 0.5 copy.37
  520.4 0.1 copy-done.4
  520.4 0.9 copy.38
  521.3 0.0 copy-done.6
  521.3 0.6 copy.39
  521.9 0.0 copy-done.5
  521.9 0.7 copy.40
  522.6 0.0 copy-done.7
  522.6 0.0 copy-start.2
  522.6 0.5 copy.41
  523.1 0.0 copy-done.3
  523.2 1.1 copy.42
  524.2 0.0 copy-done.2
  524.2 0.0 copy-start.1
  524.2 1.1 copy.43
  525.3 0.7 copy-done.1
  526.0 1.1 copy.44
Async XLA Ops:
  516.0 2.7 copy-start
  518.7 1.1 copy-start.8
  518.7 1.7 copy-start.4
  519.8 1.5 copy-start.6
  519.8 2.1 copy-start.5
  519.8 2.8 copy-start.7
  519.8 3.3 copy-start.3
  522.6 1.6 copy-start.2
  524.2 1.8 copy-start.1

commit v6 on v5

--- a/solution.py
+++ b/solution.py
@@ -734,7 +734,8 @@
 
 
 class Scatter:
-    def __init__(self, at, held, chunk, count, beside_in, line_in, pair_in, pair_beside, total, sems, credits):
+    def __init__(self, at, held, chunk, count, mixed, beside_in, line_in, pair_in, pair_beside, total, sems, credits):
+        self.mixed = mixed
         self.at, self.held, self.chunk, self.count = at, held, chunk, count
         self.beside_in, self.line_in, self.pair_in, self.pair_beside = beside_in, line_in, pair_in, pair_beside
         self.total, self.credits = total, credits
@@ -746,8 +747,15 @@
         here = rows_of(chip * self.chunk, count * self.chunk)
         return self.held.at[p, here, pl.ds(0, width or self.width)]
 
+    def where_it_crosses(self, p, act):
+        if p == self.mixed:
+            pl.when(self.at.core == 0)(act)
+        else:
+            act()
+
     def run(self, act, copy, p, *rest):
-        by_core(self.at, p, self.short, self.width, lambda width: act(copy(p, *rest, width)))
+        each = lambda width: act(copy(p, *rest, width))
+        self.where_it_crosses(p, lambda: by_core(self.at, p, self.short, self.width, each))
 
     def beside_copy(self, p, m, z, width):
         slot = m % self.ydepth
@@ -771,12 +779,13 @@
         )
 
     def pair_copy(self, p, z, up):
+        second = 1 if p == self.mixed else 0
         into = z + 1 if up else z
         return remote(
             self.block(p, 2 * z, 2),
             self.pair_in.at[into],
-            self.pair_sems.at[0 if up else 1, z],
-            self.pair_sems.at[2, into],
+            self.pair_sems.at[3 * second + (0 if up else 1), z],
+            self.pair_sems.at[3 * second + 2, into],
             self.at.upper if up else self.at.lower,
         )
 
@@ -855,7 +864,12 @@
             z = self.turn(s)
             own = self.block(p, 2 * z + at.y)
             self.run(wait_recv, self.beside_copy, p, m, z)
-            own[...] = (own[...].astype(f32) + self.beside_in[m % self.ydepth, z].astype(f32)).astype(bf16)
+
+            def add():
+                came = self.beside_in[m % self.ydepth, z].astype(f32)
+                own[...] = (own[...].astype(f32) + came).astype(bf16)
+
+            self.where_it_crosses(p, add)
             for up in (True, False):
 
                 @pl.when(jnp.logical_and(z > at.z if up else z < at.z, self.opens(up)))
@@ -877,8 +891,12 @@
     def pass_on(self, p, m, z, up):
         self.run(wait_recv, self.line_copy, p, m, z, up)
         own = self.block(p, 2 * z + self.at.y)
-        came = self.line_in[m % self.zdepth, z + 1 if up else z].astype(f32)
-        own[...] = (own[...].astype(f32) + came).astype(bf16)
+
+        def add():
+            came = self.line_in[m % self.zdepth, z + 1 if up else z].astype(f32)
+            own[...] = (own[...].astype(f32) + came).astype(bf16)
+
+        self.where_it_crosses(p, add)
         self.run(start, self.line_copy, p, m, z, up)
 
     def hop(self, p, m, has):
@@ -919,13 +937,29 @@
 
     def pair_y_copy(self, p):
         at = self.at
+        second = 1 if p == self.mixed else 0
         return remote(
             self.block(p, 2 * at.z + 1 - at.y),
-            self.pair_beside,
-            self.pair_y_sems.at[0],
-            self.pair_y_sems.at[1],
+            self.pair_beside.at[second],
+            self.pair_y_sems.at[2 * second],
+            self.pair_y_sems.at[2 * second + 1],
             at.beside,
         )
+
+    def pairs_free(self):
+        at = self.at
+        for has, dev, credit in ((at.has_lower, at.lower, 3), (at.has_upper, at.upper, 4)):
+
+            @pl.when(has)
+            def _():
+                pl.semaphore_signal(self.credits.at[credit], 1, device_id=dev, device_id_type=MESH)
+
+    def pairs_wait(self):
+        for has, credit in ((self.at.has_upper, 3), (self.at.has_lower, 4)):
+
+            @pl.when(has)
+            def _():
+                pl.semaphore_wait(self.credits.at[credit], 1)
 
     def pairs_cross(self, p):
         at = self.at
@@ -944,7 +978,7 @@
         at = self.at
         self.pair_y_copy(p).wait()
         mine = self.block(p, 2 * at.z + at.y)[...].astype(f32)
-        self.total[slot] = mine + self.pair_beside[...].astype(f32)
+        self.total[slot] = mine + self.pair_beside[1 if p == self.mixed else 0].astype(f32)
         self.ways(lambda up: True, lambda z, up: self.pair_copy(p, z, up).wait_send())
 
 
@@ -1013,6 +1047,7 @@
     channels = piece // 2
     order = [2] + list(range(4, pieces)) + [0, 1]
     paired = 3
+    mixed = 0
     share = Share(at, rows_a, rows, share_sems)
     sums = Sums(at, acc, rows, core_out, core_in, far_in, core_sems, far_sems)
     scatter = Scatter(
@@ -1020,6 +1055,7 @@
         held,
         chunk,
         len(order),
+        mixed,
         beside_in,
         line_in,
         pair_in,
@@ -1166,8 +1202,15 @@
     def beside(m):
         scatter.send_beside(order[m], m, order[m - YDEPTH] if m >= YDEPTH else None)
 
+    on_core_one = pl.when(at.core == 1)
+
     def finish(m):
-        give(order[m], functools.partial(scatter.collect, order[m], m))
+        def fill(slot):
+            scatter.where_it_crosses(order[m], lambda: scatter.collect(order[m], m, slot))
+            if order[m] == mixed:
+                on_core_one(lambda: scatter.pairs_close(mixed, slot))
+
+        give(order[m], fill)
 
     def advance(m):
         onward = m == len(order) - 1
@@ -1177,17 +1220,17 @@
         scatter.add_beside(order[m], m, order[m - ZDEPTH] if m >= ZDEPTH else None, onward)
         if onward:
             return
-        scatter.hop(order[m], m, scatter.near)
-        if m == 0:
-            scatter.pair_hop(paired, scatter.near)
-        if m >= 1:
-            scatter.hop(order[m - 1], m - 1, scatter.far)
+        for k in (0, 1) if m == 1 else (m,) if m > 1 else ():
+            scatter.hop(order[k], k, scatter.near)
+        for k in (0, 1) if m == 2 else (m - 1,) if m > 2 else ():
+            scatter.hop(order[k], k, scatter.far)
         if m == 2:
             scatter.pair_hop(paired, scatter.far)
-        if m >= 2:
-            finish(m - 2)
+        for k in (0, 1) if m == 3 else (m - 2,) if m > 3 else ():
+            finish(k)
         if m == 3:
             scatter.pairs_cross(paired)
+            on_core_one(scatter.pairs_free)
         if m == 4:
             give(paired, functools.partial(scatter.pairs_close, paired))
 
@@ -1200,14 +1243,15 @@
     advance(0)
     ffn(6)
     beside(3)
+    scatter.pair_hop(paired, scatter.near)
     for p in range(7, pieces):
         ffn(p)
     sums.to_core()
     load_normed = load(normed_in, rows_b, 4)
     load_normed.start()
+    sums.to_far()
     advance(1)
     beside(4)
-    sums.to_far()
     load_first.wait()
     load_grad.wait()
     gain_two_grad = jnp.zeros((1, width), f32)
@@ -1278,8 +1322,15 @@
     lax.fori_loop(0, width // channels, mixer_weights, 0)
     advance(3)
     beside(6)
+
+    @on_core_one
+    def _():
+        scatter.pairs_wait()
+        scatter.pairs_open(mixed)
+
     sums.to_far()
     advance(4)
+    on_core_one(lambda: scatter.pair_hop(mixed, scatter.near))
     gain_one_grad = jnp.zeros((1, width), f32)
     for j in range(NSUB):
         part = rows_of(j * sub, sub)
@@ -1303,7 +1354,9 @@
     steps = len(at.cube)
     count = len(order)
     advance(5)
+    on_core_one(lambda: scatter.pair_hop(mixed, scatter.far))
     advance(6)
+    on_core_one(lambda: scatter.pairs_cross(mixed))
     total_end(at, 2, cur, got, tally(2))
     tally(3).start()
     advance(7)
@@ -1369,7 +1422,7 @@
         pltpu.VMEM((YDEPTH, depth, chunk, piece), bf16),
         pltpu.VMEM((ZDEPTH, depth + 1, chunk, piece), bf16),
         pltpu.VMEM((depth + 1, 2 * chunk, piece), bf16),
-        pltpu.VMEM((chunk, piece), bf16),
+        pltpu.VMEM((2, chunk, piece), bf16),
         pltpu.VMEM((2, chunk, piece), f32),
         pltpu.VMEM((cube + 1, 8, width), f32),
         pltpu.VMEM((cube, 8, width), f32),
@@ -1382,10 +1435,10 @@
         dma((2,)),
         dma((2, YDEPTH, depth)),
         dma((3, ZDEPTH, depth + 1)),
-        dma((3, depth + 1)),
-        dma((2,)),
+        dma((6, depth + 1)),
+        dma((4,)),
         dma((3, pieces, 6)),
-        pltpu.SemaphoreType.REGULAR((3,)),
+        pltpu.SemaphoreType.REGULAR((5,)),
     ]
     return pl.pallas_call(
         functools.partial(backward_kernel, ndp),

time: 532 us -> 524 us (0.985)
  Pallas kernels: 513 us -> 505 us
    pallas_call x1, Pallas kernels: 246 us -> 238 us  [backward(): pl.pallas_call(functools.partial(backward_kernel, ndp), out_shape=outs, i...]
where the time goes in v6:
time: 524 us; the launch traced here: 520 us
  Pallas kernels  505 us (96%)
  local copies, waits for them, and re-layouts  11.8 us (2%)
    pallas_call x1, Pallas kernels, forward(): pl.pallas_call(functools.partial(forward_kernel, ndp, early_y), out_shape...  267 us
    pallas_call x1, Pallas kernels, backward(): pl.pallas_call(functools.partial(backward_kernel, ndp), out_shape=outs, i...  238 us
    unnamed x28, local copies, waits for them, and re-layouts  11 us

profile of v6, /device:TPU:0, one launch (start us, length us, event | category | flops | bytes accessed | tf_op | source)
XLA Modules:
  0.0 520.1 jit_solution(774189685042385367)
XLA Ops:
  0.6 0.7 convert_element_type.3
  1.3 0.8 copy.22.valid
  2.1 266.9 %shard_map.194 = (bf16[9,1536,768]{2,1,0:T(8,128)(2,1)}, bf16[960,1536]{1,0:T(8,128)(2,1)}, bf16[960,1536]{1,0:T(8,128)(2,1)}, bf16[960,1536]{1,0:T(8,128)(2,1)}...) custom-call(bf16[3,96,768]{2,1,0:T(8,128)(2,1)} %bitcast.9, ...), custom_call_target="tpu_custom_call" | custom-call | tf_op jit(solution)/shard_map/pallas_call | solution.py:720
  269.0 238.0 %shard_map.195 = (f32[3,96,768]{2,1,0:T(8,128)}, f32[96,768]{1,0:T(8,128)}, f32[96,3456]{1,0:T(8,128)}, f32[96,3456]{1,0:T(8,128)}, f32[96,3456]{1,0:T(8,128)}, ...) custom-call(bf16[9,1536,768]{2,1,0:T(8,128)(2,1)} %get-tuple-element.32.held_i, ...), custom_call_target="tpu_custom_call" | custom-call | tf_op jit(solution)/shard_map/pallas_call | solution.py:1443
  507.7 0.0 copy-start
  507.7 2.7 copy.35
  510.4 0.0 copy-done
  510.4 0.0 copy-start.8
  510.4 0.0 copy-start.4
  510.4 1.1 copy.36
  511.5 0.0 copy-done.8
  511.5 0.0 copy-start.6
  511.6 0.0 copy-start.5
  511.6 0.0 copy-start.7
  511.6 0.0 copy-start.3
  511.6 0.5 copy.37
  512.1 0.1 copy-done.4
  512.1 0.9 copy.38
  513.0 0.0 copy-done.6
  513.1 0.6 copy.39
  513.6 0.0 copy-done.5
  513.6 0.7 copy.40
  514.3 0.0 copy-done.7
  514.3 0.0 copy-start.2
  514.4 0.5 copy.41
  514.9 0.0 copy-done.3
  514.9 1.1 copy.42
  515.9 0.0 copy-done.2
  515.9 0.0 copy-start.1
  515.9 1.1 copy.43
  517.0 0.7 copy-done.1
  517.7 1.1 copy.44
Async XLA Ops:
  507.7 2.7 copy-start
  510.4 1.1 copy-start.8
  510.4 1.7 copy-start.4
  511.5 1.5 copy-start.6
  511.6 2.1 copy-start.5
  511.6 2.8 copy-start.7
  511.6 3.3 copy-start.3
  514.3 1.6 copy-start.2
  515.9 1.8 copy-start.1

commit v7 on v6

--- a/solution.py
+++ b/solution.py
@@ -1360,13 +1360,15 @@
     total_end(at, 2, cur, got, tally(2))
     tally(3).start()
     advance(7)
-    for step in range(3, steps):
+    finish(count - 2)
+    total_end(at, 3, cur, got, tally(3))
+    if steps > 4:
+        tally(4).start()
+    finish(count - 1)
+    for step in range(4, steps):
         total_end(at, step, cur, got, tally(step))
         if step + 1 < steps:
             tally(step + 1).start()
-        if step == 3:
-            finish(count - 2)
-    finish(count - 1)
     share_lanes = mixer_gain_grad.shape[1]
     own = pltpu.roll(cur[steps], (width - (at.d * 2 + at.x) * share_lanes) % width, 1)
     mixer_gain_grad[...] = own[0:1, 0:share_lanes]

time: 524 us -> 523 us (level)
  no operation moved by 1% of the time
where the time goes in v7:
time: 523 us; the launch traced here: 519 us
  Pallas kernels  504 us (96%)
  local copies, waits for them, and re-layouts  11.8 us (2%)
    pallas_call x1, Pallas kernels, forward(): pl.pallas_call(functools.partial(forward_kernel, ndp, early_y), out_shape...  267 us
    pallas_call x1, Pallas kernels, backward(): pl.pallas_call(functools.partial(backward_kernel, ndp), out_shape=outs, i...  237 us
    unnamed x28, local copies, waits for them, and re-layouts  11 us

profile of v7, /device:TPU:0, one launch (start us, length us, event | category | flops | bytes accessed | tf_op | source)
XLA Modules:
  0.0 519.2 jit_solution(10052000466536947765)
XLA Ops:
  0.6 0.7 convert_element_type.3
  1.3 0.8 copy.22.valid
  2.1 266.9 %shard_map.194 = (bf16[9,1536,768]{2,1,0:T(8,128)(2,1)}, bf16[960,1536]{1,0:T(8,128)(2,1)}, bf16[960,1536]{1,0:T(8,128)(2,1)}, bf16[960,1536]{1,0:T(8,128)(2,1)}...) custom-call(bf16[3,96,768]{2,1,0:T(8,128)(2,1)} %bitcast.9, ...), custom_call_target="tpu_custom_call" | custom-call | tf_op jit(solution)/shard_map/pallas_call | solution.py:720
  269.0 237.1 %shard_map.195 = (f32[3,96,768]{2,1,0:T(8,128)}, f32[96,768]{1,0:T(8,128)}, f32[96,3456]{1,0:T(8,128)}, f32[96,3456]{1,0:T(8,128)}, f32[96,3456]{1,0:T(8,128)}, ...) custom-call(bf16[9,1536,768]{2,1,0:T(8,128)(2,1)} %get-tuple-element.32.held_i, ...), custom_call_target="tpu_custom_call" | custom-call | tf_op jit(solution)/shard_map/pallas_call | solution.py:1445
  506.8 0.0 copy-start
  506.8 2.7 copy.35
  509.5 0.0 copy-done
  509.5 0.0 copy-start.8
  509.5 0.0 copy-start.4
  509.5 1.1 copy.36
  510.6 0.0 copy-done.8
  510.6 0.0 copy-start.6
  510.6 0.0 copy-start.5
  510.6 0.0 copy-start.7
  510.6 0.0 copy-start.3
  510.6 0.5 copy.37
  511.1 0.1 copy-done.4
  511.2 0.9 copy.38
  512.1 0.0 copy-done.6
  512.1 0.6 copy.39
  512.7 0.0 copy-done.5
  512.7 0.7 copy.40
  513.4 0.0 copy-done.7
  513.4 0.0 copy-start.2
  513.4 0.5 copy.41
  513.9 0.0 copy-done.3
  513.9 1.1 copy.42
  515.0 0.0 copy-done.2
  515.0 0.0 copy-start.1
  515.0 1.1 copy.43
  516.0 0.7 copy-done.1
  516.8 1.1 copy.44
Async XLA Ops:
  506.8 2.7 copy-start
  509.5 1.1 copy-start.8
  509.5 1.7 copy-start.4
  510.6 1.5 copy-start.6
  510.6 2.1 copy-start.5
  510.6 2.8 copy-start.7
  510.6 3.3 copy-start.3
  513.4 1.6 copy-start.2
  515.0 1.8 copy-start.1

commit v8 on v7

--- a/solution.py
+++ b/solution.py
@@ -671,7 +671,7 @@
     pieces = 2 - (-weights[2].shape[1] // (2 * LANES))
     rows, width = tokens.shape
     cube = small_steps(ndp)
-    early_y = {3: "both", 6: "half"}
+    early_y = {4: "both", 7: "half"}
     dma = pltpu.SemaphoreType.DMA
     landing = (pieces, part_rows, piece) if part_rows % 16 else (1, 16, 128)
     shape = jax.ShapeDtypeStruct

time: 523 us -> 521 us (level)
  no operation moved by 1% of the time
where the time goes in v8:
time: 521 us; the launch traced here: 518 us
  Pallas kernels  503 us (97%)
  local copies, waits for them, and re-layouts  11.8 us (2%)
    pallas_call x1, Pallas kernels, forward(): pl.pallas_call(functools.partial(forward_kernel, ndp, early_y), out_shape...  264 us
    pallas_call x1, Pallas kernels, backward(): pl.pallas_call(functools.partial(backward_kernel, ndp), out_shape=outs, i...  239 us
    unnamed x28, local copies, waits for them, and re-layouts  11 us

profile of v8, /device:TPU:0, one launch (start us, length us, event | category | flops | bytes accessed | tf_op | source)
XLA Modules:
  0.0 517.7 jit_solution(7639076750399642877)
XLA Ops:
  0.6 0.7 convert_element_type.3
  1.3 0.8 copy.22.valid
  2.1 264.0 %shard_map.194 = (bf16[9,1536,768]{2,1,0:T(8,128)(2,1)}, bf16[960,1536]{1,0:T(8,128)(2,1)}, bf16[960,1536]{1,0:T(8,128)(2,1)}, bf16[960,1536]{1,0:T(8,128)(2,1)}...) custom-call(bf16[3,96,768]{2,1,0:T(8,128)(2,1)} %bitcast.9, ...), custom_call_target="tpu_custom_call" | custom-call | tf_op jit(solution)/shard_map/pallas_call | solution.py:720
  266.1 238.5 %shard_map.195 = (f32[3,96,768]{2,1,0:T(8,128)}, f32[96,768]{1,0:T(8,128)}, f32[96,3456]{1,0:T(8,128)}, f32[96,3456]{1,0:T(8,128)}, f32[96,3456]{1,0:T(8,128)}, ...) custom-call(bf16[9,1536,768]{2,1,0:T(8,128)(2,1)} %get-tuple-element.32.held_i, ...), custom_call_target="tpu_custom_call" | custom-call | tf_op jit(solution)/shard_map/pallas_call | solution.py:1445
  505.3 0.0 copy-start
  505.3 2.7 copy.35
  508.0 0.0 copy-done
  508.0 0.0 copy-start.8
  508.0 0.0 copy-start.4
  508.0 1.1 copy.36
  509.1 0.0 copy-done.8
  509.1 0.0 copy-start.6
  509.1 0.0 copy-start.5
  509.1 0.0 copy-start.7
  509.1 0.0 copy-start.3
  509.1 0.5 copy.37
  509.6 0.1 copy-done.4
  509.7 0.9 copy.38
  510.6 0.0 copy-done.6
  510.6 0.6 copy.39
  511.2 0.0 copy-done.5
  511.2 0.7 copy.40
  511.9 0.0 copy-done.7
  511.9 0.0 copy-start.2
  511.9 0.5 copy.41
  512.4 0.0 copy-done.3
  512.4 1.1 copy.42
  513.5 0.0 copy-done.2
  513.5 0.0 copy-start.1
  513.5 1.1 copy.43
  514.5 0.7 copy-done.1
  515.3 1.1 copy.44
Async XLA Ops:
  505.3 2.7 copy-start
  508.0 1.1 copy-start.8
  508.0 1.7 copy-start.4
  509.1 1.5 copy-start.6
  509.1 2.1 copy-start.5
  509.1 2.8 copy-start.7
  509.1 3.3 copy-start.3
  511.9 1.6 copy-start.2
  513.5 1.8 copy-start.1
